TPU v7x, 32 devices: a whole 2x2x4 slice. The times are simulated.
32 devices in a mesh: row: 4 (over y, x), col: 8 (over z, core).
Axes of the slice: x: 2, y: 2, z: 4, core: 2. Of those that a mesh axis runs over, the one named last changes fastest.
Arguments:
- positions: float32 [3, 32768], P(None, ('row', 'col')), may hold values from 0 to 1
- strengths: float32 [3, 32768], P(None, ('row', 'col')), may hold values from -0.06 to 0.06
- radii: float32 [32768], P(('row', 'col')), may hold values from 0.1 to 0.3
- pair_list: int32 [2, 4, 8, 2], P(None, 'row', 'col'), may hold values from 0 to 7, as said below
- pair_count: int32 [4, 8], P('row', 'col'), may hold values from 1 to 2, as said below
Outputs:
- velocity: float32 [3, 32768], P(None, ('row', 'col'))
- stretching: float32 [3, 32768], P(None, ('row', 'col'))
Inputs may be any that keep to these rules, and one draw needn't show every extreme that they name: `pair_list`: row-block indices lie in 0 to 7, column-block indices in 0 to 3; slot 0 of every tile pairs a group with itself. `pair_count`: some tile fills all 2 slots.
All inputs are finite; a program needn't handle non-finite values.
Results may differ from a plain program's by a relative error of at most 0.0003.
Values sent between devices are 32-bit elements; how exact they have to be, the bound alone decides.
No kernel may reach another device: no remote copies, remote signals or barrier semaphores. Data moves between devices by JAX's collectives and lax.ppermute only.
A program may use at most 192 MiB of HBM per device.

v0:
```python
import jax
import jax.numpy as jnp
from jax import lax
from jax.sharding import PartitionSpec as P

G = 1024
GD = 1


def cross_rows(u_a, u_b):
    return jnp.stack(
        [
            u_a[1] * u_b[2] - u_a[2] * u_b[1],
            u_a[2] * u_b[0] - u_a[0] * u_b[2],
            u_a[0] * u_b[1] - u_a[1] * u_b[0],
        ]
    )


def pair_terms(pos_a, str_a, rad_a, pos_b, str_b, rad_b):
    rvec = pos_a[:, :, None] - pos_b[:, None, :]
    rho = jnp.sum(rvec * rvec, axis=0)
    spread = 0.5 * (rad_a[:, None] ** 2 + rad_b[None, :] ** 2)
    inner = rho + spread
    power = inner ** (-2.5)
    upper = rho + 2.5 * spread
    kern = upper * power
    slope = 2.0 * (power - 2.5 * upper * power / inner)
    scale = 1.0 / (4.0 * jnp.pi)
    sa = str_a[:, :, None]
    sb = str_b[:, None, :]
    r_x_b = cross_rows(rvec, sb)
    r_x_a = cross_rows(rvec, sa)
    a_x_b = cross_rows(sa, sb)
    dot_a = jnp.sum(sa * rvec, axis=0)
    dot_b = jnp.sum(sb * rvec, axis=0)
    vel_a = -scale * jnp.sum(kern * r_x_b, axis=2)
    vel_b = scale * jnp.sum(kern * r_x_a, axis=1)
    str_ta = -scale * jnp.sum(kern * a_x_b + slope * dot_a * r_x_b, axis=2)
    str_tb = -scale * jnp.sum(-kern * a_x_b + slope * dot_b * r_x_a, axis=1)
    return (jnp.concatenate([vel_a, str_ta]), jnp.concatenate([vel_b, str_tb]))


def local(positions, strengths, radii, pair_list, pair_count):
    row_pos, row_str, row_rad = (
        lax.all_gather(positions, "col", axis=1, tiled=True),
        lax.all_gather(strengths, "col", axis=1, tiled=True),
        lax.all_gather(radii, "col", axis=0, tiled=True),
    )
    col_pos, col_str, col_rad = (
        lax.all_gather(positions, "row", axis=1, tiled=True),
        lax.all_gather(strengths, "row", axis=1, tiled=True),
        lax.all_gather(radii, "row", axis=0, tiled=True),
    )
    row_here = lax.axis_index("row")
    col_here = lax.axis_index("col")
    listed = pair_list[:, 0, 0, :]
    count = pair_count[0, 0]
    row_acc = jnp.zeros((6, row_pos.shape[1]), jnp.float32)
    col_acc = jnp.zeros((6, col_pos.shape[1]), jnp.float32)

    def visit(slot, accs):
        acc_row, acc_col = accs
        kk = listed[0, slot]
        mm = listed[1, slot]
        sa = kk * G
        sb = mm * G
        pa = lax.dynamic_slice_in_dim(row_pos, sa, G, 1)
        ta = lax.dynamic_slice_in_dim(row_str, sa, G, 1)
        ra = lax.dynamic_slice_in_dim(row_rad, sa, G, 0)
        pb = lax.dynamic_slice_in_dim(col_pos, sb, G, 1)
        tb = lax.dynamic_slice_in_dim(col_str, sb, G, 1)
        rb = lax.dynamic_slice_in_dim(col_rad, sb, G, 0)
        side_a, side_b = pair_terms(pa, ta, ra, pb, tb, rb)
        same = (kk // GD == col_here) & (mm // GD == row_here) & (kk % GD == mm % GD)
        live = jnp.where(slot < count, 1.0, 0.0).astype(jnp.float32)
        other = live * jnp.where(same, 0.0, 1.0).astype(jnp.float32)
        cur_a = lax.dynamic_slice_in_dim(acc_row, sa, G, 1)
        acc_row = lax.dynamic_update_slice_in_dim(acc_row, cur_a + live * side_a, sa, 1)
        cur_b = lax.dynamic_slice_in_dim(acc_col, sb, G, 1)
        acc_col = lax.dynamic_update_slice_in_dim(acc_col, cur_b + other * side_b, sb, 1)
        return (acc_row, acc_col)

    row_acc, col_acc = lax.fori_loop(0, listed.shape[1], visit, (row_acc, col_acc))
    row_part = lax.psum_scatter(row_acc, "col", scatter_dimension=1, tiled=True)
    col_part = lax.psum_scatter(col_acc, "row", scatter_dimension=1, tiled=True)
    total = row_part + col_part
    return (total[:3], total[3:])


def solution(mesh):
    placed = (
        P(None, ("row", "col")),
        P(None, ("row", "col")),
        P(("row", "col")),
        P(None, "row", "col", None),
        P("row", "col"),
    )
    return jax.shard_map(
        local,
        mesh=mesh,
        in_specs=placed,
        out_specs=(P(None, ("row", "col")), P(None, ("row", "col"))),
        check_vma=False,
    )
```

profile of v0, /device:TPU:0, one launch (start us, length us, event | category | flops | bytes accessed | tf_op | source)
XLA Modules:
  0.0 264.5 jit_solution(13581524105895750102)
XLA Ops:
  7.2 15.9 %all_gather.18 = f32[3,8192]{1,0:T(4,128)S(1)} all-gather(f32[3,1024]{1,0:T(4,128)} %param.7), channel_id=1, replica_groups=mesh['row'=4,'col'=8] {'col'}, dimensions={1}, use_global_device_ids=true | all-gather | bytes 110592 | tf_op jit(solution)/shard_map/all_gather | solution.py:46
  23.1 8.4 %all_gather.19 = f32[3,4096]{1,0:T(4,128)S(1)} all-gather(f32[3,1024]{1,0:T(4,128)} %param.7), channel_id=1, replica_groups=mesh['row'=4,'col'=8] {'row'}, dimensions={1}, use_global_device_ids=true | all-gather | bytes 61440 | tf_op jit(solution)/shard_map/all_gather | solution.py:51
  31.5 14.1 %all_gather.20 = f32[8192]{0:T(1024)S(1)} all-gather(f32[1024]{0:T(1024)} %param.9), channel_id=1, replica_groups=mesh['row'=4,'col'=8] {'col'}, dimensions={0}, use_global_device_ids=true | all-gather | bytes 36864 | tf_op jit(solution)/shard_map/all_gather | solution.py:48
  45.7 8.0 %all_gather.21 = f32[4096]{0:T(1024)S(1)} all-gather(f32[1024]{0:T(1024)} %param.9), channel_id=1, replica_groups=mesh['row'=4,'col'=8] {'row'}, dimensions={0}, use_global_device_ids=true | all-gather | bytes 20480 | tf_op jit(solution)/shard_map/all_gather | solution.py:53
  53.6 7.4 %all_gather.22 = f32[3,4096]{1,0:T(4,128)S(1)} all-gather(f32[3,1024]{1,0:T(4,128)} %param.8), channel_id=1, replica_groups=mesh['row'=4,'col'=8] {'row'}, dimensions={1}, use_global_device_ids=true | all-gather | bytes 61440 | tf_op jit(solution)/shard_map/all_gather | solution.py:52
  61.0 14.2 %all_gather.23 = f32[3,8192]{1,0:T(4,128)S(1)} all-gather(f32[3,1024]{1,0:T(4,128)} %param.8), channel_id=1, replica_groups=mesh['row'=4,'col'=8] {'col'}, dimensions={1}, use_global_device_ids=true | all-gather | bytes 110592 | tf_op jit(solution)/shard_map/all_gather | solution.py:47
  75.3 123.6 %while.18 = (s32[]{:T(128)}, f32[6,8192]{1,0:T(8,128)S(1)}, f32[6,4096]{1,0:T(8,128)S(1)}, s32[2,2]{1,0:T(2,128)}, s32[]{:T(128)}, /*index=5*/f32[3,8192]{1,0:T(...) while((s32[]{:T(128)}, f32[6,8192]{1,0:T(8,128)S(1)}, ...), condition=%wide.region_8.9_spmd, body=%wide.region_0.8_spmd.sunk | while | flops 118528008 | bytes 227082864 | solution.py:84
  75.3 1.4 constant_dynamic-slice_fusion.13
  78.2 11.8 %fusion.20 = (f32[1024,1024]{1,0:T(8,128)}, f32[1024,1024]{1,0:T(8,128)}, f32[1024,1024]{1,0:T(8,128)}, f32[3,1024,1024]{2,1,0:T(8,128)}) fusion(f32[3,1024]{1,0:T(4,128)S(1)} %constant_dynamic-slice_fusion.14, f32[3,1024]{1,0:T(4,128)S(1)} %constant_dynamic-slice_fusion.15, f32[3,1024]{1,0:T(4,128)S(1)} %constant_dynamic-slice_fusion.16, ...), kind=kLoop, calls=%fused_computation.5.clone.1 | loop fusion | flops 18874368 | bytes 25214976 | tf_op jit(solution)/shard_map/while/body/eval_jaxpr/reduce_sum | solution.py:36
  90.2 17.5 %multiply_subtract_fusion.10 = (f32[1,1024,1024]{2,1,0:T(8,128)}, f32[1,1024,1024]{2,1,0:T(8,128)}, f32[1,1024,1024]{2,1,0:T(8,128)}, f32[1,1024,1024]{2,1,0:T(8...) fusion(f32[3,1024,1024]{2,1,0:T(8,128)} %get-tuple-element.533,, ...), kind=kLoop, calls=%fused_computation.20.clone.1 | loop fusion | flops 28311552 | bytes 50356224 | tf_op jit(solution)/shard_map/while/body/eval_jaxpr/sub | solution.py:13
  107.8 11.7 %fusion.23 = (f32[1024,1024]{1,0:T(8,128)}, f32[1024,1024]{1,0:T(8,128)}, f32[1024,1024]{1,0:T(8,128)}, f32[1024,1024]{1,0:T(8,128)}) fusion(f32[1024,1024]{1,0:T(8,128)} %get-tuple-element.543, f32[1024]{0:T(1024)S(1)} %dynamic-slice_multiply_fusion.4, f32[1024]{0:T(1024)S(1)} %dynamic-slice_multiply_fusion.5, f32[1024,1024]{1,0:T(8,128)S(1)} %copy-done, ...), kind=kLoop, calls=%fused_computation.51.clone.1 | loop fusion | flops 14680064 | bytes 29368320 | tf_op jit(solution)/shard_map/while/body/eval_jaxpr/neg | solution.py:40
  119.5 0.3 copy-done.3
  119.8 15.3 %multiply_reduce_fusion.3 = (f32[3,1024]{1,0:T(4,128)S(1)}, f32[3,1024]{1,0:T(4,128)S(1)}, f32[3,1024]{1,0:T(4,128)S(1)}, f32[3,1024]{1,0:T(4,128)S(1)}) fusion(f32[1,1024,1024]{2,1,0:T(8,128)} %get-tuple-element.540, f32[1,1024,1024]{2,1,0:T(8,128)} %get-tuple-element.541, f32[1,1024,1024]{2,1,0:T(8,128)} %get-tuple-element.542, ...), kind=kLoop, calls=%fused_computation.12.clone.1 | loop fusion | flops 56610816 | bytes 54575104 | tf_op jit(solution)/shard_map/while/body/eval_jaxpr/reduce_sum | solution.py:37
  137.1 1.4 constant_dynamic-slice_fusion.13
  140.0 11.8 %fusion.20 = (f32[1024,1024]{1,0:T(8,128)}, f32[1024,1024]{1,0:T(8,128)}, f32[1024,1024]{1,0:T(8,128)}, f32[3,1024,1024]{2,1,0:T(8,128)}) fusion(f32[3,1024]{1,0:T(4,128)S(1)} %constant_dynamic-slice_fusion.14, f32[3,1024]{1,0:T(4,128)S(1)} %constant_dynamic-slice_fusion.15, f32[3,1024]{1,0:T(4,128)S(1)} %constant_dynamic-slice_fusion.16, ...), kind=kLoop, calls=%fused_computation.5.clone.1 | loop fusion | flops 18874368 | bytes 25214976 | tf_op jit(solution)/shard_map/while/body/eval_jaxpr/reduce_sum | solution.py:36
  152.0 17.5 %multiply_subtract_fusion.10 = (f32[1,1024,1024]{2,1,0:T(8,128)}, f32[1,1024,1024]{2,1,0:T(8,128)}, f32[1,1024,1024]{2,1,0:T(8,128)}, f32[1,1024,1024]{2,1,0:T(8...) fusion(f32[3,1024,1024]{2,1,0:T(8,128)} %get-tuple-element.533,, ...), kind=kLoop, calls=%fused_computation.20.clone.1 | loop fusion | flops 28311552 | bytes 50356224 | tf_op jit(solution)/shard_map/while/body/eval_jaxpr/sub | solution.py:13
  169.6 11.7 %fusion.23 = (f32[1024,1024]{1,0:T(8,128)}, f32[1024,1024]{1,0:T(8,128)}, f32[1024,1024]{1,0:T(8,128)}, f32[1024,1024]{1,0:T(8,128)}) fusion(f32[1024,1024]{1,0:T(8,128)} %get-tuple-element.543, f32[1024]{0:T(1024)S(1)} %dynamic-slice_multiply_fusion.4, f32[1024]{0:T(1024)S(1)} %dynamic-slice_multiply_fusion.5, f32[1024,1024]{1,0:T(8,128)S(1)} %copy-done, ...), kind=kLoop, calls=%fused_computation.51.clone.1 | loop fusion | flops 14680064 | bytes 29368320 | tf_op jit(solution)/shard_map/while/body/eval_jaxpr/neg | solution.py:40
  181.6 15.3 %multiply_reduce_fusion.3 = (f32[3,1024]{1,0:T(4,128)S(1)}, f32[3,1024]{1,0:T(4,128)S(1)}, f32[3,1024]{1,0:T(4,128)S(1)}, f32[3,1024]{1,0:T(4,128)S(1)}) fusion(f32[1,1024,1024]{2,1,0:T(8,128)} %get-tuple-element.540, f32[1,1024,1024]{2,1,0:T(8,128)} %get-tuple-element.541, f32[1,1024,1024]{2,1,0:T(8,128)} %get-tuple-element.542, ...), kind=kLoop, calls=%fused_computation.12.clone.1 | loop fusion | flops 56610816 | bytes 54575104 | tf_op jit(solution)/shard_map/while/body/eval_jaxpr/reduce_sum | solution.py:37
  199.0 0.6 copy-done.5
  199.7 0.7 reduce-scatter.3.cloned.1.call-update
  200.4 23.2 %reduce-scatter.5.cloned.1.call-done = f32[6,1024]{1,0:T(8,128)} async-done(((f32[6,4096]{1,0:T(8,128)}), f32[6,1024]{1,0:T(8,128)}) %reduce-scatter.5.cloned.1.call-update) | async-done | bytes 24592 | tf_op jit(solution)/shard_map/reduce_scatter | solution.py:86
  223.6 32.7 %reduce-scatter.3.cloned.1.call-done = f32[6,1024]{1,0:T(8,128)} async-done(((f32[6,8192]{1,0:T(8,128)}), f32[6,1024]{1,0:T(8,128)}) %reduce-scatter.3.cloned.1.call-update) | async-done | bytes 24592 | tf_op jit(solution)/shard_map/reduce_scatter | solution.py:85
  256.2 0.8 add.280
  257.0 0.6 fusion.14
  (49 shorter events, 1.0 us)
Async XLA Ops:
  7.2 216.4 %reduce-scatter.5.cloned.1.call-start = ((), (), s32[]{:S(2)}) async-start(), calls=%async_computation.3 | async-start | bytes 163840 | tf_op jit(solution)/shard_map/reduce_scatter | solution.py:86
  90.2 17.6 %copy-start = (f32[1024,1024]{1,0:T(8,128)S(1)}, f32[1024,1024]{1,0:T(8,128)}, u32[]{:S(2)}) copy-start(f32[1024,1024]{1,0:T(8,128)} %get-tuple-element.544) | copy-start | bytes 12582916 | tf_op jit(solution)/shard_map/while
  107.7 11.7 %copy-start.1 = (f32[1,1024,1024]{2,1,0:T(8,128)S(1)}, f32[1,1024,1024]{2,1,0:T(8,128)}, u32[]{:S(2)}) copy-start(f32[1,1024,1024]{2,1,0:T(8,128)} %get-tuple-element.553) | copy-start | bytes 12582916 | tf_op jit(solution)/shard_map/while
  107.8 11.7 %copy-start.2 = (f32[1,1024,1024]{2,1,0:T(8,128)S(1)}, f32[1,1024,1024]{2,1,0:T(8,128)}, u32[]{:S(2)}) copy-start(f32[1,1024,1024]{2,1,0:T(8,128)} %get-tuple-element.552) | copy-start | bytes 12582916 | tf_op jit(solution)/shard_map/while
  107.8 12.0 %copy-start.3 = (f32[1,1024,1024]{2,1,0:T(8,128)S(1)}, f32[1,1024,1024]{2,1,0:T(8,128)}, u32[]{:S(2)}) copy-start(f32[1,1024,1024]{2,1,0:T(8,128)} %get-tuple-element.551) | copy-start | bytes 12582916 | tf_op jit(solution)/shard_map/while
  152.0 17.6 %copy-start = (f32[1024,1024]{1,0:T(8,128)S(1)}, f32[1024,1024]{1,0:T(8,128)}, u32[]{:S(2)}) copy-start(f32[1024,1024]{1,0:T(8,128)} %get-tuple-element.544) | copy-start | bytes 12582916 | tf_op jit(solution)/shard_map/while
  169.6 11.7 %copy-start.1 = (f32[1,1024,1024]{2,1,0:T(8,128)S(1)}, f32[1,1024,1024]{2,1,0:T(8,128)}, u32[]{:S(2)}) copy-start(f32[1,1024,1024]{2,1,0:T(8,128)} %get-tuple-element.553) | copy-start | bytes 12582916 | tf_op jit(solution)/shard_map/while
  169.6 11.7 %copy-start.2 = (f32[1,1024,1024]{2,1,0:T(8,128)S(1)}, f32[1,1024,1024]{2,1,0:T(8,128)}, u32[]{:S(2)}) copy-start(f32[1,1024,1024]{2,1,0:T(8,128)} %get-tuple-element.552) | copy-start | bytes 12582916 | tf_op jit(solution)/shard_map/while
  169.6 12.0 %copy-start.3 = (f32[1,1024,1024]{2,1,0:T(8,128)S(1)}, f32[1,1024,1024]{2,1,0:T(8,128)}, u32[]{:S(2)}) copy-start(f32[1,1024,1024]{2,1,0:T(8,128)} %get-tuple-element.551) | copy-start | bytes 12582916 | tf_op jit(solution)/shard_map/while
  199.0 0.7 copy-start.5
  199.0 0.7 copy-start.4
  199.6 56.6 %reduce-scatter.3.cloned.1.call-start = ((), (), s32[]{:S(2)}) async-start(), calls=%async_computation.2 | async-start | bytes 294912 | tf_op jit(solution)/shard_map/reduce_scatter | solution.py:85
Sparse Core Ops, SparseCore 0:
  199.8 23.7 reduce-scatter.4
  225.9 30.2 reduce-scatter.2
where the time goes:
time: 265 us; the launch traced here: 264 us
  other arithmetic  114 us (43%)
  blocking collectives  68.1 us (26%)
  waiting for transfers between devices  56.5 us (21%)
  between operations  14.1 us (5%)
  loops' own time  6.87 us (3%)
  local copies, waits for them, and re-layouts  5.21 us (2%)
    sub x2, other arithmetic, cross_rows(): u_a[1] * u_b[2] - u_a[2] * u_b[1]  35.1 us
    reduce_scatter x1, waiting for transfers between devices, local(): row_part = lax.psum_scatter(row_acc, 'col', scatter_dimension=1, tiled=True)  32.7 us
    reduce_sum x2, other arithmetic, pair_terms(): vel_a = -scale * jnp.sum(kern * r_x_b, axis=2)  30.5 us
    reduce_sum x2, other arithmetic, pair_terms(): dot_b = jnp.sum(sb * rvec, axis=0)  23.7 us
    neg x2, other arithmetic, pair_terms(): str_tb = -scale * jnp.sum(-kern * a_x_b + slope * dot_b * r_x_a, axis=1)  23.4 us
    reduce_scatter x1, waiting for transfers between devices, local(): col_part = lax.psum_scatter(col_acc, 'row', scatter_dimension=1, tiled=True)  23.2 us
    all_gather x1, blocking collectives, local(): lax.all_gather(positions, 'col', axis=1, tiled=True)  15.9 us
    all_gather x1, blocking collectives, local(): lax.all_gather(strengths, 'col', axis=1, tiled=True)  14.2 us
  transfers between devices with their start and end apart: 2, of which 2 were waited for; matrix products, arithmetic and copies ran while one was open for 0% of the time, Pallas kernels for 0%

commit v1 on v0

v1 whole, which is shorter than its diff:
```python
import functools
import math

import jax
import jax.numpy as jnp
from jax import lax
from jax.experimental import pallas as pl
from jax.experimental.pallas import tpu as pltpu
from jax.sharding import PartitionSpec as P

F32 = jnp.float32
BF16 = jnp.bfloat16
UNIT = 256
STRIP = 16
G_ROWS = 32
H_ROWS = 96
G_SCALE = -1.5 / (4.0 * math.pi)
H_SCALE = 7.5 / (4.0 * math.pi)
VMEM = 48 * 1024 * 1024


def cross(u, v):
    return jnp.concatenate(
        [
            u[1:2] * v[2:3] - u[2:3] * v[1:2],
            u[2:3] * v[0:1] - u[0:1] * v[2:3],
            u[0:1] * v[1:2] - u[1:2] * v[0:1],
        ]
    )


def split(f):
    hi = f.astype(BF16).astype(F32)
    mid = (f - hi).astype(BF16).astype(F32)
    return [hi, mid, (f - hi) - mid]


def features(pack):
    pos = pack[0:3] - 0.5
    st = pack[3:6]
    e0 = jnp.concatenate([st, cross(pos, st), jnp.zeros((2, pack.shape[1]), F32)])
    moments = jnp.concatenate([e0, pos[0:1] * e0, pos[1:2] * e0, pos[2:3] * e0])
    for_g = jnp.concatenate(split(e0) + [jnp.zeros_like(e0)]).astype(BF16)
    return for_g, jnp.concatenate(split(moments)).astype(BF16)


def finish(pack, g, h, code):
    g = g[0:8] + g[8:16] + g[16:24]
    h = h[0:32] + h[32:64] + h[64:96]
    pos = pack[0:3] - 0.5
    st = pack[3:6]
    dot = jnp.sum(pos * st, axis=0, keepdims=True)
    d = dot * h[0:8] - st[0:1] * h[8:16] - st[1:2] * h[16:24] - st[2:3] * h[24:32]
    vel = G_SCALE * (cross(pos, g[0:3]) - g[3:6])
    stretch = G_SCALE * cross(st, g[0:3]) + H_SCALE * (cross(pos, d[0:3]) - d[3:6])
    return jnp.concatenate([vel, stretch, jnp.full((2, pack.shape[1]), code, F32)])


def strip(col, row, images, r):
    ghi, glo, hhi, hlo = images
    here = slice(r, r + STRIP)
    dx = col[:, 0:1] - row[0]
    dy = col[:, 1:2] - row[1]
    dz = col[:, 2:3] - row[2]
    s = col[:, 3:4] + row[3]
    qq = dx * dx + dy * dy + dz * dz + s
    t = lax.rsqrt(qq)
    t2 = t * t
    v = s * t2
    t3 = t2 * t
    g = t3 * (v + 2.0 / 3.0)
    h = (t3 * t2) * (v + 0.4)
    high = g.astype(BF16)
    ghi[here] = high
    glo[here] = (g - high.astype(F32)).astype(BF16)
    high = h.astype(BF16)
    hhi[here] = high
    hlo[here] = (h - high.astype(F32)).astype(BF16)


def down(f, image):
    return jnp.dot(f, image, preferred_element_type=F32)


def across(f, image):
    return lax.dot_general(f, image, (((1,), (1,)), ((), ())), preferred_element_type=F32)


def placed(pack):
    half = 0.5 * pack[6:7] * pack[6:7]
    return jnp.concatenate([pack[0:3], half, jnp.zeros((4, pack.shape[1]), F32)])


def interact(acol, brow, feat_a, slots, sums_b, feat_b=None, sums_a=None):
    for total in sums_b + (sums_a or ()):
        total[...] = jnp.zeros_like(total)

    def products(i, j, images):
        pi, pj = slice(i, i + UNIT), slice(j, j + UNIT)
        steps = []

        def add(total, part, f, form, image):
            total[:, part] += form(f, image[...])

        for n, image in enumerate(images):
            kind = n // 2
            f = feat_a[kind][:, pi]
            steps.append(functools.partial(add, sums_b[kind], pj, f, down, image))
            if sums_a is not None:
                f = feat_b[kind][:, pj]
                steps.append(functools.partial(add, sums_a[kind], pi, f, across, image))
        return steps

    n_strip = UNIT // STRIP
    waiting = []
    count = 0
    for j in range(0, brow.shape[1], UNIT):
        row = [jnp.broadcast_to(brow[n : n + 1, j : j + UNIT], (STRIP, UNIT)) for n in range(4)]
        for i in range(0, acol.shape[0], UNIT):
            images = slots[count % 2]
            count += 1
            per = n_strip // max(1, len(waiting))
            for n in range(n_strip):
                strip(acol[i + n * STRIP : i + (n + 1) * STRIP, :], row, images, n * STRIP)
                if waiting and (n + 1) % per == 0:
                    waiting.pop(0)()
            waiting = products(i, j, images)
    for step in waiting:
        step()


def own_chunk(n, pack, acol, feat, out, brow, sums, slots):
    part = slice(n * out.shape[1], (n + 1) * out.shape[1])
    brow[...] = placed(pack[:, part])
    interact(acol, brow, feat, slots, sums)
    out[...] = finish(pack[:, part], sums[0][...], sums[1][...], 0.0)


def first_kernel(pack, out, acol, feat_g, feat_h, brow, b_g, b_h, *flat):
    acol[...] = jnp.transpose(placed(pack[...]))
    feat_g[...], feat_h[...] = features(pack[...])
    own_chunk(0, pack, acol, (feat_g, feat_h), out, brow, (b_g, b_h), (flat[0:4], flat[4:8]))


def second_kernel(pair_list, pair_count, pack, acol, feat_g, feat_h, after, out, info, brow, b_g, b_h, *flat):
    del after
    k, m = pair_list[0, 0, 0, 1], pair_list[1, 0, 0, 1]
    info[0] = k
    info[1] = m
    info[2] = pair_count[0, 0]
    own_chunk(1, pack, acol, (feat_g, feat_h), out, brow, (b_g, b_h), (flat[0:4], flat[4:8]))


def later_kernel(n, pack, acol, feat_g, feat_h, after, out, brow, b_g, b_h, *flat):
    del after
    own_chunk(n, pack, acol, (feat_g, feat_h), out, brow, (b_g, b_h), (flat[0:4], flat[4:8]))


def pack_kernel(positions, strengths, radii, pack, sems):
    copies = [
        pltpu.make_async_copy(positions, pack.at[0:3], sems.at[0]),
        pltpu.make_async_copy(strengths, pack.at[3:6], sems.at[1]),
        pltpu.make_async_copy(radii, pack.at[6:7], sems.at[2]),
    ]
    for copy in copies:
        copy.start()
    for copy in copies:
        copy.wait()


def here(axis):
    return lax.axis_index(axis).astype(jnp.int32)


def choose(relative, near, far):
    at = relative // 2
    return jnp.where(relative % 2 == 0, near[at], far[at])


def stack_kernel(n_a, after, *refs):
    del after
    blocks_a, blocks_b, (near_a, near_b) = refs[:n_a], refs[n_a:-2], refs[-2:]
    for blocks, near in ((blocks_a, near_a), (blocks_b, near_b)):
        for n, block in enumerate(blocks):
            near[n] = block[...]


def pair_kernel(info, near_a, far_a, near_b, far_b, after, out_a, out_b, apack, bpack, acol, brow, *rest):
    del after
    sums_b, sums_a, slots = rest[0:2], rest[2:4], (rest[4:8], rest[8:12])
    blank = jnp.full((2, out_a.shape[1]), -1.0, F32)
    out_a[6:8] = blank
    out_b[6:8] = blank

    @pl.when(info[2] > 1)
    def _():
        k = info[0]
        m = info[1]
        from_a = k ^ here("col")
        from_b = m ^ here("row")
        apack[...] = choose(from_a, near_a, far_a)
        bpack[...] = choose(from_b, near_b, far_b)
        acol[...] = jnp.transpose(placed(apack[...]))
        brow[...] = placed(bpack[...])
        feat_a, feat_b = features(apack[...]), features(bpack[...])
        interact(acol, brow, feat_a, slots, sums_b, feat_b, sums_a)
        out_a[...] = finish(apack[...], sums_a[0][...], sums_a[1][...], k.astype(F32))

        @pl.when((from_a | from_b) != 0)
        def _():
            out_b[...] = finish(bpack[...], sums_b[0][...], sums_b[1][...], m.astype(F32))


def merge_kernel(n_a, after, *refs):
    del after
    parts_a, parts_b, (keep, send_a, send_b) = refs[:n_a], refs[n_a:-3], refs[-3:]
    total = jnp.zeros(keep.shape, F32)
    for axis, parts, send in (("col", parts_a, send_a), ("row", parts_b, send_b)):
        at = here(axis)
        onward = jnp.zeros_like(total)
        for part in parts:
            block = part[...]
            total += jnp.where(block[6:7] == at.astype(F32), block, 0.0)
            onward += jnp.where(block[6:7] == (at ^ 1).astype(F32), block, 0.0)
        send[...] = onward
    keep[...] = total


def sum_kernel(keep, part_a, part_b, *refs):
    own, (velocity, stretching) = refs[:-2], refs[-2:]
    total = keep[...] + part_a[...] + part_b[...]
    total += jnp.concatenate([chunk[...] for chunk in own], axis=1)
    velocity[...] = total[0:3]
    stretching[...] = total[3:6]


def work(cols, rows, sides):
    images = [pltpu.VMEM((UNIT, UNIT), BF16)] * 8
    sums_b = [pltpu.VMEM((G_ROWS, cols), F32), pltpu.VMEM((H_ROWS, cols), F32)]
    sums_a = [pltpu.VMEM((G_ROWS, rows), F32), pltpu.VMEM((H_ROWS, rows), F32)]
    return [pltpu.VMEM((8, cols), F32)] + sums_b + sums_a * (sides - 1) + images


def swap(block, axis, size, step):
    return lax.ppermute(block, axis, [(i, i ^ step) for i in range(size)])


def spread(block, axis, size):
    return [block] + [swap(block, axis, size, 2 * s) for s in range(1, size // 2)]


def local(n_row, n_col, positions, strengths, radii, pair_list, pair_count):
    g = radii.shape[0]
    part = g // 4
    hbm_spec = pl.BlockSpec(memory_space=pltpu.HBM)
    vmem_spec = pl.BlockSpec(memory_space=pltpu.VMEM)
    smem_spec = pl.BlockSpec(memory_space=pltpu.SMEM)
    params = pltpu.CompilerParams(vmem_limit_bytes=VMEM)
    block = jax.ShapeDtypeStruct((8, g), F32)
    chunk = jax.ShapeDtypeStruct((8, part), F32)
    chunk_cost = pl.CostEstimate(flops=30 * g * part, bytes_accessed=64 * g, transcendentals=g * part)
    chunk_call = functools.partial(
        pl.pallas_call, scratch_shapes=work(part, g, 1), compiler_params=params, cost_estimate=chunk_cost
    )

    pack = pl.pallas_call(
        pack_kernel,
        out_shape=block,
        in_specs=[hbm_spec] * 3,
        out_specs=vmem_spec,
        scratch_shapes=[pltpu.SemaphoreType.DMA((3,))],
        name="pack_group",
    )(positions, strengths, radii[None])

    blocks_a = spread(pack, "col", n_col)
    blocks_b = spread(pack, "row", n_row)
    own_0, *common = chunk_call(
        first_kernel,
        out_shape=(
            chunk,
            jax.ShapeDtypeStruct((g, 8), F32),
            jax.ShapeDtypeStruct((G_ROWS, g), BF16),
            jax.ShapeDtypeStruct((H_ROWS, g), BF16),
        ),
        in_specs=[vmem_spec],
        out_specs=(vmem_spec,) * 4,
        name="own_first",
    )(pack)
    near_a, near_b = pl.pallas_call(
        functools.partial(stack_kernel, len(blocks_a)),
        out_shape=(
            jax.ShapeDtypeStruct((len(blocks_a), 8, g), F32),
            jax.ShapeDtypeStruct((len(blocks_b), 8, g), F32),
        ),
        in_specs=[vmem_spec] * (1 + len(blocks_a) + len(blocks_b)),
        out_specs=(vmem_spec,) * 2,
        compiler_params=params,
        name="stack_groups",
    )(own_0, *blocks_a, *blocks_b)

    far_a = swap(near_a, "col", n_col, 1)
    far_b = swap(near_b, "row", n_row, 1)
    own_1, info = chunk_call(
        second_kernel,
        out_shape=(chunk, jax.ShapeDtypeStruct((3,), jnp.int32)),
        in_specs=[smem_spec] * 2 + [vmem_spec] * 5,
        out_specs=(vmem_spec, smem_spec),
        name="own_second",
    )(pair_list, pair_count, pack, *common, near_b)

    side_a, side_b = pl.pallas_call(
        pair_kernel,
        out_shape=(block, block),
        in_specs=[smem_spec] + [vmem_spec] * 5,
        out_specs=(vmem_spec, vmem_spec),
        scratch_shapes=[pltpu.VMEM((8, g), F32)] * 2 + [pltpu.VMEM((g, 8), F32)] + work(g, g, 2),
        compiler_params=params,
        cost_estimate=pl.CostEstimate(flops=60 * g * g, bytes_accessed=128 * g, transcendentals=g * g),
        name="listed_pair",
    )(info, near_a, far_a, near_b, far_b, own_1)

    parts_a = spread(side_a, "col", n_col)
    parts_b = spread(side_b, "row", n_row)
    own_2 = chunk_call(
        functools.partial(later_kernel, 2),
        out_shape=chunk,
        in_specs=[vmem_spec] * 5,
        out_specs=vmem_spec,
        name="own_third",
    )(pack, *common, side_b)
    keep, send_a, send_b = pl.pallas_call(
        functools.partial(merge_kernel, len(parts_a)),
        out_shape=(block,) * 3,
        in_specs=[vmem_spec] * (1 + len(parts_a) + len(parts_b)),
        out_specs=(vmem_spec,) * 3,
        compiler_params=params,
        name="merge_parts",
    )(own_2, *parts_a, *parts_b)

    far_a = swap(send_a, "col", n_col, 1)
    far_b = swap(send_b, "row", n_row, 1)
    own_3 = chunk_call(
        functools.partial(later_kernel, 3),
        out_shape=chunk,
        in_specs=[vmem_spec] * 5,
        out_specs=vmem_spec,
        name="own_fourth",
    )(pack, *common, keep)

    three = jax.ShapeDtypeStruct((3, g), F32)
    return pl.pallas_call(
        sum_kernel,
        out_shape=(three, three),
        in_specs=[vmem_spec] * 7,
        out_specs=(vmem_spec, vmem_spec),
        compiler_params=params,
        name="sum_parts",
    )(keep, far_a, far_b, own_0, own_1, own_2, own_3)


def solution(mesh):
    placed = (
        P(None, ("row", "col")),
        P(None, ("row", "col")),
        P(("row", "col")),
        P(None, "row", "col", None),
        P("row", "col"),
    )
    return jax.shard_map(
        functools.partial(local, mesh.shape["row"], mesh.shape["col"]),
        mesh=mesh,
        in_specs=placed,
        out_specs=(P(None, ("row", "col")), P(None, ("row", "col"))),
        check_vma=False,
    )
```

time: 265 us -> 36.6 us (0.14)
  other arithmetic: 114 us -> 0 us
  blocking collectives: 68.1 us -> 0 us
  waiting for transfers between devices: 56.5 us -> 4.59 us
  starting transfers between devices: 0.08 us -> 14.8 us
  Pallas kernels: 0 us -> 13.9 us
  between operations: 14.1 us -> 1.42 us
  loops' own time: 6.87 us -> 0 us
  local copies, waits for them, and re-layouts: 5.21 us -> 1.47 us
    all_gather x6 -> x0, blocking collectives: 68.1 us -> none  [the longest x1 15.9 us: local(): lax.all_gather(positions, 'col', axis=1, tiled=True)]
    reduce_scatter x2 -> x0, waiting for transfers between devices: 55.8 us -> none  [the longest x1 32.7 us: local(): row_part = lax.psum_scatter(row_acc, 'col', scatter_dimension=1, tiled=True)]
    reduce_sum x4 -> x0, other arithmetic: 54.2 us -> none  [the longest x2 30.5 us: pair_terms(): vel_a = -scale * jnp.sum(kern * r_x_b, axis=2)]
    sub x2 -> x0, other arithmetic: 35.1 us -> none  [cross_rows(): u_a[1] * u_b[2] - u_a[2] * u_b[1]]
    neg x2 -> x0, other arithmetic: 23.4 us -> none  [pair_terms(): str_tb = -scale * jnp.sum(-kern * a_x_b + slope * dot_b * r_x_a, axis=1)]
    ppermute x0 -> x12, starting transfers between devices: none -> 14.8 us  [swap(): return lax.ppermute(block, axis, [(i, i ^ step) for i in range(size)])]
    pallas_call x0 -> x9, Pallas kernels: none -> 13.9 us  [the longest x1 5.7 us: local(): pl.pallas_call(pair_kernel, out_shape=(block, block), in_specs=[smem_spec...]
    another operation x1 -> x0, loops' own time: 6.87 us -> none  [local(): lax.fori_loop(0, listed.shape[1], visit, (row_acc, col_acc))]
  transfers between devices with their start and end apart: 2 -> 12, of which waited for: 2 -> 5; matrix products, arithmetic and copies ran while one was open for 0% -> 0% of each run, Pallas kernels for 0% -> 17%
where the time goes in v1:
time: 36.6 us; the launch traced here: 36.2 us
  starting transfers between devices  14.8 us (40%)
  Pallas kernels  13.9 us (38%)
  waiting for transfers between devices  4.59 us (13%)
  local copies, waits for them, and re-layouts  1.47 us (4%)
  between operations  1.42 us (4%)
    ppermute x12, starting transfers between devices, swap(): return lax.ppermute(block, axis, [(i, i ^ step) for i in range(size)])  14.8 us
    pallas_call x1, Pallas kernels, local(): pl.pallas_call(pair_kernel, out_shape=(block, block), in_specs=[smem_spec...  5.7 us
    ppermute x12, waiting for transfers between devices, swap(): return lax.ppermute(block, axis, [(i, i ^ step) for i in range(size)])  4.59 us
    pallas_call x1, Pallas kernels, local(): chunk_call(second_kernel, out_shape=(chunk, jax.ShapeDtypeStruct((3,), jn...  2.2 us
    pallas_call x1, Pallas kernels, local(): chunk_call(first_kernel, out_shape=(chunk, jax.ShapeDtypeStruct((g, 8), F...  1.47 us
    unnamed x6, local copies, waits for them, and re-layouts  1.47 us
    pallas_call x1, Pallas kernels, local(): pl.pallas_call(pack_kernel, out_shape=block, in_specs=[hbm_spec] * 3, out...  1.37 us
    pallas_call x1, Pallas kernels, local(): chunk_call(functools.partial(later_kernel, 3), out_shape=chunk, in_specs=...  1.23 us
  transfers between devices with their start and end apart: 12, of which 5 were waited for; matrix products, arithmetic and copies ran while one was open for 0% of the time, Pallas kernels for 17%

profile of v1, /device:TPU:0, one launch (start us, length us, event | category | flops | bytes accessed | tf_op | source)
XLA Modules:
  0.0 36.2 jit_solution(9926712215424456189)
XLA Ops:
  0.6 1.4 %pack_group.1.pack.refs_0_.refs_4_ = f32[8,1024]{1,0:T(8,128)} custom-call(f32[3,1024]{1,0:T(4,128)} %positions.1, f32[3,1024]{1,0:T(4,128)} %strengths.1, f32[1,1024]{1,0:T(1,128)} %bitcast.1), custom_call_target="tpu_custom_call" | custom-call | tf_op jit(solution)/shard_map/pack_group/pallas_call | solution.py:266
  2.0 3.0 %collective-permute-start.3 = (f32[8,1024]{1,0:T(8,128)}, f32[8,1024]{1,0:T(8,128)S(1)}, u32[]{:S(2)}, u32[]{:S(2)}) collective-permute-start(f32[8,1024]{1,0:T(8,128)} %pack_group.1.pack.refs_0_.refs_4_), channel_id=1, source_target_pairs={{0,16},{8,24},{16,0},{24,8},{1,17},{9,25},{17,1},{25,9},{2,18},{10... | collective-permute-start | bytes 98312 | tf_op jit(solution)/shard_map/ppermute | solution.py:245
  5.0 3.6 %collective-permute-start.2 = (f32[8,1024]{1,0:T(8,128)}, f32[8,1024]{1,0:T(8,128)S(1)}, u32[]{:S(2)}, u32[]{:S(2)}) collective-permute-start(f32[8,1024]{1,0:T(8,128)} %pack_group.1.pack.refs_0_.refs_4_), channel_id=1, source_target_pairs={{0,6},{1,7},{2,4},{3,5},{4,2},{5,3},{6,0},{7,1},{8,14},{9,15},{10,... | collective-permute-start | bytes 98312 | tf_op jit(solution)/shard_map/ppermute | solution.py:245
  8.6 0.8 %collective-permute-start = (f32[8,1024]{1,0:T(8,128)}, f32[8,1024]{1,0:T(8,128)S(1)}, u32[]{:S(2)}, u32[]{:S(2)}) collective-permute-start(f32[8,1024]{1,0:T(8,128)} %pack_group.1.pack.refs_0_.refs_4_), channel_id=1, source_target_pairs={{0,2},{1,3},{2,0},{3,1},{4,6},{5,7},{6,4},{7,5},{8,10},{9,11},{10,... | collective-permute-start | bytes 98312 | tf_op jit(solution)/shard_map/ppermute | solution.py:245
  9.4 0.8 %copy-done = f32[8,1024]{1,0:T(8,128)S(1)} copy-done((f32[8,1024]{1,0:T(8,128)S(1)}, f32[8,1024]{1,0:T(8,128)}, u32[]{:S(2)}) %copy-start) | copy-done | bytes 32792
  10.2 1.5 %own_first.1 = (f32[8,256]{1,0:T(8,128)S(1)}, f32[1024,8]{1,0:T(8,128)S(1)}, bf16[32,1024]{1,0:T(8,128)(2,1)S(1)}, bf16[96,1024]{1,0:T(8,128)(2,1)S(1)}) custom-call(f32[8,1024]{1,0:T(8,128)S(1)} %copy-done), custom_call_target="tpu_custom_call" | custom-call | flops 7864320 | bytes 65536 | tf_op jit(solution)/shard_map/own_first/pallas_call | solution.py:277
  11.7 1.9 %collective-permute-done.1.refs_2_ = f32[8,1024]{1,0:T(8,128)S(1)} collective-permute-done((f32[8,1024]{1,0:T(8,128)}, f32[8,1024]{1,0:T(8,128)S(1)}, u32[]{:S(2)}, u32[]{:S(2)}) %collective-permute-start.1) | collective-permute-done | bytes 32800 | tf_op jit(solution)/shard_map/ppermute | solution.py:245
  13.7 0.1 collective-permute-start.4
  13.8 1.6 %collective-permute-start.5 = (f32[2,8,1024]{2,1,0:T(8,128)S(1)}, f32[2,8,1024]{2,1,0:T(8,128)S(1)}, u32[]{:S(2)}, u32[]{:S(2)}) collective-permute-start(f32[2,8,1024]{2,1,0:T(8,128)S(1)} %get-tuple-element.19.after.near_b), channel_id=1, source_target_pairs={{0,8},{8,0},{16,24},{24,16},{1,9},{9,1},{17,25},{25,17},{2,10},{10... | collective-permute-start | bytes 196616 | tf_op jit(solution)/shard_map/ppermute | solution.py:245
  16.0 0.7 %copy-done.2 = s32[2,1,1,2]{3,2,1,0:T(1,128)S(1)} copy-done((s32[2,1,1,2]{3,2,1,0:T(1,128)S(1)}, s32[2,1,1,2]{3,2,1,0:T(1,128)}, u32[]{:S(2)}) %copy-start.2) | copy-done | bytes 40
  16.7 2.2 %own_second.1 = (f32[8,256]{1,0:T(8,128)S(1)}, s32[3]{0:T(128)S(1)}) custom-call(s32[2,1,1,2]{3,2,1,0:T(1,128)S(1)} %copy-done.2, s32[1,1]{1,0:T(1,128)S(6)} %copy.7.pair_count, f32[8,1024]{1,0:T(8,128)S(1)} %copy-done.1, f32[1024,8]{1,0:T(8,128)S(1)} %get-tuple-element.15.acol, bf16[32,1024]{1,0:T(8,128)(2,1)S(1)} %get-tuple-element.16.feat_g, ...), custom_call_target="tpu_custom_call" | custom-call | flops 7864320 | bytes 65536 | tf_op jit(solution)/shard_map/own_second/pallas_call | solution.py:303
  18.9 5.7 %listed_pair.1 = (f32[8,1024]{1,0:T(8,128)S(1)}, f32[8,1024]{1,0:T(8,128)S(1)}) custom-call(s32[3]{0:T(128)S(1)} %get-tuple-element.20.info, f32[4,8,1024]{2,1,0:T(8,128)S(1)} %get-tuple-element.21.near_a, f32[4,8,1024]{2,1,0:T(8,128)S(1)} %collective-permute-done.4.far_a, f32[2,8,1024]{2,1,0:T(8,128)S(1)} %get-tuple-element.19.after.near_b, ...), custom_call_target="tpu_custom_call" | custom-call | flops 62914560 | bytes 131072 | tf_op jit(solution)/shard_map/listed_pair/pallas_call | solution.py:311
  24.7 1.8 %collective-permute-start.8 = (f32[8,1024]{1,0:T(8,128)S(1)}, f32[8,1024]{1,0:T(8,128)S(1)}, u32[]{:S(2)}, u32[]{:S(2)}) collective-permute-start(f32[8,1024]{1,0:T(8,128)S(1)} %get-tuple-element.24.refs_0_), channel_id=1, source_target_pairs={{0,6},{1,7},{2,4},{3,5},{4,2},{5,3},{6,0},{7,1},{8,14},{9,15},{10,... | collective-permute-start | bytes 98312 | tf_op jit(solution)/shard_map/ppermute | solution.py:245
  26.4 0.8 %collective-permute-start.7 = (f32[8,1024]{1,0:T(8,128)S(1)}, f32[8,1024]{1,0:T(8,128)S(1)}, u32[]{:S(2)}, u32[]{:S(2)}) collective-permute-start(f32[8,1024]{1,0:T(8,128)S(1)} %get-tuple-element.24.refs_0_), channel_id=1, source_target_pairs={{0,4},{1,5},{2,6},{3,7},{4,0},{5,1},{6,2},{7,3},{8,12},{9,13},{10,... | collective-permute-start | bytes 98312 | tf_op jit(solution)/shard_map/ppermute | solution.py:245
  27.2 1.9 %collective-permute-start.6 = (f32[8,1024]{1,0:T(8,128)S(1)}, f32[8,1024]{1,0:T(8,128)S(1)}, u32[]{:S(2)}, u32[]{:S(2)}) collective-permute-start(f32[8,1024]{1,0:T(8,128)S(1)} %get-tuple-element.24.refs_0_), channel_id=1, source_target_pairs={{0,2},{1,3},{2,0},{3,1},{4,6},{5,7},{6,4},{7,5},{8,10},{9,11},{10,... | collective-permute-start | bytes 98312 | tf_op jit(solution)/shard_map/ppermute | solution.py:245
  29.1 1.2 %own_third.1.after.refs_2_ = f32[8,256]{1,0:T(8,128)S(1)} custom-call(f32[8,1024]{1,0:T(8,128)S(1)} %copy-done.1, f32[1024,8]{1,0:T(8,128)S(1)} %get-tuple-element.15.acol, bf16[32,1024]{1,0:T(8,128)(2,1)S(1)} %get-tuple-element.16.feat_g, bf16[96,1024]{1,0:T(8,128)(2,1)S(1)} %get-tuple-element.17.feat_h, f32[8,1024]{1,0:T(8,128)S(1)} %get-tuple-element.23.after.refs_4_), custom_call_target="tpu_custom_call" | custom-call | flops 7864320 | bytes 65536 | tf_op jit(solution)/shard_map/own_third/pallas_call | solution.py:324
  30.4 0.1 collective-permute-done.8.refs_3_
  30.5 0.8 %collective-permute-done.7.refs_2_ = f32[8,1024]{1,0:T(8,128)S(1)} collective-permute-done((f32[8,1024]{1,0:T(8,128)S(1)}, f32[8,1024]{1,0:T(8,128)S(1)}, u32[]{:S(2)}, u32[]{:S(2)}) %collective-permute-start.7) | collective-permute-done | bytes 32800 | tf_op jit(solution)/shard_map/ppermute | solution.py:245
  31.3 0.2 collective-permute-done.6.refs_1_
  31.5 0.1 merge_parts.1
  31.6 1.2 %collective-permute-start.11 = (f32[8,1024]{1,0:T(8,128)S(1)}, f32[8,1024]{1,0:T(8,128)S(1)}, u32[]{:S(2)}, u32[]{:S(2)}) collective-permute-start(f32[8,1024]{1,0:T(8,128)S(1)} %get-tuple-element.27), channel_id=1, source_target_pairs={{0,8},{8,0},{16,24},{24,16},{1,9},{9,1},{17,25},{25,17},{2,10},{10... | collective-permute-start | bytes 98312 | tf_op jit(solution)/shard_map/ppermute | solution.py:245
  32.8 1.2 %own_fourth.1.refs_3_ = f32[8,256]{1,0:T(8,128)S(1)} custom-call(f32[8,1024]{1,0:T(8,128)S(1)} %copy-done.1, f32[1024,8]{1,0:T(8,128)S(1)} %get-tuple-element.15.acol, bf16[32,1024]{1,0:T(8,128)(2,1)S(1)} %get-tuple-element.16.feat_g, bf16[96,1024]{1,0:T(8,128)(2,1)S(1)} %get-tuple-element.17.feat_h, f32[8,1024]{1,0:T(8,128)S(1)} %get-tuple-element.25.after.keep), custom_call_target="tpu_custom_call" | custom-call | flops 7864320 | bytes 65536 | tf_op jit(solution)/shard_map/own_fourth/pallas_call | solution.py:342
  34.1 1.5 %collective-permute-done.11.part_b = f32[8,1024]{1,0:T(8,128)S(1)} collective-permute-done((f32[8,1024]{1,0:T(8,128)S(1)}, f32[8,1024]{1,0:T(8,128)S(1)}, u32[]{:S(2)}, u32[]{:S(2)}) %collective-permute-start.11) | collective-permute-done | bytes 32800 | tf_op jit(solution)/shard_map/ppermute | solution.py:245
  35.6 0.6 %sum_parts.1 = (f32[3,1024]{1,0:T(4,128)}, f32[3,1024]{1,0:T(4,128)}) custom-call(f32[8,1024]{1,0:T(8,128)S(1)} %get-tuple-element.25.after.keep, f32[8,1024]{1,0:T(8,128)S(1)} %collective-permute-done.10.part_a, f32[8,1024]{1,0:T(8,128)S(1)} %collective-permute-done.11.part_b, f32[8,256]{1,0:T(8,128)S(1)} %get-tuple-element.18.after.refs_0_, ...), custom_call_target="tpu_custom_call" | custom-call | tf_op jit(solution)/shard_map/sum_parts/pallas_call | solution.py:351
  (15 shorter events, 0.2 us)
Async XLA Ops:
  2.0 9.7 %collective-permute-start.3 = (f32[8,1024]{1,0:T(8,128)}, f32[8,1024]{1,0:T(8,128)S(1)}, u32[]{:S(2)}, u32[]{:S(2)}) collective-permute-start(f32[8,1024]{1,0:T(8,128)} %pack_group.1.pack.refs_0_.refs_4_), channel_id=1, source_target_pairs={{0,16},{8,24},{16,0},{24,8},{1,17},{9,25},{17,1},{25,9},{2,18},{10... | collective-permute-start | bytes 98312 | tf_op jit(solution)/shard_map/ppermute | solution.py:245
  5.0 6.7 %collective-permute-start.2 = (f32[8,1024]{1,0:T(8,128)}, f32[8,1024]{1,0:T(8,128)S(1)}, u32[]{:S(2)}, u32[]{:S(2)}) collective-permute-start(f32[8,1024]{1,0:T(8,128)} %pack_group.1.pack.refs_0_.refs_4_), channel_id=1, source_target_pairs={{0,6},{1,7},{2,4},{3,5},{4,2},{5,3},{6,0},{7,1},{8,14},{9,15},{10,... | collective-permute-start | bytes 98312 | tf_op jit(solution)/shard_map/ppermute | solution.py:245
  8.6 5.0 %collective-permute-start.1 = (f32[8,1024]{1,0:T(8,128)}, f32[8,1024]{1,0:T(8,128)S(1)}, u32[]{:S(2)}, u32[]{:S(2)}) collective-permute-start(f32[8,1024]{1,0:T(8,128)} %pack_group.1.pack.refs_0_.refs_4_), channel_id=1, source_target_pairs={{0,4},{1,5},{2,6},{3,7},{4,0},{5,1},{6,2},{7,3},{8,12},{9,13},{10,... | collective-permute-start | bytes 98312 | tf_op jit(solution)/shard_map/ppermute | solution.py:245
  8.6 5.0 %collective-permute-start = (f32[8,1024]{1,0:T(8,128)}, f32[8,1024]{1,0:T(8,128)S(1)}, u32[]{:S(2)}, u32[]{:S(2)}) collective-permute-start(f32[8,1024]{1,0:T(8,128)} %pack_group.1.pack.refs_0_.refs_4_), channel_id=1, source_target_pairs={{0,2},{1,3},{2,0},{3,1},{4,6},{5,7},{6,4},{7,5},{8,10},{9,11},{10,... | collective-permute-start | bytes 98312 | tf_op jit(solution)/shard_map/ppermute | solution.py:245
  9.4 0.8 %copy-start = (f32[8,1024]{1,0:T(8,128)S(1)}, f32[8,1024]{1,0:T(8,128)}, u32[]{:S(2)}) copy-start(f32[8,1024]{1,0:T(8,128)} %pack_group.1.pack.refs_0_.refs_4_) | copy-start | bytes 98308
  10.2 3.5 %copy-start.1 = (f32[8,1024]{1,0:T(8,128)S(1)}, f32[8,1024]{1,0:T(8,128)}, u32[]{:S(2)}) copy-start(f32[8,1024]{1,0:T(8,128)} %pack_group.1.pack.refs_0_.refs_4_) | copy-start | bytes 98308
  13.7 5.2 %collective-permute-start.4 = (f32[4,8,1024]{2,1,0:T(8,128)S(1)}, f32[4,8,1024]{2,1,0:T(8,128)S(1)}, u32[]{:S(2)}, u32[]{:S(2)}) collective-permute-start(f32[4,8,1024]{2,1,0:T(8,128)S(1)} %get-tuple-element.21.near_a), channel_id=1, source_target_pairs={{0,1},{1,0},{2,3},{3,2},{4,5},{5,4},{6,7},{7,6},{8,9},{9,8},{10,11... | collective-permute-start | bytes 393224 | tf_op jit(solution)/shard_map/ppermute | solution.py:245
  13.8 5.1 %collective-permute-start.5 = (f32[2,8,1024]{2,1,0:T(8,128)S(1)}, f32[2,8,1024]{2,1,0:T(8,128)S(1)}, u32[]{:S(2)}, u32[]{:S(2)}) collective-permute-start(f32[2,8,1024]{2,1,0:T(8,128)S(1)} %get-tuple-element.19.after.near_b), channel_id=1, source_target_pairs={{0,8},{8,0},{16,24},{24,16},{1,9},{9,1},{17,25},{25,17},{2,10},{10... | collective-permute-start | bytes 196616 | tf_op jit(solution)/shard_map/ppermute | solution.py:245
  16.0 0.7 %copy-start.2 = (s32[2,1,1,2]{3,2,1,0:T(1,128)S(1)}, s32[2,1,1,2]{3,2,1,0:T(1,128)}, u32[]{:S(2)}) copy-start(s32[2,1,1,2]{3,2,1,0:T(1,128)} %pair_list.1) | copy-start | bytes 52
  24.6 5.8 %collective-permute-start.9 = (f32[8,1024]{1,0:T(8,128)S(1)}, f32[8,1024]{1,0:T(8,128)S(1)}, u32[]{:S(2)}, u32[]{:S(2)}) collective-permute-start(f32[8,1024]{1,0:T(8,128)S(1)} %get-tuple-element.23.after.refs_4_), channel_id=1, source_target_pairs={{0,16},{8,24},{16,0},{24,8},{1,17},{9,25},{17,1},{25,9},{2,18},{10... | collective-permute-start | bytes 98312 | tf_op jit(solution)/shard_map/ppermute | solution.py:245
  24.7 5.8 %collective-permute-start.8 = (f32[8,1024]{1,0:T(8,128)S(1)}, f32[8,1024]{1,0:T(8,128)S(1)}, u32[]{:S(2)}, u32[]{:S(2)}) collective-permute-start(f32[8,1024]{1,0:T(8,128)S(1)} %get-tuple-element.24.refs_0_), channel_id=1, source_target_pairs={{0,6},{1,7},{2,4},{3,5},{4,2},{5,3},{6,0},{7,1},{8,14},{9,15},{10,... | collective-permute-start | bytes 98312 | tf_op jit(solution)/shard_map/ppermute | solution.py:245
  26.4 4.9 %collective-permute-start.7 = (f32[8,1024]{1,0:T(8,128)S(1)}, f32[8,1024]{1,0:T(8,128)S(1)}, u32[]{:S(2)}, u32[]{:S(2)}) collective-permute-start(f32[8,1024]{1,0:T(8,128)S(1)} %get-tuple-element.24.refs_0_), channel_id=1, source_target_pairs={{0,4},{1,5},{2,6},{3,7},{4,0},{5,1},{6,2},{7,3},{8,12},{9,13},{10,... | collective-permute-start | bytes 98312 | tf_op jit(solution)/shard_map/ppermute | solution.py:245
  27.2 4.3 %collective-permute-start.6 = (f32[8,1024]{1,0:T(8,128)S(1)}, f32[8,1024]{1,0:T(8,128)S(1)}, u32[]{:S(2)}, u32[]{:S(2)}) collective-permute-start(f32[8,1024]{1,0:T(8,128)S(1)} %get-tuple-element.24.refs_0_), channel_id=1, source_target_pairs={{0,2},{1,3},{2,0},{3,1},{4,6},{5,7},{6,4},{7,5},{8,10},{9,11},{10,... | collective-permute-start | bytes 98312 | tf_op jit(solution)/shard_map/ppermute | solution.py:245
  31.5 2.5 %collective-permute-start.10 = (f32[8,1024]{1,0:T(8,128)S(1)}, f32[8,1024]{1,0:T(8,128)S(1)}, u32[]{:S(2)}, u32[]{:S(2)}) collective-permute-start(f32[8,1024]{1,0:T(8,128)S(1)} %get-tuple-element.26), channel_id=1, source_target_pairs={{0,1},{1,0},{2,3},{3,2},{4,5},{5,4},{6,7},{7,6},{8,9},{9,8},{10,11... | collective-permute-start | bytes 98312 | tf_op jit(solution)/shard_map/ppermute | solution.py:245
  31.6 4.0 %collective-permute-start.11 = (f32[8,1024]{1,0:T(8,128)S(1)}, f32[8,1024]{1,0:T(8,128)S(1)}, u32[]{:S(2)}, u32[]{:S(2)}) collective-permute-start(f32[8,1024]{1,0:T(8,128)S(1)} %get-tuple-element.27), channel_id=1, source_target_pairs={{0,8},{8,0},{16,24},{24,16},{1,9},{9,1},{17,25},{25,17},{2,10},{10... | collective-permute-start | bytes 98312 | tf_op jit(solution)/shard_map/ppermute | solution.py:245

commit v2 on v1

v2 whole, which is shorter than its diff:
```python
import functools
import math

import jax
import jax.numpy as jnp
from jax import lax
from jax.experimental import pallas as pl
from jax.experimental.pallas import tpu as pltpu
from jax.sharding import PartitionSpec as P

F32 = jnp.float32
BF16 = jnp.bfloat16
UNIT = 256
STRIP = 16
G_ROWS = 32
H_ROWS = 96
Q_ROWS = 32
G_SCALE = -1.5 / (4.0 * math.pi)
H_SCALE = 7.5 / (4.0 * math.pi)
VMEM = 48 * 1024 * 1024


def cross(u, v):
    return jnp.concatenate(
        [
            u[1:2] * v[2:3] - u[2:3] * v[1:2],
            u[2:3] * v[0:1] - u[0:1] * v[2:3],
            u[0:1] * v[1:2] - u[1:2] * v[0:1],
        ]
    )


def split(f):
    hi = f.astype(BF16).astype(F32)
    mid = (f - hi).astype(BF16).astype(F32)
    return [hi, mid, (f - hi) - mid]


def features(pack):
    pos = pack[0:3] - 0.5
    st = pack[3:6]
    e0 = jnp.concatenate([st, cross(pos, st), jnp.zeros((2, pack.shape[1]), F32)])
    moments = jnp.concatenate([e0, pos[0:1] * e0, pos[1:2] * e0, pos[2:3] * e0])
    for_g = jnp.concatenate(split(e0) + [jnp.zeros_like(e0)]).astype(BF16)
    return for_g, jnp.concatenate(split(moments)).astype(BF16)


def widen(pack, wide):
    for_g, for_h = features(pack)
    both = jnp.transpose(jnp.concatenate([for_h, for_g]).astype(F32)).astype(BF16)
    at = lax.broadcasted_iota(jnp.int32, both.shape, 1)
    wide[0][...] = jnp.where(at < H_ROWS, 0.0, both.astype(F32)).astype(BF16)
    wide[1][...] = jnp.where(at < H_ROWS, both.astype(F32), 0.0).astype(BF16)


def finish(pack, g, h, code):
    g = g[0:8] + g[8:16] + g[16:24]
    h = h[0:32] + h[32:64] + h[64:96]
    pos = pack[0:3] - 0.5
    st = pack[3:6]
    dot = jnp.sum(pos * st, axis=0, keepdims=True)
    d = dot * h[0:8] - st[0:1] * h[8:16] - st[1:2] * h[16:24] - st[2:3] * h[24:32]
    vel = G_SCALE * (cross(pos, g[0:3]) - g[3:6])
    stretch = G_SCALE * cross(st, g[0:3]) + H_SCALE * (cross(pos, d[0:3]) - d[3:6])
    return jnp.concatenate([vel, stretch, jnp.full((2, pack.shape[1]), code, F32)])


def strip(qq, s, images, r):
    ghi, glo, hhi, hlo = images
    here = slice(r, r + STRIP)
    t = lax.rsqrt(qq)
    t2 = t * t
    v = s * t2
    t3 = t2 * t
    g = t3 * (v + 2.0 / 3.0)
    h = (t3 * t2) * (v + 0.4)
    high = g.astype(BF16)
    ghi[here] = high
    glo[here] = (g - high.astype(F32)).astype(BF16)
    high = h.astype(BF16)
    hhi[here] = high
    hlo[here] = (h - high.astype(F32)).astype(BF16)


def down(f, image):
    return jnp.dot(f, image, preferred_element_type=F32)


def halves(pack):
    return 0.5 * pack[6:7] * pack[6:7]


def distances(pack):
    pos = pack[0:3] - 0.5
    x1, x2, x3 = split(pos)
    norm = jnp.concatenate(split(jnp.sum(pos * pos, axis=0, keepdims=True) + halves(pack)))
    one = jnp.ones_like(norm)
    blank = jnp.zeros((8, pack.shape[1]), F32)
    left = [-2.0 * x for x in (x1, x1, x2, x2, x1, x3)] + [norm, one, blank]
    right = [x1, x2, x1, x2, x3, x1, one, norm, blank]
    return jnp.concatenate(left), jnp.concatenate(right).astype(BF16)


def columns(pack, dist, spread_s):
    left, right = distances(pack)
    dist[...] = jnp.transpose(left).astype(BF16)
    spread_s[...] = jnp.transpose(jnp.broadcast_to(halves(pack), (8, pack.shape[1])))
    return right


def interact(dist_a, s_a, dist_b, s_b, feat_a, qq, slots, sums_b):
    for total in sums_b:
        total[...] = jnp.zeros_like(total)

    def products(i, j, images):
        pi, pj = slice(i, i + UNIT), slice(j, j + UNIT)
        steps = []

        def add(total, f, high, low):
            total[:, pj] += down(f, high[...]) + down(f, low[...])

        for kind in range(2):
            f = feat_a[kind][:, pi]
            steps.append(functools.partial(add, sums_b[kind], f, *images[2 * kind : 2 * kind + 2]))
        return steps

    def measure(unit, into):
        i, j = unit
        into[...] = down(dist_a[i : i + UNIT, :], dist_b[:, j : j + UNIT])

    n_strip = UNIT // STRIP
    units = [(i, j) for j in range(0, s_b.shape[1], UNIT) for i in range(0, s_a.shape[0], UNIT)]
    measure(units[0], qq[0])
    waiting = []
    for count, (i, j) in enumerate(units):
        images = slots[count % 2]
        if count + 1 < len(units):
            waiting.insert(0, functools.partial(measure, units[count + 1], qq[(count + 1) % 2]))
        per = n_strip // max(1, len(waiting))
        row = jnp.broadcast_to(s_b[0:1, j : j + UNIT], (STRIP, UNIT))
        for n in range(n_strip):
            at = slice(i + n * STRIP, i + (n + 1) * STRIP)
            here = slice(n * STRIP, (n + 1) * STRIP)
            strip(qq[count % 2][here, :], s_a[at, 0:1] + row, images, n * STRIP)
            if waiting and (n + 1) % per == 0:
                waiting.pop(0)()
        for step in waiting:
            step()
        waiting = products(i, j, images)
    for step in waiting:
        step()


def interact_both(dist_a, s_a, dist_b, s_b, feat_a, wide_b, qq, images, acc, sums_b):
    rows, n = s_a.shape[0], UNIT
    blocks = s_b.shape[1] // n

    def measure(block):
        part = slice(block * n, (block + 1) * n)
        for i in range(0, rows, n):
            qq[block % 2][i : i + n, :] = down(dist_a[i : i + n, :], dist_b[:, part])

    def onto_a(block, i):
        here, part = slice(i, i + n), slice(block * n, (block + 1) * n)
        wide = jnp.concatenate([wide_b[0][part, :]] * 2 + [wide_b[1][part, :]] * 2)
        share = down(images[block % 2][here, :], wide)
        acc[here, :] = share if block == 0 else acc[here, :] + share

    def onto_b(block, kind):
        part = slice(block * n, (block + 1) * n)
        image = images[block % 2]
        at = 2 * kind * n
        total = down(feat_a[kind], image[:, at : at + n])
        sums_b[kind][:, part] = total + down(feat_a[kind], image[:, at + n : at + 2 * n])

    measure(0)
    waiting = []
    for block in range(blocks):
        image = images[block % 2]
        part = slice(block * n, (block + 1) * n)
        slots = [image.at[:, m * n : (m + 1) * n] for m in range(4)]
        row = jnp.broadcast_to(s_b[0:1, part], (STRIP, n))
        if block + 1 < blocks:
            waiting.append(functools.partial(measure, block + 1))
        n_strip = rows // STRIP
        per = max(1, n_strip // max(1, len(waiting)))
        for m in range(n_strip):
            here = slice(m * STRIP, (m + 1) * STRIP)
            strip(qq[block % 2][here, :], s_a[here, 0:1] + row, slots, m * STRIP)
            if waiting and (m + 1) % per == 0:
                waiting.pop(0)()
        for step in waiting:
            step()
        waiting = []
        for m, i in enumerate(range(0, rows, n)):
            waiting.append(functools.partial(onto_a, block, i))
            if m % 2 == 1 and m // 2 < 2:
                waiting.append(functools.partial(onto_b, block, 1 - m // 2))
    for step in waiting:
        step()


def own_chunk(n, pack, dist, s_col, right, feat, out, sums, qq, slots):
    part = slice(n * out.shape[1], (n + 1) * out.shape[1])
    interact(dist, s_col, right[:, part], halves(pack[:, part]), feat, qq, slots, sums)
    out[...] = finish(pack[:, part], sums[0][...], sums[1][...], 0.0)


def first_kernel(pack, after, out, dist, s_col, right, feat_g, feat_h, b_g, b_h, *flat):
    del after
    right[...] = columns(pack[...], dist, s_col)
    feat_g[...], feat_h[...] = features(pack[...])
    own_chunk(0, pack, dist, s_col, right, (feat_g, feat_h), out, (b_g, b_h), flat[0:2], (flat[2:6], flat[6:10]))


def later_kernel(n, pack, dist, s_col, right, feat_g, feat_h, after, out, b_g, b_h, *flat):
    del after
    own_chunk(n, pack, dist, s_col, right, (feat_g, feat_h), out, (b_g, b_h), flat[0:2], (flat[2:6], flat[6:10]))


def pack_kernel(positions, strengths, radii, pair_list, pair_count, pack, listed, count, sems):
    copies = [
        pltpu.make_async_copy(pair_list, listed, sems.at[0]),
        pltpu.make_async_copy(pair_count, count, sems.at[1]),
        pltpu.make_async_copy(positions, pack.at[0:3], sems.at[2]),
        pltpu.make_async_copy(strengths, pack.at[3:6], sems.at[3]),
        pltpu.make_async_copy(radii, pack.at[6:7], sems.at[4]),
    ]
    for copy in copies:
        copy.start()
    for copy in copies[:2]:
        copy.wait()
    for n, value in enumerate((listed[0, 0, 0, 1], listed[1, 0, 0, 1], count[0, 0])):
        pack[7:8, n * 128 : (n + 1) * 128] = jnp.full((1, 128), value.astype(F32))
    rest = pack.shape[1] - 3 * 128
    pack[7:8, 3 * 128 :] = jnp.zeros((1, rest), F32)
    for copy in copies[2:]:
        copy.wait()


def here(axis):
    return lax.axis_index(axis).astype(jnp.int32)


def choose(relative, near, far):
    at = relative // 2
    return jnp.where(relative % 2 == 0, near[at], far[at])


def stack_kernel(after, *refs):
    del after
    blocks, near = refs[:-1], refs[-1]
    for n, block in enumerate(blocks):
        near[n] = block[...]


def pair_kernel(pack, near_a, far_a, near_b, far_b, after, out_a, out_b, apack, bpack, dist, s_col, *rest):
    del after
    sums_b, wide_b, qq, images, acc = rest[0:2], rest[2:4], rest[4:6], rest[6:8], rest[8]
    k, m, count = [jnp.max(pack[7:8, n * 128 : (n + 1) * 128]).astype(jnp.int32) for n in range(3)]
    blank = jnp.full((2, out_a.shape[1]), -1.0, F32)
    out_a[6:8] = blank
    out_b[6:8] = blank

    @pl.when(count > 1)
    def _():
        from_a = k ^ here("col")
        from_b = m ^ here("row")
        apack[...] = choose(from_a, near_a, far_a)
        bpack[...] = choose(from_b, near_b, far_b)
        columns(apack[...], dist, s_col)
        right = distances(bpack[...])[1]
        widen(bpack[...], wide_b)
        feat_a = features(apack[...])
        interact_both(dist, s_col, right, halves(bpack[...]), feat_a, wide_b, qq, images, acc, sums_b)
        total = jnp.transpose(acc[...])
        out_a[...] = finish(apack[...], total[H_ROWS:], total[:H_ROWS], k.astype(F32))

        @pl.when((from_a | from_b) != 0)
        def _():
            out_b[...] = finish(bpack[...], sums_b[0][...], sums_b[1][...], m.astype(F32))


def merge_kernel(axis, after, *refs):
    del after
    parts, (keep, send) = refs[:-2], refs[-2:]
    at = here(axis)
    total = onward = jnp.zeros(keep.shape, F32)
    for part in parts:
        block = part[...]
        total += jnp.where(block[6:7] == at.astype(F32), block, 0.0)
        onward += jnp.where(block[6:7] == (at ^ 1).astype(F32), block, 0.0)
    keep[...] = total
    send[...] = onward


def sum_kernel(keep_a, keep_b, part_a, part_b, *refs):
    own, (velocity, stretching) = refs[:-2], refs[-2:]
    total = keep_a[...] + keep_b[...] + part_a[...] + part_b[...]
    total += jnp.concatenate([chunk[...] for chunk in own], axis=1)
    velocity[...] = total[0:3]
    stretching[...] = total[3:6]


def own_work(cols):
    return [
        pltpu.VMEM((G_ROWS, cols), F32),
        pltpu.VMEM((H_ROWS, cols), F32),
        *[pltpu.VMEM((UNIT, UNIT), F32)] * 2,
        *[pltpu.VMEM((UNIT, UNIT), BF16)] * 8,
    ]


def pair_work(g):
    return [
        *[pltpu.VMEM((8, g), F32)] * 2,
        pltpu.VMEM((g, Q_ROWS), BF16),
        pltpu.VMEM((g, 8), F32),
        pltpu.VMEM((G_ROWS, g), F32),
        pltpu.VMEM((H_ROWS, g), F32),
        *[pltpu.VMEM((g, G_ROWS + H_ROWS), BF16)] * 2,
        *[pltpu.VMEM((g, UNIT), F32)] * 2,
        *[pltpu.VMEM((g, 4 * UNIT), BF16)] * 2,
        pltpu.VMEM((g, G_ROWS + H_ROWS), F32),
    ]


def swap(block, axis, size, step):
    return lax.ppermute(block, axis, [(i, i ^ step) for i in range(size)])


def spread(block, axis, size):
    return [block] + [swap(block, axis, size, 2 * s) for s in range(1, size // 2)]


def local(n_row, n_col, positions, strengths, radii, pair_list, pair_count):
    g = radii.shape[0]
    part = g // 4
    hbm_spec = pl.BlockSpec(memory_space=pltpu.HBM)
    vmem_spec = pl.BlockSpec(memory_space=pltpu.VMEM)
    params = pltpu.CompilerParams(vmem_limit_bytes=VMEM)
    block = jax.ShapeDtypeStruct((8, g), F32)
    chunk = jax.ShapeDtypeStruct((8, part), F32)
    chunk_cost = pl.CostEstimate(flops=30 * g * part, bytes_accessed=64 * g, transcendentals=g * part)
    chunk_call = functools.partial(
        pl.pallas_call, scratch_shapes=own_work(part), compiler_params=params, cost_estimate=chunk_cost
    )

    pack = pl.pallas_call(
        pack_kernel,
        out_shape=block,
        in_specs=[hbm_spec] * 5,
        out_specs=vmem_spec,
        scratch_shapes=[
            pltpu.SMEM(pair_list.shape, jnp.int32),
            pltpu.SMEM(pair_count.shape, jnp.int32),
            pltpu.SemaphoreType.DMA((5,)),
        ],
        compiler_params=params,
        name="pack_group",
    )(positions, strengths, radii[None], pair_list, pair_count)

    blocks_a = spread(pack, "col", n_col)
    blocks_b = spread(pack, "row", n_row)
    def stack(after, blocks, name):
        return pl.pallas_call(
            stack_kernel,
            out_shape=jax.ShapeDtypeStruct((len(blocks), 8, g), F32),
            in_specs=[vmem_spec] * (1 + len(blocks)),
            out_specs=vmem_spec,
            compiler_params=params,
            name=name,
        )(after, *blocks)

    near_b = stack(pack, blocks_b, "stack_row")
    far_b = swap(near_b, "row", n_row, 1)
    own_0, *common = chunk_call(
        first_kernel,
        out_shape=(
            chunk,
            jax.ShapeDtypeStruct((g, Q_ROWS), BF16),
            jax.ShapeDtypeStruct((g, 8), F32),
            jax.ShapeDtypeStruct((Q_ROWS, g), BF16),
            jax.ShapeDtypeStruct((G_ROWS, g), BF16),
            jax.ShapeDtypeStruct((H_ROWS, g), BF16),
        ),
        in_specs=[vmem_spec] * 2,
        out_specs=(vmem_spec,) * 6,
        name="own_first",
    )(pack, near_b)
    near_a = stack(own_0, blocks_a, "stack_col")
    far_a = swap(near_a, "col", n_col, 1)
    own_1 = chunk_call(
        functools.partial(later_kernel, 1),
        out_shape=chunk,
        in_specs=[vmem_spec] * 7,
        out_specs=vmem_spec,
        name="own_second",
    )(pack, *common, near_a)

    side_a, side_b = pl.pallas_call(
        pair_kernel,
        out_shape=(block, block),
        in_specs=[vmem_spec] * 6,
        out_specs=(vmem_spec, vmem_spec),
        scratch_shapes=pair_work(g),
        compiler_params=params,
        cost_estimate=pl.CostEstimate(flops=60 * g * g, bytes_accessed=128 * g, transcendentals=g * g),
        name="listed_pair",
    )(pack, near_a, far_a, near_b, far_b, own_1)

    parts_a = spread(side_a, "col", n_col)
    parts_b = spread(side_b, "row", n_row)
    own_2 = chunk_call(
        functools.partial(later_kernel, 2),
        out_shape=chunk,
        in_specs=[vmem_spec] * 7,
        out_specs=vmem_spec,
        name="own_third",
    )(pack, *common, side_b)
    def merge(after, parts, axis):
        return pl.pallas_call(
            functools.partial(merge_kernel, axis),
            out_shape=(block,) * 2,
            in_specs=[vmem_spec] * (1 + len(parts)),
            out_specs=(vmem_spec,) * 2,
            compiler_params=params,
            name="merge_" + axis,
        )(after, *parts)

    keep_b, send_b = merge(pack, parts_b, "row")
    far_b = swap(send_b, "row", n_row, 1)
    keep_a, send_a = merge(own_2, parts_a, "col")
    far_a = swap(send_a, "col", n_col, 1)
    own_3 = chunk_call(
        functools.partial(later_kernel, 3),
        out_shape=chunk,
        in_specs=[vmem_spec] * 7,
        out_specs=vmem_spec,
        name="own_fourth",
    )(pack, *common, keep_a)

    three = jax.ShapeDtypeStruct((3, g), F32)
    return pl.pallas_call(
        sum_kernel,
        out_shape=(three, three),
        in_specs=[vmem_spec] * 8,
        out_specs=(vmem_spec, vmem_spec),
        compiler_params=params,
        name="sum_parts",
    )(keep_a, keep_b, far_a, far_b, own_0, own_1, own_2, own_3)


def solution(mesh):
    placed = (
        P(None, ("row", "col")),
        P(None, ("row", "col")),
        P(("row", "col")),
        P(None, "row", "col", None),
        P("row", "col"),
    )
    return jax.shard_map(
        functools.partial(local, mesh.shape["row"], mesh.shape["col"]),
        mesh=mesh,
        in_specs=placed,
        out_specs=(P(None, ("row", "col")), P(None, ("row", "col"))),
        check_vma=False,
    )
```

time: 36.6 us -> 36.7 us (level)
  Pallas kernels: 13.9 us -> 10.6 us
  waiting for transfers between devices: 4.59 us -> 7.39 us
  local copies, waits for them, and re-layouts: 1.47 us -> 2.79 us
  starting transfers between devices: 14.8 us -> 13.9 us
    ppermute x12, waiting for transfers between devices: 4.59 us -> 7.39 us  [swap(): return lax.ppermute(block, axis, [(i, i ^ step) for i in range(size)])]
    pallas_call x6 -> x8, Pallas kernels: 10.8 us -> 8.12 us  [the longest x1 5.18 us: local(): pl.pallas_call(pair_kernel, out_shape=(block, block), in_specs=[vmem_spec...]
    unnamed x6 -> x8, local copies, waits for them, and re-layouts: 1.47 us -> 2.79 us
    ppermute x12, starting transfers between devices: 14.8 us -> 13.9 us  [swap(): return lax.ppermute(block, axis, [(i, i ^ step) for i in range(size)])]
  transfers between devices with their start and end apart: 12 -> 12, of which waited for: 5 -> 7; matrix products, arithmetic and copies ran while one was open for 0% -> 0% of each run, Pallas kernels for 17% -> 11%
where the time goes in v2:
time: 36.7 us; the launch traced here: 36.1 us
  starting transfers between devices  13.9 us (38%)
  Pallas kernels  10.6 us (29%)
  waiting for transfers between devices  7.39 us (20%)
  local copies, waits for them, and re-layouts  2.79 us (8%)
  between operations  1.4 us (4%)
    ppermute x12, starting transfers between devices, swap(): return lax.ppermute(block, axis, [(i, i ^ step) for i in range(size)])  13.9 us
    ppermute x12, waiting for transfers between devices, swap(): return lax.ppermute(block, axis, [(i, i ^ step) for i in range(size)])  7.39 us
    pallas_call x1, Pallas kernels, local(): pl.pallas_call(pair_kernel, out_shape=(block, block), in_specs=[vmem_spec...  5.18 us
    unnamed x8, local copies, waits for them, and re-layouts  2.79 us
    pallas_call x1, Pallas kernels, local(): chunk_call(first_kernel, out_shape=(chunk, jax.ShapeDtypeStruct((g, Q_ROW...  1.3 us
    pallas_call x1, Pallas kernels, local(): chunk_call(functools.partial(later_kernel, 3), out_shape=chunk, in_specs=...  0.92 us
    pallas_call x1, Pallas kernels, local(): chunk_call(functools.partial(later_kernel, 1), out_shape=chunk, in_specs=...  0.92 us
    pallas_call x1, Pallas kernels, local(): chunk_call(functools.partial(later_kernel, 2), out_shape=chunk, in_specs=...  0.91 us
  transfers between devices with their start and end apart: 12, of which 7 were waited for; matrix products, arithmetic and copies ran while one was open for 0% of the time, Pallas kernels for 11%

profile of v2, /device:TPU:0, one launch (start us, length us, event | category | flops | bytes accessed | tf_op | source)
XLA Modules:
  0.0 36.1 jit_solution(4645168921186219085)
XLA Ops:
  1.3 0.7 %copy-done.3 = s32[2,1,1,2]{3,2,1,0:T(1,128)S(1)} copy-done((s32[2,1,1,2]{3,2,1,0:T(1,128)S(1)}, s32[2,1,1,2]{3,2,1,0:T(1,128)}, u32[]{:S(2)}) %copy-start.3) | copy-done | bytes 40
  2.0 0.7 %copy-done = f32[3,1024]{1,0:T(4,128)S(1)} copy-done((f32[3,1024]{1,0:T(4,128)S(1)}, f32[3,1024]{1,0:T(4,128)}, u32[]{:S(2)}) %copy-start) | copy-done | bytes 12312
  2.7 0.7 %copy-done.1 = f32[3,1024]{1,0:T(4,128)S(1)} copy-done((f32[3,1024]{1,0:T(4,128)S(1)}, f32[3,1024]{1,0:T(4,128)}, u32[]{:S(2)}) %copy-start.1) | copy-done | bytes 12312
  3.4 0.7 %copy-done.2 = f32[1024]{0:T(1024)S(1)} copy-done((f32[1024]{0:T(1024)S(1)}, f32[1024]{0:T(1024)}, u32[]{:S(2)}) %copy-start.2) | copy-done | bytes 4120
  4.1 0.6 %pack_group.1.after.refs_0_.pack = f32[8,1024]{1,0:T(8,128)S(1)} custom-call(f32[3,1024]{1,0:T(4,128)S(1)} %copy-done, f32[3,1024]{1,0:T(4,128)S(1)} %copy-done.1, f32[1,1024]{1,0:T(1,128)S(1)} %bitcast.1, s32[2,1,1,2]{3,2,1,0:T(1,128)S(1)} %copy-done.3, s32[1,1]{1,0:T(1,128)S(6)} %copy.7.pair_count), custom_call_target="tpu_custom_call" | custom-call | tf_op jit(solution)/shard_map/pack_group/pallas_call | solution.py:349
  4.7 3.0 %collective-permute-start = (f32[8,1024]{1,0:T(8,128)S(1)}, f32[8,1024]{1,0:T(8,128)S(1)}, u32[]{:S(2)}, u32[]{:S(2)}) collective-permute-start(f32[8,1024]{1,0:T(8,128)S(1)} %pack_group.1.after.refs_0_.pack), channel_id=1, source_target_pairs={{0,16},{8,24},{16,0},{24,8},{1,17},{9,25},{17,1},{25,9},{2,18},{10... | collective-permute-start | bytes 98312 | tf_op jit(solution)/shard_map/ppermute | solution.py:329
  7.7 3.6 %collective-permute-start.3 = (f32[8,1024]{1,0:T(8,128)S(1)}, f32[8,1024]{1,0:T(8,128)S(1)}, u32[]{:S(2)}, u32[]{:S(2)}) collective-permute-start(f32[8,1024]{1,0:T(8,128)S(1)} %pack_group.1.after.refs_0_.pack), channel_id=1, source_target_pairs={{0,6},{1,7},{2,4},{3,5},{4,2},{5,3},{6,0},{7,1},{8,14},{9,15},{10,... | collective-permute-start | bytes 98312 | tf_op jit(solution)/shard_map/ppermute | solution.py:329
  11.3 0.8 %collective-permute-start.1 = (f32[8,1024]{1,0:T(8,128)S(1)}, f32[8,1024]{1,0:T(8,128)S(1)}, u32[]{:S(2)}, u32[]{:S(2)}) collective-permute-start(f32[8,1024]{1,0:T(8,128)S(1)} %pack_group.1.after.refs_0_.pack), channel_id=1, source_target_pairs={{0,2},{1,3},{2,0},{3,1},{4,6},{5,7},{6,4},{7,5},{8,10},{9,11},{10,... | collective-permute-start | bytes 98312 | tf_op jit(solution)/shard_map/ppermute | solution.py:329
  12.1 1.3 %own_first.1 = (f32[8,256]{1,0:T(8,128)S(1)}, bf16[1024,32]{1,0:T(8,128)(2,1)S(1)}, f32[1024,8]{1,0:T(8,128)S(1)}, bf16[32,1024]{1,0:T(8,128)(2,1)S(1)}, bf16[32...) custom-call(f32[8,1024]{1,0:T(8,128)S(1)} %pack_group.1.after.refs_0_.pack, f32[2,8,1024]{2,1,0:T(8,128)S(1)} %stack_row.1.after.near_b), custom_call_target="tpu_custom_call" | custom-call | flops 7864320 | bytes 65536 | tf_op jit(solution)/shard_map/own_first/pallas_call | solution.py:377
  13.4 0.4 collective-permute-done.3.refs_3_
  13.8 2.4 %collective-permute-done.2.refs_2_ = f32[8,1024]{1,0:T(8,128)S(1)} collective-permute-done((f32[8,1024]{1,0:T(8,128)S(1)}, f32[8,1024]{1,0:T(8,128)S(1)}, u32[]{:S(2)}, u32[]{:S(2)}) %collective-permute-start.2) | collective-permute-done | bytes 32800 | tf_op jit(solution)/shard_map/ppermute | solution.py:329
  16.2 1.6 %collective-permute-start.5 = (f32[2,8,1024]{2,1,0:T(8,128)S(1)}, f32[2,8,1024]{2,1,0:T(8,128)S(1)}, u32[]{:S(2)}, u32[]{:S(2)}) collective-permute-start(f32[2,8,1024]{2,1,0:T(8,128)S(1)} %stack_row.1.after.near_b), channel_id=1, source_target_pairs={{0,8},{8,0},{16,24},{24,16},{1,9},{9,1},{17,25},{25,17},{2,10},{10... | collective-permute-start | bytes 196616 | tf_op jit(solution)/shard_map/ppermute | solution.py:329
  17.8 0.9 %own_second.1.after.refs_1_ = f32[8,256]{1,0:T(8,128)S(1)} custom-call(f32[8,1024]{1,0:T(8,128)S(1)} %pack_group.1.after.refs_0_.pack, bf16[1024,32]{1,0:T(8,128)(2,1)S(1)} %get-tuple-element.14.dist, f32[1024,8]{1,0:T(8,128)S(1)} %get-tuple-element.15.s_col, bf16[32,1024]{1,0:T(8,128)(2,1)S(1)} %get-tuple-element.16.right, ...), custom_call_target="tpu_custom_call" | custom-call | flops 7864320 | bytes 65536 | tf_op jit(solution)/shard_map/own_second/pallas_call | solution.py:393
  18.7 2.0 %collective-permute-done.5.far_b = f32[2,8,1024]{2,1,0:T(8,128)S(1)} collective-permute-done((f32[2,8,1024]{2,1,0:T(8,128)S(1)}, f32[2,8,1024]{2,1,0:T(8,128)S(1)}, u32[]{:S(2)}, u32[]{:S(2)}) %collective-permute-start.5) | collective-permute-done | bytes 65568 | tf_op jit(solution)/shard_map/ppermute | solution.py:329
  20.8 5.2 %listed_pair.1 = (f32[8,1024]{1,0:T(8,128)S(1)}, f32[8,1024]{1,0:T(8,128)S(1)}) custom-call(f32[8,1024]{1,0:T(8,128)S(1)} %pack_group.1.after.refs_0_.pack, f32[4,8,1024]{2,1,0:T(8,128)S(1)} %stack_col.1.after.near_a, f32[4,8,1024]{2,1,0:T(8,128)S(1)} %collective-permute-done.4.far_a, f32[2,8,1024]{2,1,0:T(8,128)S(1)} %stack_row.1.after.near_b, ...), custom_call_target="tpu_custom_call" | custom-call | flops 62914560 | bytes 131072 | tf_op jit(solution)/shard_map/listed_pair/pallas_call | solution.py:401
  26.1 2.2 %collective-permute-start.7 = (f32[8,1024]{1,0:T(8,128)S(1)}, f32[8,1024]{1,0:T(8,128)S(1)}, u32[]{:S(2)}, u32[]{:S(2)}) collective-permute-start(f32[8,1024]{1,0:T(8,128)S(1)} %get-tuple-element.21.refs_0_), channel_id=1, source_target_pairs={{0,4},{1,5},{2,6},{3,7},{4,0},{5,1},{6,2},{7,3},{8,12},{9,13},{10,... | collective-permute-start | bytes 98312 | tf_op jit(solution)/shard_map/ppermute | solution.py:329
  28.3 2.2 %collective-permute-start.6 = (f32[8,1024]{1,0:T(8,128)S(1)}, f32[8,1024]{1,0:T(8,128)S(1)}, u32[]{:S(2)}, u32[]{:S(2)}) collective-permute-start(f32[8,1024]{1,0:T(8,128)S(1)} %get-tuple-element.21.refs_0_), channel_id=1, source_target_pairs={{0,2},{1,3},{2,0},{3,1},{4,6},{5,7},{6,4},{7,5},{8,10},{9,11},{10,... | collective-permute-start | bytes 98312 | tf_op jit(solution)/shard_map/ppermute | solution.py:329
  30.5 0.9 %own_third.1.after.refs_2_ = f32[8,256]{1,0:T(8,128)S(1)} custom-call(f32[8,1024]{1,0:T(8,128)S(1)} %pack_group.1.after.refs_0_.pack, bf16[1024,32]{1,0:T(8,128)(2,1)S(1)} %get-tuple-element.14.dist, f32[1024,8]{1,0:T(8,128)S(1)} %get-tuple-element.15.s_col, bf16[32,1024]{1,0:T(8,128)(2,1)S(1)} %get-tuple-element.16.right, ...), custom_call_target="tpu_custom_call" | custom-call | flops 7864320 | bytes 65536 | tf_op jit(solution)/shard_map/own_third/pallas_call | solution.py:414
  31.5 0.3 collective-permute-start.11
  31.7 0.1 collective-permute-done.8.refs_3_
  32.0 0.4 %collective-permute-done.6.refs_1_ = f32[8,1024]{1,0:T(8,128)S(1)} collective-permute-done((f32[8,1024]{1,0:T(8,128)S(1)}, f32[8,1024]{1,0:T(8,128)S(1)}, u32[]{:S(2)}, u32[]{:S(2)}) %collective-permute-start.6) | collective-permute-done | bytes 32800 | tf_op jit(solution)/shard_map/ppermute | solution.py:329
  32.5 0.9 %own_fourth.1.refs_3_ = f32[8,256]{1,0:T(8,128)S(1)} custom-call(f32[8,1024]{1,0:T(8,128)S(1)} %pack_group.1.after.refs_0_.pack, bf16[1024,32]{1,0:T(8,128)(2,1)S(1)} %get-tuple-element.14.dist, f32[1024,8]{1,0:T(8,128)S(1)} %get-tuple-element.15.s_col, bf16[32,1024]{1,0:T(8,128)(2,1)S(1)} %get-tuple-element.16.right, ...), custom_call_target="tpu_custom_call" | custom-call | flops 7864320 | bytes 65536 | tf_op jit(solution)/shard_map/own_fourth/pallas_call | solution.py:435
  33.5 2.0 %collective-permute-done.11.part_b = f32[8,1024]{1,0:T(8,128)S(1)} collective-permute-done((f32[8,1024]{1,0:T(8,128)S(1)}, f32[8,1024]{1,0:T(8,128)S(1)}, u32[]{:S(2)}, u32[]{:S(2)}) %collective-permute-start.11) | collective-permute-done | bytes 32800 | tf_op jit(solution)/shard_map/ppermute | solution.py:329
  35.4 0.6 %sum_parts.1 = (f32[3,1024]{1,0:T(4,128)}, f32[3,1024]{1,0:T(4,128)}) custom-call(f32[8,1024]{1,0:T(8,128)S(1)} %get-tuple-element.22.after.keep_a, f32[8,1024]{1,0:T(8,128)S(1)} %get-tuple-element.23.keep_b, f32[8,1024]{1,0:T(8,128)S(1)} %collective-permute-done.10.part_a, f32[8,1024]{1,0:T(8,128)S(1)} %collective-permute-done.11.part_b, ...), custom_call_target="tpu_custom_call" | custom-call | tf_op jit(solution)/shard_map/sum_parts/pallas_call | solution.py:444
  (19 shorter events, 0.6 us)
Async XLA Ops:
  1.3 0.7 %copy-start.3 = (s32[2,1,1,2]{3,2,1,0:T(1,128)S(1)}, s32[2,1,1,2]{3,2,1,0:T(1,128)}, u32[]{:S(2)}) copy-start(s32[2,1,1,2]{3,2,1,0:T(1,128)} %pair_list.1) | copy-start | bytes 52
  2.0 0.7 %copy-start = (f32[3,1024]{1,0:T(4,128)S(1)}, f32[3,1024]{1,0:T(4,128)}, u32[]{:S(2)}) copy-start(f32[3,1024]{1,0:T(4,128)} %positions.1) | copy-start | bytes 36868
  2.7 0.7 %copy-start.1 = (f32[3,1024]{1,0:T(4,128)S(1)}, f32[3,1024]{1,0:T(4,128)}, u32[]{:S(2)}) copy-start(f32[3,1024]{1,0:T(4,128)} %strengths.1) | copy-start | bytes 36868
  3.4 0.7 %copy-start.2 = (f32[1024]{0:T(1024)S(1)}, f32[1024]{0:T(1024)}, u32[]{:S(2)}) copy-start(f32[1024]{0:T(1024)} %param.7) | copy-start | bytes 12292
  4.7 7.4 %collective-permute-start = (f32[8,1024]{1,0:T(8,128)S(1)}, f32[8,1024]{1,0:T(8,128)S(1)}, u32[]{:S(2)}, u32[]{:S(2)}) collective-permute-start(f32[8,1024]{1,0:T(8,128)S(1)} %pack_group.1.after.refs_0_.pack), channel_id=1, source_target_pairs={{0,16},{8,24},{16,0},{24,8},{1,17},{9,25},{17,1},{25,9},{2,18},{10... | collective-permute-start | bytes 98312 | tf_op jit(solution)/shard_map/ppermute | solution.py:329
  7.7 6.1 %collective-permute-start.3 = (f32[8,1024]{1,0:T(8,128)S(1)}, f32[8,1024]{1,0:T(8,128)S(1)}, u32[]{:S(2)}, u32[]{:S(2)}) collective-permute-start(f32[8,1024]{1,0:T(8,128)S(1)} %pack_group.1.after.refs_0_.pack), channel_id=1, source_target_pairs={{0,6},{1,7},{2,4},{3,5},{4,2},{5,3},{6,0},{7,1},{8,14},{9,15},{10,... | collective-permute-start | bytes 98312 | tf_op jit(solution)/shard_map/ppermute | solution.py:329
  11.3 4.8 %collective-permute-start.2 = (f32[8,1024]{1,0:T(8,128)S(1)}, f32[8,1024]{1,0:T(8,128)S(1)}, u32[]{:S(2)}, u32[]{:S(2)}) collective-permute-start(f32[8,1024]{1,0:T(8,128)S(1)} %pack_group.1.after.refs_0_.pack), channel_id=1, source_target_pairs={{0,4},{1,5},{2,6},{3,7},{4,0},{5,1},{6,2},{7,3},{8,12},{9,13},{10,... | collective-permute-start | bytes 98312 | tf_op jit(solution)/shard_map/ppermute | solution.py:329
  11.3 4.8 %collective-permute-start.1 = (f32[8,1024]{1,0:T(8,128)S(1)}, f32[8,1024]{1,0:T(8,128)S(1)}, u32[]{:S(2)}, u32[]{:S(2)}) collective-permute-start(f32[8,1024]{1,0:T(8,128)S(1)} %pack_group.1.after.refs_0_.pack), channel_id=1, source_target_pairs={{0,2},{1,3},{2,0},{3,1},{4,6},{5,7},{6,4},{7,5},{8,10},{9,11},{10,... | collective-permute-start | bytes 98312 | tf_op jit(solution)/shard_map/ppermute | solution.py:329
  16.2 4.6 %collective-permute-start.4 = (f32[4,8,1024]{2,1,0:T(8,128)S(1)}, f32[4,8,1024]{2,1,0:T(8,128)S(1)}, u32[]{:S(2)}, u32[]{:S(2)}) collective-permute-start(f32[4,8,1024]{2,1,0:T(8,128)S(1)} %stack_col.1.after.near_a), channel_id=1, source_target_pairs={{0,1},{1,0},{2,3},{3,2},{4,5},{5,4},{6,7},{7,6},{8,9},{9,8},{10,11... | collective-permute-start | bytes 393224 | tf_op jit(solution)/shard_map/ppermute | solution.py:329
  16.2 4.5 %collective-permute-start.5 = (f32[2,8,1024]{2,1,0:T(8,128)S(1)}, f32[2,8,1024]{2,1,0:T(8,128)S(1)}, u32[]{:S(2)}, u32[]{:S(2)}) collective-permute-start(f32[2,8,1024]{2,1,0:T(8,128)S(1)} %stack_row.1.after.near_b), channel_id=1, source_target_pairs={{0,8},{8,0},{16,24},{24,16},{1,9},{9,1},{17,25},{25,17},{2,10},{10... | collective-permute-start | bytes 196616 | tf_op jit(solution)/shard_map/ppermute | solution.py:329
  25.9 5.5 %collective-permute-start.9 = (f32[8,1024]{1,0:T(8,128)S(1)}, f32[8,1024]{1,0:T(8,128)S(1)}, u32[]{:S(2)}, u32[]{:S(2)}) collective-permute-start(f32[8,1024]{1,0:T(8,128)S(1)} %get-tuple-element.20.after.refs_0_), channel_id=1, source_target_pairs={{0,16},{8,24},{16,0},{24,8},{1,17},{9,25},{17,1},{25,9},{2,18},{10... | collective-permute-start | bytes 98312 | tf_op jit(solution)/shard_map/ppermute | solution.py:329
  26.0 5.8 %collective-permute-start.8 = (f32[8,1024]{1,0:T(8,128)S(1)}, f32[8,1024]{1,0:T(8,128)S(1)}, u32[]{:S(2)}, u32[]{:S(2)}) collective-permute-start(f32[8,1024]{1,0:T(8,128)S(1)} %get-tuple-element.21.refs_0_), channel_id=1, source_target_pairs={{0,6},{1,7},{2,4},{3,5},{4,2},{5,3},{6,0},{7,1},{8,14},{9,15},{10,... | collective-permute-start | bytes 98312 | tf_op jit(solution)/shard_map/ppermute | solution.py:329
  26.1 5.9 %collective-permute-start.7 = (f32[8,1024]{1,0:T(8,128)S(1)}, f32[8,1024]{1,0:T(8,128)S(1)}, u32[]{:S(2)}, u32[]{:S(2)}) collective-permute-start(f32[8,1024]{1,0:T(8,128)S(1)} %get-tuple-element.21.refs_0_), channel_id=1, source_target_pairs={{0,4},{1,5},{2,6},{3,7},{4,0},{5,1},{6,2},{7,3},{8,12},{9,13},{10,... | collective-permute-start | bytes 98312 | tf_op jit(solution)/shard_map/ppermute | solution.py:329
  28.3 4.1 %collective-permute-start.6 = (f32[8,1024]{1,0:T(8,128)S(1)}, f32[8,1024]{1,0:T(8,128)S(1)}, u32[]{:S(2)}, u32[]{:S(2)}) collective-permute-start(f32[8,1024]{1,0:T(8,128)S(1)} %get-tuple-element.21.refs_0_), channel_id=1, source_target_pairs={{0,2},{1,3},{2,0},{3,1},{4,6},{5,7},{6,4},{7,5},{8,10},{9,11},{10,... | collective-permute-start | bytes 98312 | tf_op jit(solution)/shard_map/ppermute | solution.py:329
  31.5 4.0 %collective-permute-start.11 = (f32[8,1024]{1,0:T(8,128)S(1)}, f32[8,1024]{1,0:T(8,128)S(1)}, u32[]{:S(2)}, u32[]{:S(2)}) collective-permute-start(f32[8,1024]{1,0:T(8,128)S(1)} %get-tuple-element.25), channel_id=1, source_target_pairs={{0,8},{8,0},{16,24},{24,16},{1,9},{9,1},{17,25},{25,17},{2,10},{10... | collective-permute-start | bytes 98312 | tf_op jit(solution)/shard_map/ppermute | solution.py:329
  32.5 3.0 %collective-permute-start.10 = (f32[8,1024]{1,0:T(8,128)S(1)}, f32[8,1024]{1,0:T(8,128)S(1)}, u32[]{:S(2)}, u32[]{:S(2)}) collective-permute-start(f32[8,1024]{1,0:T(8,128)S(1)} %get-tuple-element.24), channel_id=1, source_target_pairs={{0,1},{1,0},{2,3},{3,2},{4,5},{5,4},{6,7},{7,6},{8,9},{9,8},{10,11... | collective-permute-start | bytes 98312 | tf_op jit(solution)/shard_map/ppermute | solution.py:329

commit v3 on v2

v3 whole, which is shorter than its diff:
```python
import functools
import math

import jax
import jax.numpy as jnp
from jax import lax
from jax.experimental import pallas as pl
from jax.experimental.pallas import tpu as pltpu
from jax.sharding import PartitionSpec as P

F32 = jnp.float32
BF16 = jnp.bfloat16
UNIT = 256
STRIP = 16
G_ROWS = 32
H_ROWS = 96
Q_ROWS = 32
G_SCALE = -1.5 / (4.0 * math.pi)
H_SCALE = 7.5 / (4.0 * math.pi)
VMEM = 48 * 1024 * 1024


def cross(u, v):
    return jnp.concatenate(
        [
            u[1:2] * v[2:3] - u[2:3] * v[1:2],
            u[2:3] * v[0:1] - u[0:1] * v[2:3],
            u[0:1] * v[1:2] - u[1:2] * v[0:1],
        ]
    )


def split(f):
    hi = f.astype(BF16).astype(F32)
    mid = (f - hi).astype(BF16).astype(F32)
    return [hi, mid, (f - hi) - mid]


def features(pack):
    pos = pack[0:3] - 0.5
    st = pack[3:6]
    e0 = jnp.concatenate([st, cross(pos, st), jnp.zeros((2, pack.shape[1]), F32)])
    moments = jnp.concatenate([e0, pos[0:1] * e0, pos[1:2] * e0, pos[2:3] * e0])
    for_g = jnp.concatenate(split(e0) + [jnp.zeros_like(e0)]).astype(BF16)
    return for_g, jnp.concatenate(split(moments)).astype(BF16)


def finish(pack, g, h):
    g = g[0:8] + g[8:16] + g[16:24]
    h = h[0:32] + h[32:64] + h[64:96]
    pos = pack[0:3] - 0.5
    st = pack[3:6]
    dot = jnp.sum(pos * st, axis=0, keepdims=True)
    d = dot * h[0:8] - st[0:1] * h[8:16] - st[1:2] * h[16:24] - st[2:3] * h[24:32]
    vel = G_SCALE * (cross(pos, g[0:3]) - g[3:6])
    stretch = G_SCALE * cross(st, g[0:3]) + H_SCALE * (cross(pos, d[0:3]) - d[3:6])
    return jnp.concatenate([vel, stretch])


def store_dense(out, value):
    rows = value.shape[0]
    for n in range(value.shape[1] // 128):
        out[n * rows : (n + 1) * rows, :] = value[:, n * 128 : (n + 1) * 128]


def load_dense(value, rows):
    return jnp.concatenate([value[n : n + rows] for n in range(0, value.shape[0], rows)], axis=1)


def strip(qq, s, images, r):
    ghi, glo, hhi, hlo = images
    here = slice(r, r + STRIP)
    t = lax.rsqrt(qq)
    t2 = t * t
    v = s * t2
    t3 = t2 * t
    g = t3 * (v + 2.0 / 3.0)
    h = (t3 * t2) * (v + 0.4)
    high = g.astype(BF16)
    ghi[here] = high
    glo[here] = (g - high.astype(F32)).astype(BF16)
    high = h.astype(BF16)
    hhi[here] = high
    hlo[here] = (h - high.astype(F32)).astype(BF16)


def down(f, image):
    return jnp.dot(f, image, preferred_element_type=F32)


def across(f, image):
    return lax.dot_general(f, image, (((1,), (1,)), ((), ())), preferred_element_type=F32)


def halves(pack):
    return 0.5 * pack[6:7] * pack[6:7]


def distances(pack):
    pos = pack[0:3] - 0.5
    x1, x2, x3 = split(pos)
    norm = jnp.concatenate(split(jnp.sum(pos * pos, axis=0, keepdims=True) + halves(pack)))
    one = jnp.ones_like(norm)
    blank = jnp.zeros((8, pack.shape[1]), F32)
    left = [-2.0 * x for x in (x1, x1, x2, x2, x1, x3)] + [norm, one, blank]
    right = [x1, x2, x1, x2, x3, x1, one, norm, blank]
    return jnp.concatenate(left), jnp.concatenate(right).astype(BF16)


def columns(pack, dist, spread_s):
    left, right = distances(pack)
    dist[...] = jnp.transpose(left).astype(BF16)
    spread_s[...] = jnp.transpose(jnp.broadcast_to(halves(pack), (8, pack.shape[1])))
    return right


def interact(dist_a, s_a, dist_b, s_b, feat_a, qq, slots, sums_b):
    for total in sums_b:
        total[...] = jnp.zeros_like(total)

    def products(i, j, images):
        pi, pj = slice(i, i + UNIT), slice(j, j + UNIT)
        steps = []

        def add(total, f, high, low):
            total[:, pj] += down(f, high[...]) + down(f, low[...])

        for kind in range(2):
            f = feat_a[kind][:, pi]
            steps.append(functools.partial(add, sums_b[kind], f, *images[2 * kind : 2 * kind + 2]))
        return steps

    def measure(unit, into):
        i, j = unit
        into[...] = down(dist_a[i : i + UNIT, :], dist_b[:, j : j + UNIT])

    n_strip = UNIT // STRIP
    units = [(i, j) for j in range(0, s_b.shape[1], UNIT) for i in range(0, s_a.shape[0], UNIT)]
    measure(units[0], qq[0])
    waiting = []
    for count, (i, j) in enumerate(units):
        images = slots[count % 2]
        if count + 1 < len(units):
            waiting.insert(0, functools.partial(measure, units[count + 1], qq[(count + 1) % 2]))
        per = n_strip // max(1, len(waiting))
        row = jnp.broadcast_to(s_b[0:1, j : j + UNIT], (STRIP, UNIT))
        for n in range(n_strip):
            at = slice(i + n * STRIP, i + (n + 1) * STRIP)
            here = slice(n * STRIP, (n + 1) * STRIP)
            strip(qq[count % 2][here, :], s_a[at, 0:1] + row, images, n * STRIP)
            if waiting and (n + 1) % per == 0:
                waiting.pop(0)()
        for step in waiting:
            step()
        waiting = products(i, j, images)
    for step in waiting:
        step()


def interact_both(dist_a, s_a, dist_b, s_b, feat_a, feat_b, qq, images, sums_a, sums_b):
    rows, n = s_a.shape[0], UNIT
    blocks, chunks = s_b.shape[1] // n, rows // n
    half = rows // 2

    def measure(block, c):
        here, part = slice(c * n, (c + 1) * n), slice(block * n, (block + 1) * n)
        qq[block % 2][here, :] = down(dist_a[here, :], dist_b[:, part])

    def onto_a(block, c, kind):
        here, part = slice(c * n, (c + 1) * n), slice(block * n, (block + 1) * n)
        f = jnp.concatenate([feat_b[kind][:, part]] * 2, axis=1)
        share = across(f, images[block % 2][here, 2 * kind * n : 2 * (kind + 1) * n])
        sums_a[kind][:, here] = share if block == 0 else sums_a[kind][:, here] + share

    def onto_b(block, later, kind):
        here, part = slice(later * half, (later + 1) * half), slice(block * n, (block + 1) * n)
        image = images[block % 2]
        at = 2 * kind * n
        f = feat_a[kind][:, here]
        share = down(f, image[here, at : at + n]) + down(f, image[here, at + n : at + 2 * n])
        sums_b[kind][:, part] = sums_b[kind][:, part] + share if later else share

    for c in range(chunks):
        measure(0, c)
    ready, delayed = [], []
    for block in range(blocks):
        image = images[block % 2]
        part = slice(block * n, (block + 1) * n)
        slots = [image.at[:, m * n : (m + 1) * n] for m in range(4)]
        row = jnp.broadcast_to(s_b[0:1, part], (STRIP, n))
        for c in range(chunks):
            todo, ready, delayed = ready, delayed, []
            if block + 1 < blocks:
                todo.append(functools.partial(measure, block + 1, c))
            n_strip = n // STRIP
            per = max(1, n_strip // max(1, len(todo)))
            for m in range(n_strip):
                here = slice(c * n + m * STRIP, c * n + (m + 1) * STRIP)
                strip(qq[block % 2][here, :], s_a[here, 0:1] + row, slots, c * n + m * STRIP)
                if todo and (m + 1) % per == 0:
                    todo.pop(0)()
            for step in todo:
                step()
            for kind in range(2):
                ready.append(functools.partial(onto_a, block, c, kind))
            if (c + 1) % (chunks // 2) == 0:
                later = (c + 1) // (chunks // 2) - 1
                ready.append(functools.partial(onto_b, block, later, 0))
                delayed.append(functools.partial(onto_b, block, later, 1))
    for step in ready + delayed:
        step()


def own_chunk(n, pack, dist, s_col, right, feat, out, sums, qq, slots):
    part = slice(n * out.shape[1], (n + 1) * out.shape[1])
    interact(dist, s_col, right[:, part], halves(pack[:, part]), feat, qq, slots, sums)
    out[...] = finish(pack[:, part], sums[0][...], sums[1][...])


def first_kernel(pack, out, dist, s_col, right, feat_g, feat_h, b_g, b_h, *flat):
    right[...] = columns(pack[...], dist, s_col)
    feat_g[...], feat_h[...] = features(pack[...])
    own_chunk(0, pack, dist, s_col, right, (feat_g, feat_h), out, (b_g, b_h), flat[0:2], (flat[2:6], flat[6:10]))


def later_kernel(n, pack, dist, s_col, right, feat_g, feat_h, after, out, b_g, b_h, *flat):
    del after
    own_chunk(n, pack, dist, s_col, right, (feat_g, feat_h), out, (b_g, b_h), flat[0:2], (flat[2:6], flat[6:10]))


def pack_kernel(positions, strengths, radii, pair_list, pair_count, pack, listed, count, sems):
    copies = [
        pltpu.make_async_copy(pair_list, listed, sems.at[0]),
        pltpu.make_async_copy(pair_count, count, sems.at[1]),
        pltpu.make_async_copy(positions, pack.at[0:3], sems.at[2]),
        pltpu.make_async_copy(strengths, pack.at[3:6], sems.at[3]),
        pltpu.make_async_copy(radii, pack.at[6:7], sems.at[4]),
    ]
    for copy in copies:
        copy.start()
    for copy in copies[:2]:
        copy.wait()
    for n, value in enumerate((listed[0, 0, 0, 1], listed[1, 0, 0, 1], count[0, 0])):
        pack[7:8, n * 128 : (n + 1) * 128] = jnp.full((1, 128), value.astype(F32))
    rest = pack.shape[1] - 3 * 128
    pack[7:8, 3 * 128 :] = jnp.zeros((1, rest), F32)
    for copy in copies[2:]:
        copy.wait()


def here(axis):
    return lax.axis_index(axis).astype(jnp.int32)


def stack_kernel(n_pairs, *refs):
    for n in range(n_pairs):
        first, second, both = refs[2 * n], refs[2 * n + 1], refs[n - n_pairs]
        size = first.shape[0]
        both[0:size] = first[...]
        both[size : 2 * size] = second[...]


def place(relative, bits):
    at = 0
    for n in range(bits):
        at += ((relative >> n) & 1) << (bits - 1 - n)
    return at


def listed(pack):
    return [pack[7:8, n * 128 : (n + 1) * 128] for n in range(3)]


def pair_kernel(pack, near_a, far_a, b_0, b_1, b_2, b_3, after, out_a, out_b, apack, bpack, dist, s_col, *rest):
    del after
    sums_a, sums_b, qq, images = rest[0:2], rest[2:4], rest[4:6], rest[6:8]
    k, m, count = [jnp.max(value).astype(jnp.int32) for value in listed(pack)]

    @pl.when(count > 1)
    def _():
        from_a = k ^ here("col")
        from_b = m ^ here("row")
        at = place(from_a >> 1, near_a.shape[0].bit_length() - 1)
        apack[...] = jnp.where(from_a % 2 == 0, near_a[at], far_a[at])
        at = place(from_b >> 2, b_0.shape[0].bit_length() - 1)
        for n, block in enumerate((b_0, b_1, b_2, b_3)):

            @pl.when(from_b % 4 == n)
            def _(block=block):
                bpack[...] = block[at]

        columns(apack[...], dist, s_col)
        right = distances(bpack[...])[1]
        feat_a, feat_b = features(apack[...]), features(bpack[...])
        interact_both(dist, s_col, right, halves(bpack[...]), feat_a, feat_b, qq, images, sums_a, sums_b)
        store_dense(out_a, finish(apack[...], sums_a[0][...], sums_a[1][...]))
        store_dense(out_b, finish(bpack[...], sums_b[0][...], sums_b[1][...]))


def merge_kernel(axis, n_parts, *refs):
    parts, packs, (keep, send) = refs[:n_parts], refs[n_parts:-2], refs[-2:]
    at = here(axis)
    total = onward = jnp.zeros(keep.shape, F32)
    for n, part in enumerate(parts):
        relative = 2 * n
        if axis == "col":
            k, m, count = listed(packs[0][place(n, packs[0].shape[0].bit_length() - 1)])
            target = jnp.where(count > 1, k, -1.0)
        else:
            run = packs[1] if relative & 2 else packs[0]
            k, m, count = listed(run[place(relative >> 2, run.shape[0].bit_length() - 1)])
            itself = (k == here("col").astype(F32)) & (m == (at ^ relative).astype(F32))
            target = jnp.where((count > 1) & ~itself, m, -1.0)
        block = part[...]
        total += jnp.where(target == at.astype(F32), block, 0.0)
        onward += jnp.where(target == (at ^ 1).astype(F32), block, 0.0)
    keep[...] = total
    send[...] = onward


def sum_kernel(keep_a, keep_b, part_a, part_b, *refs):
    own, (velocity, stretching) = refs[:-2], refs[-2:]
    total = load_dense(keep_a[...] + keep_b[...] + part_a[...] + part_b[...], 6)
    total += jnp.concatenate([chunk[...] for chunk in own], axis=1)
    velocity[...] = total[0:3]
    stretching[...] = total[3:6]


def own_work(cols):
    return [
        pltpu.VMEM((G_ROWS, cols), F32),
        pltpu.VMEM((H_ROWS, cols), F32),
        *[pltpu.VMEM((UNIT, UNIT), F32)] * 2,
        *[pltpu.VMEM((UNIT, UNIT), BF16)] * 8,
    ]


def pair_work(g):
    return [
        *[pltpu.VMEM((8, g), F32)] * 2,
        pltpu.VMEM((g, Q_ROWS), BF16),
        pltpu.VMEM((g, 8), F32),
        *[pltpu.VMEM((G_ROWS, g), F32), pltpu.VMEM((H_ROWS, g), F32)] * 2,
        *[pltpu.VMEM((g, UNIT), F32)] * 2,
        *[pltpu.VMEM((g, 4 * UNIT), BF16)] * 2,
    ]


def swap(block, axis, size, step):
    return lax.ppermute(block, axis, [(i, i ^ step) for i in range(size)])


def spread(block, axis, size):
    return [block] + [swap(block, axis, size, s) for s in range(2, size, 2)]


def local(n_row, n_col, positions, strengths, radii, pair_list, pair_count):
    g = radii.shape[0]
    part = g // 4
    hbm_spec = pl.BlockSpec(memory_space=pltpu.HBM)
    vmem_spec = pl.BlockSpec(memory_space=pltpu.VMEM)
    params = pltpu.CompilerParams(vmem_limit_bytes=VMEM)
    block = jax.ShapeDtypeStruct((8, g), F32)
    chunk = jax.ShapeDtypeStruct((6, part), F32)
    dense = jax.ShapeDtypeStruct((6 * g // 128, 128), F32)
    chunk_cost = pl.CostEstimate(flops=30 * g * part, bytes_accessed=64 * g, transcendentals=g * part)
    chunk_call = functools.partial(
        pl.pallas_call, scratch_shapes=own_work(part), compiler_params=params, cost_estimate=chunk_cost
    )

    def later(n, after):
        return chunk_call(
            functools.partial(later_kernel, n),
            out_shape=chunk,
            in_specs=[vmem_spec] * 7,
            out_specs=vmem_spec,
            name=f"own_{n}",
        )(pack, *common, after)

    pack = pl.pallas_call(
        pack_kernel,
        out_shape=block,
        in_specs=[hbm_spec] * 5,
        out_specs=vmem_spec,
        scratch_shapes=[
            pltpu.SMEM(pair_list.shape, jnp.int32),
            pltpu.SMEM(pair_count.shape, jnp.int32),
            pltpu.SemaphoreType.DMA((5,)),
        ],
        name="pack_group",
    )(positions, strengths, radii[None], pair_list, pair_count)

    own = []
    common = ()
    near_a, have_b = pack[None], pack[None]
    after = pack
    for stage in range(n_col.bit_length() - 1):
        step_a, step_b = n_col >> (1 + stage), n_row >> (1 + stage)
        far_a = swap(near_a, "col", n_col, step_a)
        if step_b >= 2:
            far_b = swap(have_b, "row", n_row, step_b)
            if step_b == 2:
                next_b = swap(have_b, "row", n_row, 1)
        elif step_b == 1:
            last_b = swap(far_b, "row", n_row, 1)
        if stage == 0:
            chunk_0, *common = chunk_call(
                first_kernel,
                out_shape=(
                    chunk,
                    jax.ShapeDtypeStruct((g, Q_ROWS), BF16),
                    jax.ShapeDtypeStruct((g, 8), F32),
                    jax.ShapeDtypeStruct((Q_ROWS, g), BF16),
                    jax.ShapeDtypeStruct((G_ROWS, g), BF16),
                    jax.ShapeDtypeStruct((H_ROWS, g), BF16),
                ),
                in_specs=[vmem_spec],
                out_specs=(vmem_spec,) * 6,
                name="own_first",
            )(pack)
            own.append(chunk_0)
        elif stage < 3:
            own.append(later(stage, after))
        if step_a == 1:
            break
        runs = [(near_a, far_a)]
        if step_b > 2:
            runs.append((have_b, far_b))
        arrived = [own[-1], last_b if step_b == 1 else far_b]
        if step_b == 2:
            arrived.append(next_b)
        stacked = pl.pallas_call(
            functools.partial(stack_kernel, len(runs)),
            out_shape=tuple(jax.ShapeDtypeStruct((2 * n.shape[0], 8, g), F32) for n, _ in runs),
            in_specs=[vmem_spec] * (2 * len(runs) + len(arrived)),
            out_specs=(vmem_spec,) * len(runs),
            compiler_params=params,
            name="stack_groups",
        )(*[block for run in runs for block in run], *arrived)
        near_a = after = stacked[0]
        if len(runs) > 1:
            have_b = stacked[1]

    side_a, side_b = pl.pallas_call(
        pair_kernel,
        out_shape=(dense, dense),
        in_specs=[vmem_spec] * 8,
        out_specs=(vmem_spec, vmem_spec),
        scratch_shapes=pair_work(g),
        compiler_params=params,
        cost_estimate=pl.CostEstimate(flops=60 * g * g, bytes_accessed=128 * g, transcendentals=g * g),
        name="listed_pair",
    )(pack, near_a, far_a, have_b, next_b, far_b, last_b, own[-1])

    def merge(parts, packs, axis):
        return pl.pallas_call(
            functools.partial(merge_kernel, axis, len(parts)),
            out_shape=(dense,) * 2,
            in_specs=[vmem_spec] * (len(parts) + len(packs)),
            out_specs=(vmem_spec,) * 2,
            compiler_params=params,
            name="merge_" + axis,
        )(*parts, *packs)

    parts_a = spread(side_a, "col", n_col)
    parts_b = spread(side_b, "row", n_row)
    keep_b, send_b = merge(parts_b, [have_b, far_b], "row")
    far_b = swap(send_b, "row", n_row, 1)
    keep_a, send_a = merge(parts_a, [near_a], "col")
    far_a = swap(send_a, "col", n_col, 1)
    own.append(later(3, keep_a))

    three = jax.ShapeDtypeStruct((3, g), F32)
    return pl.pallas_call(
        sum_kernel,
        out_shape=(three, three),
        in_specs=[vmem_spec] * 8,
        out_specs=(vmem_spec, vmem_spec),
        compiler_params=params,
        name="sum_parts",
    )(keep_a, keep_b, far_a, far_b, *own)


def solution(mesh):
    placed = (
        P(None, ("row", "col")),
        P(None, ("row", "col")),
        P(("row", "col")),
        P(None, "row", "col", None),
        P("row", "col"),
    )
    return jax.shard_map(
        functools.partial(local, mesh.shape["row"], mesh.shape["col"]),
        mesh=mesh,
        in_specs=placed,
        out_specs=(P(None, ("row", "col")), P(None, ("row", "col"))),
        check_vma=False,
    )
```

time: 36.7 us -> 34 us (0.926); the launches traced: 36.1 us -> 33.9 us
  starting transfers between devices: 13.9 us -> 19.3 us
  Pallas kernels: 10.6 us -> 6.25 us
  local copies, waits for them, and re-layouts: 2.79 us -> 0.8 us
  waiting for transfers between devices: 7.39 us -> 6.16 us
    ppermute x12, starting transfers between devices: 13.9 us -> 19.3 us  [swap(): return lax.ppermute(block, axis, [(i, i ^ step) for i in range(size)])]
    pallas_call x8, Pallas kernels: 8.04 us -> 2.95 us  [the longest x3 2.77 us: later(): chunk_call(functools.partial(later_kernel, n), out_shape=chunk, in_specs=...]
    unnamed x8 -> x4, local copies, waits for them, and re-layouts: 2.79 us -> 0.8 us
    ppermute x12, waiting for transfers between devices: 7.39 us -> 6.16 us  [swap(): return lax.ppermute(block, axis, [(i, i ^ step) for i in range(size)])]
    pallas_call x1, Pallas kernels: 0.61 us -> 1.38 us  [local(): pl.pallas_call(pack_kernel, out_shape=block, in_specs=[hbm_spec] * 5, out...]
  transfers between devices with their start and end apart: 12 -> 12, of which waited for: 7 -> 5; matrix products, arithmetic and copies ran while one was open for 0% -> 0% of each run, Pallas kernels for 11% -> 12%
where the time goes in v3:
time: 34 us; the launch traced here: 33.9 us
  starting transfers between devices  19.3 us (57%)
  Pallas kernels  6.25 us (18%)
  waiting for transfers between devices  6.16 us (18%)
  between operations  1.4 us (4%)
  local copies, waits for them, and re-layouts  0.8 us (2%)
    ppermute x12, starting transfers between devices, swap(): return lax.ppermute(block, axis, [(i, i ^ step) for i in range(size)])  19.3 us
    ppermute x12, waiting for transfers between devices, swap(): return lax.ppermute(block, axis, [(i, i ^ step) for i in range(size)])  6.16 us
    pallas_call x3, Pallas kernels, later(): chunk_call(functools.partial(later_kernel, n), out_shape=chunk, in_specs=...  2.77 us
    pallas_call x1, Pallas kernels, local(): pl.pallas_call(pack_kernel, out_shape=block, in_specs=[hbm_spec] * 5, out...  1.38 us
    pallas_call x1, Pallas kernels, local(): chunk_call(first_kernel, out_shape=(chunk, jax.ShapeDtypeStruct((g, Q_ROW...  1.29 us
    unnamed x4, local copies, waits for them, and re-layouts  0.8 us
  transfers between devices with their start and end apart: 12, of which 5 were waited for; matrix products, arithmetic and copies ran while one was open for 0% of the time, Pallas kernels for 12%

profile of v3, /device:TPU:0, one launch (start us, length us, event | category | flops | bytes accessed | tf_op | source)
XLA Modules:
  0.0 33.9 jit_solution(6097824839094565489)
XLA Ops:
  1.3 1.4 %pack_group.1.pack = f32[8,1024]{1,0:T(8,128)} custom-call(f32[3,1024]{1,0:T(4,128)} %positions.1, f32[3,1024]{1,0:T(4,128)} %strengths.1, f32[1,1024]{1,0:T(1,128)} %bitcast.8, s32[2,1,1,2]{3,2,1,0:T(1,128)} %pair_list.1, s32[1,1]{1,0:T(1,128)S(6)} %copy.7.pair_count), custom_call_target="tpu_custom_call" | custom-call | tf_op jit(solution)/shard_map/pack_group/pallas_call | solution.py:380
  2.7 3.0 %collective-permute-start.2 = (f32[1,8,1024]{2,1,0:T(8,128)}, f32[1,8,1024]{2,1,0:T(8,128)S(1)}, u32[]{:S(2)}, u32[]{:S(2)}) collective-permute-start(f32[1,8,1024]{2,1,0:T(8,128)} %bitcast.2), channel_id=1, source_target_pairs={{0,8},{8,0},{16,24},{24,16},{1,9},{9,1},{17,25},{25,17},{2,10},{10... | collective-permute-start | bytes 98312 | tf_op jit(solution)/shard_map/ppermute | solution.py:350
  5.7 1.5 %collective-permute-start.1 = (f32[1,8,1024]{2,1,0:T(8,128)}, f32[1,8,1024]{2,1,0:T(8,128)S(1)}, u32[]{:S(2)}, u32[]{:S(2)}) collective-permute-start(f32[1,8,1024]{2,1,0:T(8,128)} %bitcast.3), channel_id=1, source_target_pairs={{0,16},{8,24},{16,0},{24,8},{1,17},{9,25},{17,1},{25,9},{2,18},{10... | collective-permute-start | bytes 98312 | tf_op jit(solution)/shard_map/ppermute | solution.py:350
  7.2 2.6 %collective-permute-start = (f32[1,8,1024]{2,1,0:T(8,128)}, f32[1,8,1024]{2,1,0:T(8,128)S(1)}, u32[]{:S(2)}, u32[]{:S(2)}) collective-permute-start(f32[1,8,1024]{2,1,0:T(8,128)} %bitcast.4), channel_id=1, source_target_pairs={{0,4},{1,5},{2,6},{3,7},{4,0},{5,1},{6,2},{7,3},{8,12},{9,13},{10,... | collective-permute-start | bytes 98312 | tf_op jit(solution)/shard_map/ppermute | solution.py:350
  9.8 0.8 %copy-done = f32[8,1024]{1,0:T(8,128)S(1)} copy-done((f32[8,1024]{1,0:T(8,128)S(1)}, f32[8,1024]{1,0:T(8,128)}, u32[]{:S(2)}) %copy-start) | copy-done | bytes 32792
  10.6 1.3 %own_first.1 = (f32[6,256]{1,0:T(8,128)S(1)}, bf16[1024,32]{1,0:T(8,128)(2,1)S(1)}, f32[1024,8]{1,0:T(8,128)S(1)}, bf16[32,1024]{1,0:T(8,128)(2,1)S(1)}, bf16[32...) custom-call(f32[8,1024]{1,0:T(8,128)S(1)} %copy-done), custom_call_target="tpu_custom_call" | custom-call | flops 7864320 | bytes 65536 | tf_op jit(solution)/shard_map/own_first/pallas_call | solution.py:407
  11.9 0.3 collective-permute-done.refs_1_
  12.2 1.6 %collective-permute-start.3 = (f32[2,8,1024]{2,1,0:T(8,128)S(1)}, f32[2,8,1024]{2,1,0:T(8,128)S(1)}, u32[]{:S(2)}, u32[]{:S(2)}) collective-permute-start(f32[2,8,1024]{2,1,0:T(8,128)S(1)} %stack_groups.2.after.refs_0_), channel_id=1, source_target_pairs={{0,2},{1,3},{2,0},{3,1},{4,6},{5,7},{6,4},{7,5},{8,10},{9,11},{10,... | collective-permute-start | bytes 196616 | tf_op jit(solution)/shard_map/ppermute | solution.py:350
  13.8 0.5 %collective-permute-start.4 = (f32[1,8,1024]{2,1,0:T(8,128)S(1)}, f32[1,8,1024]{2,1,0:T(8,128)S(1)}, u32[]{:S(2)}, u32[]{:S(2)}) collective-permute-start(f32[1,8,1024]{2,1,0:T(8,128)S(1)} %collective-permute-done.1.refs_3_.b_2), channel_id=1, source_target_pairs={{0,8},{8,0},{16,24},{24,16},{1,9},{9,1},{17,25},{25,17},{2,10},{10... | collective-permute-start | bytes 98312 | tf_op jit(solution)/shard_map/ppermute | solution.py:350
  14.3 0.9 %own_1.1.refs_2_.refs_1_ = f32[6,256]{1,0:T(8,128)S(1)} custom-call(f32[8,1024]{1,0:T(8,128)S(1)} %copy-done, bf16[1024,32]{1,0:T(8,128)(2,1)S(1)} %get-tuple-element.15.dist, f32[1024,8]{1,0:T(8,128)S(1)} %get-tuple-element.16.s_col, bf16[32,1024]{1,0:T(8,128)(2,1)S(1)} %get-tuple-element.17.right, bf16[32,1024]{1,0:T(8,128)(2,1)S(1)} %get-tuple-element.18.feat_g, ...), custom_call_target="tpu_custom_call" | custom-call | flops 7864320 | bytes 65536 | tf_op jit(solution)/shard_map/own_1/pallas_call | solution.py:372
  15.3 2.4 %collective-permute-done.4.refs_3_.b_3 = f32[1,8,1024]{2,1,0:T(8,128)S(1)} collective-permute-done((f32[1,8,1024]{2,1,0:T(8,128)S(1)}, f32[1,8,1024]{2,1,0:T(8,128)S(1)}, u32[]{:S(2)}, u32[]{:S(2)}) %collective-permute-start.4) | collective-permute-done | bytes 32800 | tf_op jit(solution)/shard_map/ppermute | solution.py:350
  17.7 0.1 collective-permute-start.5
  17.8 0.9 %own_2.1.after.refs_2_ = f32[6,256]{1,0:T(8,128)S(1)} custom-call(f32[8,1024]{1,0:T(8,128)S(1)} %copy-done.1, bf16[1024,32]{1,0:T(8,128)(2,1)S(1)} %get-tuple-element.15.dist, f32[1024,8]{1,0:T(8,128)S(1)} %get-tuple-element.16.s_col, bf16[32,1024]{1,0:T(8,128)(2,1)S(1)} %get-tuple-element.17.right, bf16[32,1024]{1,0:T(8,128)(2,1)S(1)} %get-tuple-element.18.feat_g, ...), custom_call_target="tpu_custom_call" | custom-call | flops 7864320 | bytes 65536 | tf_op jit(solution)/shard_map/own_2/pallas_call | solution.py:372
  18.7 0.4 %collective-permute-done.5.far_a = f32[4,8,1024]{2,1,0:T(8,128)S(1)} collective-permute-done((f32[4,8,1024]{2,1,0:T(8,128)S(1)}, f32[4,8,1024]{2,1,0:T(8,128)S(1)}, u32[]{:S(2)}, u32[]{:S(2)}) %collective-permute-start.5) | collective-permute-done | bytes 131104 | tf_op jit(solution)/shard_map/ppermute | solution.py:350
  19.1 0.1 listed_pair.1
  19.3 0.6 %collective-permute-start.9 = (f32[48,128]{1,0:T(8,128)S(1)}, f32[48,128]{1,0:T(8,128)S(1)}, u32[]{:S(2)}, u32[]{:S(2)}) collective-permute-start(f32[48,128]{1,0:T(8,128)S(1)} %get-tuple-element.22.refs_0_), channel_id=1, source_target_pairs={{0,16},{8,24},{16,0},{24,8},{1,17},{9,25},{17,1},{25,9},{2,18},{10... | collective-permute-start | bytes 73736 | tf_op jit(solution)/shard_map/ppermute | solution.py:350
  19.8 7.4 %collective-permute-start.8 = (f32[48,128]{1,0:T(8,128)S(1)}, f32[48,128]{1,0:T(8,128)S(1)}, u32[]{:S(2)}, u32[]{:S(2)}) collective-permute-start(f32[48,128]{1,0:T(8,128)S(1)} %get-tuple-element.20.refs_0_), channel_id=1, source_target_pairs={{0,6},{1,7},{2,4},{3,5},{4,2},{5,3},{6,0},{7,1},{8,14},{9,15},{10,... | collective-permute-start | bytes 73736 | tf_op jit(solution)/shard_map/ppermute | solution.py:350
  27.2 0.6 %collective-permute-start.6 = (f32[48,128]{1,0:T(8,128)S(1)}, f32[48,128]{1,0:T(8,128)S(1)}, u32[]{:S(2)}, u32[]{:S(2)}) collective-permute-start(f32[48,128]{1,0:T(8,128)S(1)} %get-tuple-element.20.refs_0_), channel_id=1, source_target_pairs={{0,2},{1,3},{2,0},{3,1},{4,6},{5,7},{6,4},{7,5},{8,10},{9,11},{10,... | collective-permute-start | bytes 73736 | tf_op jit(solution)/shard_map/ppermute | solution.py:350
  27.8 1.4 %collective-permute-start.11 = (f32[48,128]{1,0:T(8,128)S(1)}, f32[48,128]{1,0:T(8,128)S(1)}, u32[]{:S(2)}, u32[]{:S(2)}) collective-permute-start(f32[48,128]{1,0:T(8,128)S(1)} %get-tuple-element.25), channel_id=1, source_target_pairs={{0,8},{8,0},{16,24},{24,16},{1,9},{9,1},{17,25},{25,17},{2,10},{10... | collective-permute-start | bytes 73736 | tf_op jit(solution)/shard_map/ppermute | solution.py:350
  29.2 2.7 %collective-permute-done.7.refs_2_ = f32[48,128]{1,0:T(8,128)S(1)} collective-permute-done((f32[48,128]{1,0:T(8,128)S(1)}, f32[48,128]{1,0:T(8,128)S(1)}, u32[]{:S(2)}, u32[]{:S(2)}) %collective-permute-start.7) | collective-permute-done | bytes 24608 | tf_op jit(solution)/shard_map/ppermute | solution.py:350
  32.0 0.1 collective-permute-start.10
  32.1 0.9 %own_3.1.refs_3_ = f32[6,256]{1,0:T(8,128)S(1)} custom-call(f32[8,1024]{1,0:T(8,128)S(1)} %copy-done.1, bf16[1024,32]{1,0:T(8,128)(2,1)S(1)} %get-tuple-element.15.dist, f32[1024,8]{1,0:T(8,128)S(1)} %get-tuple-element.16.s_col, bf16[32,1024]{1,0:T(8,128)(2,1)S(1)} %get-tuple-element.17.right, bf16[32,1024]{1,0:T(8,128)(2,1)S(1)} %get-tuple-element.18.feat_g, ...), custom_call_target="tpu_custom_call" | custom-call | flops 7864320 | bytes 65536 | tf_op jit(solution)/shard_map/own_3/pallas_call | solution.py:372
  33.0 0.2 collective-permute-done.10.part_a
  33.3 0.6 %sum_parts.1 = (f32[3,1024]{1,0:T(4,128)}, f32[3,1024]{1,0:T(4,128)}) custom-call(f32[48,128]{1,0:T(8,128)S(1)} %get-tuple-element.21.after.keep_a, f32[48,128]{1,0:T(8,128)S(1)} %get-tuple-element.23.keep_b, f32[48,128]{1,0:T(8,128)S(1)} %collective-permute-done.10.part_a, f32[48,128]{1,0:T(8,128)S(1)} %collective-permute-done.11.part_b, ...), custom_call_target="tpu_custom_call" | custom-call | tf_op jit(solution)/shard_map/sum_parts/pallas_call | solution.py:474
  (15 shorter events, 0.1 us)
Async XLA Ops:
  2.7 9.2 %collective-permute-start.2 = (f32[1,8,1024]{2,1,0:T(8,128)}, f32[1,8,1024]{2,1,0:T(8,128)S(1)}, u32[]{:S(2)}, u32[]{:S(2)}) collective-permute-start(f32[1,8,1024]{2,1,0:T(8,128)} %bitcast.2), channel_id=1, source_target_pairs={{0,8},{8,0},{16,24},{24,16},{1,9},{9,1},{17,25},{25,17},{2,10},{10... | collective-permute-start | bytes 98312 | tf_op jit(solution)/shard_map/ppermute | solution.py:350
  5.7 6.2 %collective-permute-start.1 = (f32[1,8,1024]{2,1,0:T(8,128)}, f32[1,8,1024]{2,1,0:T(8,128)S(1)}, u32[]{:S(2)}, u32[]{:S(2)}) collective-permute-start(f32[1,8,1024]{2,1,0:T(8,128)} %bitcast.3), channel_id=1, source_target_pairs={{0,16},{8,24},{16,0},{24,8},{1,17},{9,25},{17,1},{25,9},{2,18},{10... | collective-permute-start | bytes 98312 | tf_op jit(solution)/shard_map/ppermute | solution.py:350
  7.2 5.0 %collective-permute-start = (f32[1,8,1024]{2,1,0:T(8,128)}, f32[1,8,1024]{2,1,0:T(8,128)S(1)}, u32[]{:S(2)}, u32[]{:S(2)}) collective-permute-start(f32[1,8,1024]{2,1,0:T(8,128)} %bitcast.4), channel_id=1, source_target_pairs={{0,4},{1,5},{2,6},{3,7},{4,0},{5,1},{6,2},{7,3},{8,12},{9,13},{10,... | collective-permute-start | bytes 98312 | tf_op jit(solution)/shard_map/ppermute | solution.py:350
  9.8 0.8 %copy-start = (f32[8,1024]{1,0:T(8,128)S(1)}, f32[8,1024]{1,0:T(8,128)}, u32[]{:S(2)}) copy-start(f32[8,1024]{1,0:T(8,128)} %pack_group.1.pack) | copy-start | bytes 98308
  12.2 5.5 %collective-permute-start.3 = (f32[2,8,1024]{2,1,0:T(8,128)S(1)}, f32[2,8,1024]{2,1,0:T(8,128)S(1)}, u32[]{:S(2)}, u32[]{:S(2)}) collective-permute-start(f32[2,8,1024]{2,1,0:T(8,128)S(1)} %stack_groups.2.after.refs_0_), channel_id=1, source_target_pairs={{0,2},{1,3},{2,0},{3,1},{4,6},{5,7},{6,4},{7,5},{8,10},{9,11},{10,... | collective-permute-start | bytes 196616 | tf_op jit(solution)/shard_map/ppermute | solution.py:350
  13.8 3.9 %collective-permute-start.4 = (f32[1,8,1024]{2,1,0:T(8,128)S(1)}, f32[1,8,1024]{2,1,0:T(8,128)S(1)}, u32[]{:S(2)}, u32[]{:S(2)}) collective-permute-start(f32[1,8,1024]{2,1,0:T(8,128)S(1)} %collective-permute-done.1.refs_3_.b_2), channel_id=1, source_target_pairs={{0,8},{8,0},{16,24},{24,16},{1,9},{9,1},{17,25},{25,17},{2,10},{10... | collective-permute-start | bytes 98312 | tf_op jit(solution)/shard_map/ppermute | solution.py:350
  15.3 2.5 %copy-start.1 = (f32[8,1024]{1,0:T(8,128)S(1)}, f32[8,1024]{1,0:T(8,128)}, u32[]{:S(2)}) copy-start(f32[8,1024]{1,0:T(8,128)} %pack_group.1.pack) | copy-start | bytes 98308
  17.7 1.4 %collective-permute-start.5 = (f32[4,8,1024]{2,1,0:T(8,128)S(1)}, f32[4,8,1024]{2,1,0:T(8,128)S(1)}, u32[]{:S(2)}, u32[]{:S(2)}) collective-permute-start(f32[4,8,1024]{2,1,0:T(8,128)S(1)} %stack_groups.3.after.near_a.refs_4_), channel_id=1, source_target_pairs={{0,1},{1,0},{2,3},{3,2},{4,5},{5,4},{6,7},{7,6},{8,9},{9,8},{10,11... | collective-permute-start | bytes 393224 | tf_op jit(solution)/shard_map/ppermute | solution.py:350
  19.3 8.5 %collective-permute-start.9 = (f32[48,128]{1,0:T(8,128)S(1)}, f32[48,128]{1,0:T(8,128)S(1)}, u32[]{:S(2)}, u32[]{:S(2)}) collective-permute-start(f32[48,128]{1,0:T(8,128)S(1)} %get-tuple-element.22.refs_0_), channel_id=1, source_target_pairs={{0,16},{8,24},{16,0},{24,8},{1,17},{9,25},{17,1},{25,9},{2,18},{10... | collective-permute-start | bytes 73736 | tf_op jit(solution)/shard_map/ppermute | solution.py:350
  19.8 9.4 %collective-permute-start.8 = (f32[48,128]{1,0:T(8,128)S(1)}, f32[48,128]{1,0:T(8,128)S(1)}, u32[]{:S(2)}, u32[]{:S(2)}) collective-permute-start(f32[48,128]{1,0:T(8,128)S(1)} %get-tuple-element.20.refs_0_), channel_id=1, source_target_pairs={{0,6},{1,7},{2,4},{3,5},{4,2},{5,3},{6,0},{7,1},{8,14},{9,15},{10,... | collective-permute-start | bytes 73736 | tf_op jit(solution)/shard_map/ppermute | solution.py:350
  27.2 4.7 %collective-permute-start.7 = (f32[48,128]{1,0:T(8,128)S(1)}, f32[48,128]{1,0:T(8,128)S(1)}, u32[]{:S(2)}, u32[]{:S(2)}) collective-permute-start(f32[48,128]{1,0:T(8,128)S(1)} %get-tuple-element.20.refs_0_), channel_id=1, source_target_pairs={{0,4},{1,5},{2,6},{3,7},{4,0},{5,1},{6,2},{7,3},{8,12},{9,13},{10,... | collective-permute-start | bytes 73736 | tf_op jit(solution)/shard_map/ppermute | solution.py:350
  27.2 4.7 %collective-permute-start.6 = (f32[48,128]{1,0:T(8,128)S(1)}, f32[48,128]{1,0:T(8,128)S(1)}, u32[]{:S(2)}, u32[]{:S(2)}) collective-permute-start(f32[48,128]{1,0:T(8,128)S(1)} %get-tuple-element.20.refs_0_), channel_id=1, source_target_pairs={{0,2},{1,3},{2,0},{3,1},{4,6},{5,7},{6,4},{7,5},{8,10},{9,11},{10,... | collective-permute-start | bytes 73736 | tf_op jit(solution)/shard_map/ppermute | solution.py:350
  27.8 5.2 %collective-permute-start.11 = (f32[48,128]{1,0:T(8,128)S(1)}, f32[48,128]{1,0:T(8,128)S(1)}, u32[]{:S(2)}, u32[]{:S(2)}) collective-permute-start(f32[48,128]{1,0:T(8,128)S(1)} %get-tuple-element.25), channel_id=1, source_target_pairs={{0,8},{8,0},{16,24},{24,16},{1,9},{9,1},{17,25},{25,17},{2,10},{10... | collective-permute-start | bytes 73736 | tf_op jit(solution)/shard_map/ppermute | solution.py:350
  32.0 1.3 %collective-permute-start.10 = (f32[48,128]{1,0:T(8,128)S(1)}, f32[48,128]{1,0:T(8,128)S(1)}, u32[]{:S(2)}, u32[]{:S(2)}) collective-permute-start(f32[48,128]{1,0:T(8,128)S(1)} %get-tuple-element.24), channel_id=1, source_target_pairs={{0,1},{1,0},{2,3},{3,2},{4,5},{5,4},{6,7},{7,6},{8,9},{9,8},{10,11... | collective-permute-start | bytes 73736 | tf_op jit(solution)/shard_map/ppermute | solution.py:350

commit v4 on v3

--- a/solution.py
+++ b/solution.py
@@ -107,10 +107,12 @@
     return jnp.concatenate(left), jnp.concatenate(right).astype(BF16)
 
 
-def columns(pack, dist, spread_s):
+def columns(pack, dist, s_col):
     left, right = distances(pack)
-    dist[...] = jnp.transpose(left).astype(BF16)
-    spread_s[...] = jnp.transpose(jnp.broadcast_to(halves(pack), (8, pack.shape[1])))
+    blank = jnp.zeros((7, pack.shape[1]), F32)
+    turned = jnp.transpose(jnp.concatenate([left[:24], halves(pack), blank]))
+    s_col[...] = turned
+    dist[...] = turned.astype(BF16)
     return right
 
 
@@ -147,7 +149,7 @@
         for n in range(n_strip):
             at = slice(i + n * STRIP, i + (n + 1) * STRIP)
             here = slice(n * STRIP, (n + 1) * STRIP)
-            strip(qq[count % 2][here, :], s_a[at, 0:1] + row, images, n * STRIP)
+            strip(qq[count % 2][here, :], s_a[at, 24:25] + row, images, n * STRIP)
             if waiting and (n + 1) % per == 0:
                 waiting.pop(0)()
         for step in waiting:
@@ -196,7 +198,7 @@
             per = max(1, n_strip // max(1, len(todo)))
             for m in range(n_strip):
                 here = slice(c * n + m * STRIP, c * n + (m + 1) * STRIP)
-                strip(qq[block % 2][here, :], s_a[here, 0:1] + row, slots, c * n + m * STRIP)
+                strip(qq[block % 2][here, :], s_a[here, 24:25] + row, slots, c * n + m * STRIP)
                 if todo and (m + 1) % per == 0:
                     todo.pop(0)()
             for step in todo:
@@ -252,7 +254,8 @@
     return lax.axis_index(axis).astype(jnp.int32)
 
 
-def stack_kernel(n_pairs, *refs):
+def stack_kernel(n_pairs, n_arrived, *refs):
+    del n_arrived
     for n in range(n_pairs):
         first, second, both = refs[2 * n], refs[2 * n + 1], refs[n - n_pairs]
         size = first.shape[0]
@@ -271,44 +274,46 @@
     return [pack[7:8, n * 128 : (n + 1) * 128] for n in range(3)]
 
 
-def pair_kernel(pack, near_a, far_a, b_0, b_1, b_2, b_3, after, out_a, out_b, apack, bpack, dist, s_col, *rest):
+def choose(relative, near, far):
+    at = place(relative >> 1, near.shape[0].bit_length() - 1)
+    return jnp.where(relative % 2 == 0, near[at], far[at])
+
+
+def prepare_kernel(pack, near, far, after, chosen, right, feat_g, feat_h):
+    del after
+    m = jnp.max(listed(pack)[1]).astype(jnp.int32)
+    chosen[...] = choose(m ^ here("row"), near, far)
+    right[...] = distances(chosen[...])[1]
+    feat_g[...], feat_h[...] = features(chosen[...])
+
+
+def pair_kernel(pack, near, far, bpack, right, feat_g, feat_h, after, out_a, out_b, apack, dist, s_col, *rest):
     del after
     sums_a, sums_b, qq, images = rest[0:2], rest[2:4], rest[4:6], rest[6:8]
-    k, m, count = [jnp.max(value).astype(jnp.int32) for value in listed(pack)]
+    k, _, count = [jnp.max(value).astype(jnp.int32) for value in listed(pack)]
 
     @pl.when(count > 1)
     def _():
-        from_a = k ^ here("col")
-        from_b = m ^ here("row")
-        at = place(from_a >> 1, near_a.shape[0].bit_length() - 1)
-        apack[...] = jnp.where(from_a % 2 == 0, near_a[at], far_a[at])
-        at = place(from_b >> 2, b_0.shape[0].bit_length() - 1)
-        for n, block in enumerate((b_0, b_1, b_2, b_3)):
-
-            @pl.when(from_b % 4 == n)
-            def _(block=block):
-                bpack[...] = block[at]
-
+        apack[...] = choose(k ^ here("col"), near, far)
         columns(apack[...], dist, s_col)
-        right = distances(bpack[...])[1]
-        feat_a, feat_b = features(apack[...]), features(bpack[...])
-        interact_both(dist, s_col, right, halves(bpack[...]), feat_a, feat_b, qq, images, sums_a, sums_b)
+        feat_a = features(apack[...])
+        interact_both(
+            dist, s_col, right, halves(bpack[...]), feat_a, (feat_g, feat_h), qq, images, sums_a, sums_b
+        )
         store_dense(out_a, finish(apack[...], sums_a[0][...], sums_a[1][...]))
         store_dense(out_b, finish(bpack[...], sums_b[0][...], sums_b[1][...]))
 
 
 def merge_kernel(axis, n_parts, *refs):
-    parts, packs, (keep, send) = refs[:n_parts], refs[n_parts:-2], refs[-2:]
+    parts, (near, keep, send) = refs[:n_parts], refs[n_parts:]
     at = here(axis)
     total = onward = jnp.zeros(keep.shape, F32)
     for n, part in enumerate(parts):
-        relative = 2 * n
+        relative = 2 * (n_parts - 1 - n)
+        k, m, count = listed(near[place(relative >> 1, near.shape[0].bit_length() - 1)])
         if axis == "col":
-            k, m, count = listed(packs[0][place(n, packs[0].shape[0].bit_length() - 1)])
             target = jnp.where(count > 1, k, -1.0)
         else:
-            run = packs[1] if relative & 2 else packs[0]
-            k, m, count = listed(run[place(relative >> 2, run.shape[0].bit_length() - 1)])
             itself = (k == here("col").astype(F32)) & (m == (at ^ relative).astype(F32))
             target = jnp.where((count > 1) & ~itself, m, -1.0)
         block = part[...]
@@ -337,9 +342,9 @@
 
 def pair_work(g):
     return [
-        *[pltpu.VMEM((8, g), F32)] * 2,
+        pltpu.VMEM((8, g), F32),
         pltpu.VMEM((g, Q_ROWS), BF16),
-        pltpu.VMEM((g, 8), F32),
+        pltpu.VMEM((g, Q_ROWS), F32),
         *[pltpu.VMEM((G_ROWS, g), F32), pltpu.VMEM((H_ROWS, g), F32)] * 2,
         *[pltpu.VMEM((g, UNIT), F32)] * 2,
         *[pltpu.VMEM((g, 4 * UNIT), BF16)] * 2,
@@ -351,7 +356,7 @@
 
 
 def spread(block, axis, size):
-    return [block] + [swap(block, axis, size, s) for s in range(2, size, 2)]
+    return [swap(block, axis, size, s) for s in range(size - 2, 0, -2)] + [block]
 
 
 def local(n_row, n_col, positions, strengths, radii, pair_list, pair_count):
@@ -391,25 +396,21 @@
     )(positions, strengths, radii[None], pair_list, pair_count)
 
     own = []
-    common = ()
-    near_a, have_b = pack[None], pack[None]
-    after = pack
+    near_a, near_b = pack[None], pack[None]
     for stage in range(n_col.bit_length() - 1):
         step_a, step_b = n_col >> (1 + stage), n_row >> (1 + stage)
         far_a = swap(near_a, "col", n_col, step_a)
-        if step_b >= 2:
-            far_b = swap(have_b, "row", n_row, step_b)
-            if step_b == 2:
-                next_b = swap(have_b, "row", n_row, 1)
-        elif step_b == 1:
-            last_b = swap(far_b, "row", n_row, 1)
+        if step_b:
+            far_b = swap(near_b, "row", n_row, step_b)
+        if step_a == 1:
+            break
         if stage == 0:
             chunk_0, *common = chunk_call(
                 first_kernel,
                 out_shape=(
                     chunk,
                     jax.ShapeDtypeStruct((g, Q_ROWS), BF16),
-                    jax.ShapeDtypeStruct((g, 8), F32),
+                    jax.ShapeDtypeStruct((g, Q_ROWS), F32),
                     jax.ShapeDtypeStruct((Q_ROWS, g), BF16),
                     jax.ShapeDtypeStruct((G_ROWS, g), BF16),
                     jax.ShapeDtypeStruct((H_ROWS, g), BF16),
@@ -419,27 +420,39 @@
                 name="own_first",
             )(pack)
             own.append(chunk_0)
-        elif stage < 3:
-            own.append(later(stage, after))
-        if step_a == 1:
-            break
+        elif stage == 1:
+            own.append(later(1, near_a))
+            own.append(later(2, near_a))
+        arrived = own[-2:] + [far_b]
         runs = [(near_a, far_a)]
-        if step_b > 2:
-            runs.append((have_b, far_b))
-        arrived = [own[-1], last_b if step_b == 1 else far_b]
-        if step_b == 2:
-            arrived.append(next_b)
+        if step_b > 1:
+            runs.append((near_b, far_b))
         stacked = pl.pallas_call(
-            functools.partial(stack_kernel, len(runs)),
+            functools.partial(stack_kernel, len(runs), len(arrived)),
             out_shape=tuple(jax.ShapeDtypeStruct((2 * n.shape[0], 8, g), F32) for n, _ in runs),
             in_specs=[vmem_spec] * (2 * len(runs) + len(arrived)),
             out_specs=(vmem_spec,) * len(runs),
             compiler_params=params,
             name="stack_groups",
         )(*[block for run in runs for block in run], *arrived)
-        near_a = after = stacked[0]
+        near_a = stacked[0]
         if len(runs) > 1:
-            have_b = stacked[1]
+            near_b = stacked[1]
+
+    prepared = pl.pallas_call(
+        prepare_kernel,
+        out_shape=(
+            block,
+            jax.ShapeDtypeStruct((Q_ROWS, g), BF16),
+            jax.ShapeDtypeStruct((G_ROWS, g), BF16),
+            jax.ShapeDtypeStruct((H_ROWS, g), BF16),
+        ),
+        in_specs=[vmem_spec] * 4,
+        out_specs=(vmem_spec,) * 4,
+        compiler_params=params,
+        cost_estimate=pl.CostEstimate(flops=g * g, bytes_accessed=64 * g, transcendentals=0),
+        name="prepare_group",
+    )(pack, near_b, far_b, near_a)
 
     side_a, side_b = pl.pallas_call(
         pair_kernel,
@@ -450,23 +463,23 @@
         compiler_params=params,
         cost_estimate=pl.CostEstimate(flops=60 * g * g, bytes_accessed=128 * g, transcendentals=g * g),
         name="listed_pair",
-    )(pack, near_a, far_a, have_b, next_b, far_b, last_b, own[-1])
-
-    def merge(parts, packs, axis):
+    )(pack, near_a, far_a, *prepared, own[-1])
+
+    def merge(parts, near, axis):
         return pl.pallas_call(
             functools.partial(merge_kernel, axis, len(parts)),
             out_shape=(dense,) * 2,
-            in_specs=[vmem_spec] * (len(parts) + len(packs)),
+            in_specs=[vmem_spec] * (len(parts) + 1),
             out_specs=(vmem_spec,) * 2,
             compiler_params=params,
             name="merge_" + axis,
-        )(*parts, *packs)
+        )(*parts, near)
 
     parts_a = spread(side_a, "col", n_col)
     parts_b = spread(side_b, "row", n_row)
-    keep_b, send_b = merge(parts_b, [have_b, far_b], "row")
+    keep_b, send_b = merge(parts_b, near_b, "row")
     far_b = swap(send_b, "row", n_row, 1)
-    keep_a, send_a = merge(parts_a, [near_a], "col")
+    keep_a, send_a = merge(parts_a, near_a, "col")
     far_a = swap(send_a, "col", n_col, 1)
     own.append(later(3, keep_a))
 

time: 34 us -> 32.4 us (0.953)
  starting transfers between devices: 19.3 us -> 13.9 us
  Pallas kernels: 6.25 us -> 11.1 us
  waiting for transfers between devices: 6.16 us -> 4.91 us
    ppermute x12 -> x11, starting transfers between devices: 19.3 us -> 13.9 us  [swap(): return lax.ppermute(block, axis, [(i, i ^ step) for i in range(size)])]
    pallas_call x1, Pallas kernels: 0.12 us -> 4.79 us  [local(): pl.pallas_call(pair_kernel, out_shape=(dense, dense), in_specs=[vmem_spec...]
    ppermute x12 -> x11, waiting for transfers between devices: 6.16 us -> 4.91 us  [swap(): return lax.ppermute(block, axis, [(i, i ^ step) for i in range(size)])]
  transfers between devices with their start and end apart: 12 -> 11, of which waited for: 5 -> 6; matrix products, arithmetic and copies ran while one was open for 0% -> 0% of each run, Pallas kernels for 12% -> 13%
where the time goes in v4:
time: 32.4 us; the launch traced here: 32.1 us
  starting transfers between devices  13.9 us (43%)
  Pallas kernels  11.1 us (34%)
  waiting for transfers between devices  4.91 us (15%)
  between operations  1.41 us (4%)
  local copies, waits for them, and re-layouts  0.8 us (2%)
    ppermute x11, starting transfers between devices, swap(): return lax.ppermute(block, axis, [(i, i ^ step) for i in range(size)])  13.9 us
    ppermute x11, waiting for transfers between devices, swap(): return lax.ppermute(block, axis, [(i, i ^ step) for i in range(size)])  4.91 us
    pallas_call x1, Pallas kernels, local(): pl.pallas_call(pair_kernel, out_shape=(dense, dense), in_specs=[vmem_spec...  4.79 us
    pallas_call x3, Pallas kernels, later(): chunk_call(functools.partial(later_kernel, n), out_shape=chunk, in_specs=...  2.77 us
    pallas_call x1, Pallas kernels, local(): pl.pallas_call(pack_kernel, out_shape=block, in_specs=[hbm_spec] * 5, out...  1.39 us
    pallas_call x1, Pallas kernels, local(): chunk_call(first_kernel, out_shape=(chunk, jax.ShapeDtypeStruct((g, Q_ROW...  1.19 us
    unnamed x4, local copies, waits for them, and re-layouts  0.8 us
  transfers between devices with their start and end apart: 11, of which 6 were waited for; matrix products, arithmetic and copies ran while one was open for 0% of the time, Pallas kernels for 13%

profile of v4, /device:TPU:0, one launch (start us, length us, event | category | flops | bytes accessed | tf_op | source)
XLA Modules:
  0.0 32.1 jit_solution(12200410346757172749)
XLA Ops:
  1.3 1.4 %pack_group.1.pack = f32[8,1024]{1,0:T(8,128)} custom-call(f32[3,1024]{1,0:T(4,128)} %positions.1, f32[3,1024]{1,0:T(4,128)} %strengths.1, f32[1,1024]{1,0:T(1,128)} %bitcast.6, s32[2,1,1,2]{3,2,1,0:T(1,128)} %pair_list.1, s32[1,1]{1,0:T(1,128)S(6)} %copy.7.pair_count), custom_call_target="tpu_custom_call" | custom-call | tf_op jit(solution)/shard_map/pack_group/pallas_call | solution.py:385
  2.7 4.1 %collective-permute-start = (f32[1,8,1024]{2,1,0:T(8,128)}, f32[1,8,1024]{2,1,0:T(8,128)S(1)}, u32[]{:S(2)}, u32[]{:S(2)}) collective-permute-start(f32[1,8,1024]{2,1,0:T(8,128)} %bitcast.2), channel_id=1, source_target_pairs={{0,4},{1,5},{2,6},{3,7},{4,0},{5,1},{6,2},{7,3},{8,12},{9,13},{10,... | collective-permute-start | bytes 98312 | tf_op jit(solution)/shard_map/ppermute | solution.py:355
  6.8 1.5 %collective-permute-start.1 = (f32[1,8,1024]{2,1,0:T(8,128)}, f32[1,8,1024]{2,1,0:T(8,128)S(1)}, u32[]{:S(2)}, u32[]{:S(2)}) collective-permute-start(f32[1,8,1024]{2,1,0:T(8,128)} %bitcast.3), channel_id=1, source_target_pairs={{0,16},{8,24},{16,0},{24,8},{1,17},{9,25},{17,1},{25,9},{2,18},{10... | collective-permute-start | bytes 98312 | tf_op jit(solution)/shard_map/ppermute | solution.py:355
  8.3 0.8 %copy-done = f32[8,1024]{1,0:T(8,128)S(1)} copy-done((f32[8,1024]{1,0:T(8,128)S(1)}, f32[8,1024]{1,0:T(8,128)}, u32[]{:S(2)}) %copy-start) | copy-done | bytes 32792
  9.1 1.2 %own_first.1 = (f32[6,256]{1,0:T(8,128)S(1)}, bf16[1024,32]{1,0:T(8,128)(2,1)S(1)}, f32[1024,32]{1,0:T(8,128)S(1)}, bf16[32,1024]{1,0:T(8,128)(2,1)S(1)}, bf16[3...) custom-call(f32[8,1024]{1,0:T(8,128)S(1)} %copy-done), custom_call_target="tpu_custom_call" | custom-call | flops 7864320 | bytes 65536 | tf_op jit(solution)/shard_map/own_first/pallas_call | solution.py:408
  10.3 0.6 %collective-permute-done.1.refs_3_.refs_5_ = f32[1,8,1024]{2,1,0:T(8,128)S(1)} collective-permute-done((f32[1,8,1024]{2,1,0:T(8,128)}, f32[1,8,1024]{2,1,0:T(8,128)S(1)}, u32[]{:S(2)}, u32[]{:S(2)}) %collective-permute-start.1) | collective-permute-done | bytes 32800 | tf_op jit(solution)/shard_map/ppermute | solution.py:355
  10.9 1.6 %collective-permute-start.2 = (f32[2,8,1024]{2,1,0:T(8,128)S(1)}, f32[2,8,1024]{2,1,0:T(8,128)S(1)}, u32[]{:S(2)}, u32[]{:S(2)}) collective-permute-start(f32[2,8,1024]{2,1,0:T(8,128)S(1)} %get-tuple-element.21.after.refs_0_), channel_id=1, source_target_pairs={{0,2},{1,3},{2,0},{3,1},{4,6},{5,7},{6,4},{7,5},{8,10},{9,11},{10,... | collective-permute-start | bytes 196616 | tf_op jit(solution)/shard_map/ppermute | solution.py:355
  12.6 1.5 %collective-permute-start.3 = (f32[2,8,1024]{2,1,0:T(8,128)S(1)}, f32[2,8,1024]{2,1,0:T(8,128)S(1)}, u32[]{:S(2)}, u32[]{:S(2)}) collective-permute-start(f32[2,8,1024]{2,1,0:T(8,128)S(1)} %get-tuple-element.27.near.refs_2_), channel_id=1, source_target_pairs={{0,8},{8,0},{16,24},{24,16},{1,9},{9,1},{17,25},{25,17},{2,10},{10... | collective-permute-start | bytes 196616 | tf_op jit(solution)/shard_map/ppermute | solution.py:355
  14.1 0.9 %own_2.1.refs_3_.after.refs_2_ = f32[6,256]{1,0:T(8,128)S(1)} custom-call(f32[8,1024]{1,0:T(8,128)S(1)} %copy-done, bf16[1024,32]{1,0:T(8,128)(2,1)S(1)} %get-tuple-element.22.dist, f32[1024,32]{1,0:T(8,128)S(1)} %get-tuple-element.23.s_col, bf16[32,1024]{1,0:T(8,128)(2,1)S(1)} %get-tuple-element.24.right, bf16[32,1024]{1,0:T(8,128)(2,1)S(1)} %get-tuple-element.25.feat_g, ...), custom_call_target="tpu_custom_call" | custom-call | flops 7864320 | bytes 65536 | tf_op jit(solution)/shard_map/own_2/pallas_call | solution.py:377
  15.0 0.9 %own_1.1.refs_2_.refs_1_ = f32[6,256]{1,0:T(8,128)S(1)} custom-call(f32[8,1024]{1,0:T(8,128)S(1)} %copy-done, bf16[1024,32]{1,0:T(8,128)(2,1)S(1)} %get-tuple-element.22.dist, f32[1024,32]{1,0:T(8,128)S(1)} %get-tuple-element.23.s_col, bf16[32,1024]{1,0:T(8,128)(2,1)S(1)} %get-tuple-element.24.right, bf16[32,1024]{1,0:T(8,128)(2,1)S(1)} %get-tuple-element.25.feat_g, ...), custom_call_target="tpu_custom_call" | custom-call | flops 7864320 | bytes 65536 | tf_op jit(solution)/shard_map/own_1/pallas_call | solution.py:377
  15.9 0.9 %collective-permute-done.3.refs_4_.far = f32[2,8,1024]{2,1,0:T(8,128)S(1)} collective-permute-done((f32[2,8,1024]{2,1,0:T(8,128)S(1)}, f32[2,8,1024]{2,1,0:T(8,128)S(1)}, u32[]{:S(2)}, u32[]{:S(2)}) %collective-permute-start.3) | collective-permute-done | bytes 65568 | tf_op jit(solution)/shard_map/ppermute | solution.py:355
  16.8 0.1 collective-permute-start.4
  16.9 0.3 prepare_group.1
  17.2 1.1 %collective-permute-done.4.far = f32[4,8,1024]{2,1,0:T(8,128)S(1)} collective-permute-done((f32[4,8,1024]{2,1,0:T(8,128)S(1)}, f32[4,8,1024]{2,1,0:T(8,128)S(1)}, u32[]{:S(2)}, u32[]{:S(2)}) %collective-permute-start.4) | collective-permute-done | bytes 131104 | tf_op jit(solution)/shard_map/ppermute | solution.py:355
  18.3 4.8 %listed_pair.1 = (f32[48,128]{1,0:T(8,128)S(1)}, f32[48,128]{1,0:T(8,128)S(1)}) custom-call(f32[8,1024]{1,0:T(8,128)S(1)} %copy-done.1, f32[4,8,1024]{2,1,0:T(8,128)S(1)} %stack_groups.3.after.near.refs_4_, f32[4,8,1024]{2,1,0:T(8,128)S(1)} %collective-permute-done.4.far, f32[8,1024]{1,0:T(8,128)S(1)} %get-tuple-element.28.bpack, ...), custom_call_target="tpu_custom_call" | custom-call | flops 62914560 | bytes 131072 | tf_op jit(solution)/shard_map/listed_pair/pallas_call | solution.py:457
  23.1 0.1 collective-permute-start.5
  23.2 2.6 %collective-permute-start.6 = (f32[48,128]{1,0:T(8,128)S(1)}, f32[48,128]{1,0:T(8,128)S(1)}, u32[]{:S(2)}, u32[]{:S(2)}) collective-permute-start(f32[48,128]{1,0:T(8,128)S(1)} %get-tuple-element.32.refs_3_), channel_id=1, source_target_pairs={{0,4},{1,5},{2,6},{3,7},{4,0},{5,1},{6,2},{7,3},{8,12},{9,13},{10,... | collective-permute-start | bytes 73736 | tf_op jit(solution)/shard_map/ppermute | solution.py:355
  25.8 1.8 %collective-permute-start.7 = (f32[48,128]{1,0:T(8,128)S(1)}, f32[48,128]{1,0:T(8,128)S(1)}, u32[]{:S(2)}, u32[]{:S(2)}) collective-permute-start(f32[48,128]{1,0:T(8,128)S(1)} %get-tuple-element.32.refs_3_), channel_id=1, source_target_pairs={{0,2},{1,3},{2,0},{3,1},{4,6},{5,7},{6,4},{7,5},{8,10},{9,11},{10,... | collective-permute-start | bytes 73736 | tf_op jit(solution)/shard_map/ppermute | solution.py:355
  27.6 0.5 %collective-permute-start.10 = (f32[48,128]{1,0:T(8,128)S(1)}, f32[48,128]{1,0:T(8,128)S(1)}, u32[]{:S(2)}, u32[]{:S(2)}) collective-permute-start(f32[48,128]{1,0:T(8,128)S(1)} %get-tuple-element.37), channel_id=1, source_target_pairs={{0,8},{8,0},{16,24},{24,16},{1,9},{9,1},{17,25},{25,17},{2,10},{10... | collective-permute-start | bytes 73736 | tf_op jit(solution)/shard_map/ppermute | solution.py:355
  28.1 0.7 %collective-permute-done.5.refs_0_ = f32[48,128]{1,0:T(8,128)S(1)} collective-permute-done((f32[48,128]{1,0:T(8,128)S(1)}, f32[48,128]{1,0:T(8,128)S(1)}, u32[]{:S(2)}, u32[]{:S(2)}) %collective-permute-start.5) | collective-permute-done | bytes 24608 | tf_op jit(solution)/shard_map/ppermute | solution.py:355
  28.8 0.8 %collective-permute-done.7.refs_2_ = f32[48,128]{1,0:T(8,128)S(1)} collective-permute-done((f32[48,128]{1,0:T(8,128)S(1)}, f32[48,128]{1,0:T(8,128)S(1)}, u32[]{:S(2)}, u32[]{:S(2)}) %collective-permute-start.7) | collective-permute-done | bytes 24608 | tf_op jit(solution)/shard_map/ppermute | solution.py:355
  29.7 0.9 %own_3.1.refs_3_ = f32[6,256]{1,0:T(8,128)S(1)} custom-call(f32[8,1024]{1,0:T(8,128)S(1)} %copy-done.1, bf16[1024,32]{1,0:T(8,128)(2,1)S(1)} %get-tuple-element.22.dist, f32[1024,32]{1,0:T(8,128)S(1)} %get-tuple-element.23.s_col, bf16[32,1024]{1,0:T(8,128)(2,1)S(1)} %get-tuple-element.24.right, bf16[32,1024]{1,0:T(8,128)(2,1)S(1)} %get-tuple-element.25.feat_g, ...), custom_call_target="tpu_custom_call" | custom-call | flops 7864320 | bytes 65536 | tf_op jit(solution)/shard_map/own_3/pallas_call | solution.py:377
  30.6 0.9 %collective-permute-done.10.part_b = f32[48,128]{1,0:T(8,128)S(1)} collective-permute-done((f32[48,128]{1,0:T(8,128)S(1)}, f32[48,128]{1,0:T(8,128)S(1)}, u32[]{:S(2)}, u32[]{:S(2)}) %collective-permute-start.10) | collective-permute-done | bytes 24608 | tf_op jit(solution)/shard_map/ppermute | solution.py:355
  31.5 0.6 %sum_parts.1 = (f32[3,1024]{1,0:T(4,128)}, f32[3,1024]{1,0:T(4,128)}) custom-call(f32[48,128]{1,0:T(8,128)S(1)} %get-tuple-element.33.after.keep_a, f32[48,128]{1,0:T(8,128)S(1)} %get-tuple-element.35.keep_b, f32[48,128]{1,0:T(8,128)S(1)} %collective-permute-done.9.part_a, f32[48,128]{1,0:T(8,128)S(1)} %collective-permute-done.10.part_b, ...), custom_call_target="tpu_custom_call" | custom-call | tf_op jit(solution)/shard_map/sum_parts/pallas_call | solution.py:487
  (14 shorter events, 0.2 us)
Async XLA Ops:
  2.7 7.6 %collective-permute-start = (f32[1,8,1024]{2,1,0:T(8,128)}, f32[1,8,1024]{2,1,0:T(8,128)S(1)}, u32[]{:S(2)}, u32[]{:S(2)}) collective-permute-start(f32[1,8,1024]{2,1,0:T(8,128)} %bitcast.2), channel_id=1, source_target_pairs={{0,4},{1,5},{2,6},{3,7},{4,0},{5,1},{6,2},{7,3},{8,12},{9,13},{10,... | collective-permute-start | bytes 98312 | tf_op jit(solution)/shard_map/ppermute | solution.py:355
  6.8 4.1 %collective-permute-start.1 = (f32[1,8,1024]{2,1,0:T(8,128)}, f32[1,8,1024]{2,1,0:T(8,128)S(1)}, u32[]{:S(2)}, u32[]{:S(2)}) collective-permute-start(f32[1,8,1024]{2,1,0:T(8,128)} %bitcast.3), channel_id=1, source_target_pairs={{0,16},{8,24},{16,0},{24,8},{1,17},{9,25},{17,1},{25,9},{2,18},{10... | collective-permute-start | bytes 98312 | tf_op jit(solution)/shard_map/ppermute | solution.py:355
  8.3 0.8 %copy-start = (f32[8,1024]{1,0:T(8,128)S(1)}, f32[8,1024]{1,0:T(8,128)}, u32[]{:S(2)}) copy-start(f32[8,1024]{1,0:T(8,128)} %pack_group.1.pack) | copy-start | bytes 98308
  10.9 5.0 %collective-permute-start.2 = (f32[2,8,1024]{2,1,0:T(8,128)S(1)}, f32[2,8,1024]{2,1,0:T(8,128)S(1)}, u32[]{:S(2)}, u32[]{:S(2)}) collective-permute-start(f32[2,8,1024]{2,1,0:T(8,128)S(1)} %get-tuple-element.21.after.refs_0_), channel_id=1, source_target_pairs={{0,2},{1,3},{2,0},{3,1},{4,6},{5,7},{6,4},{7,5},{8,10},{9,11},{10,... | collective-permute-start | bytes 196616 | tf_op jit(solution)/shard_map/ppermute | solution.py:355
  12.6 4.3 %collective-permute-start.3 = (f32[2,8,1024]{2,1,0:T(8,128)S(1)}, f32[2,8,1024]{2,1,0:T(8,128)S(1)}, u32[]{:S(2)}, u32[]{:S(2)}) collective-permute-start(f32[2,8,1024]{2,1,0:T(8,128)S(1)} %get-tuple-element.27.near.refs_2_), channel_id=1, source_target_pairs={{0,8},{8,0},{16,24},{24,16},{1,9},{9,1},{17,25},{25,17},{2,10},{10... | collective-permute-start | bytes 196616 | tf_op jit(solution)/shard_map/ppermute | solution.py:355
  15.9 1.0 %copy-start.1 = (f32[8,1024]{1,0:T(8,128)S(1)}, f32[8,1024]{1,0:T(8,128)}, u32[]{:S(2)}) copy-start(f32[8,1024]{1,0:T(8,128)} %pack_group.1.pack) | copy-start | bytes 98308
  16.8 1.4 %collective-permute-start.4 = (f32[4,8,1024]{2,1,0:T(8,128)S(1)}, f32[4,8,1024]{2,1,0:T(8,128)S(1)}, u32[]{:S(2)}, u32[]{:S(2)}) collective-permute-start(f32[4,8,1024]{2,1,0:T(8,128)S(1)} %stack_groups.3.after.near.refs_4_), channel_id=1, source_target_pairs={{0,1},{1,0},{2,3},{3,2},{4,5},{5,4},{6,7},{7,6},{8,9},{9,8},{10,11... | collective-permute-start | bytes 393224 | tf_op jit(solution)/shard_map/ppermute | solution.py:355
  23.1 4.5 %collective-permute-start.8 = (f32[48,128]{1,0:T(8,128)S(1)}, f32[48,128]{1,0:T(8,128)S(1)}, u32[]{:S(2)}, u32[]{:S(2)}) collective-permute-start(f32[48,128]{1,0:T(8,128)S(1)} %get-tuple-element.34.refs_1_), channel_id=1, source_target_pairs={{0,16},{8,24},{16,0},{24,8},{1,17},{9,25},{17,1},{25,9},{2,18},{10... | collective-permute-start | bytes 73736 | tf_op jit(solution)/shard_map/ppermute | solution.py:355
  23.1 5.7 %collective-permute-start.5 = (f32[48,128]{1,0:T(8,128)S(1)}, f32[48,128]{1,0:T(8,128)S(1)}, u32[]{:S(2)}, u32[]{:S(2)}) collective-permute-start(f32[48,128]{1,0:T(8,128)S(1)} %get-tuple-element.32.refs_3_), channel_id=1, source_target_pairs={{0,6},{1,7},{2,4},{3,5},{4,2},{5,3},{6,0},{7,1},{8,14},{9,15},{10,... | collective-permute-start | bytes 73736 | tf_op jit(solution)/shard_map/ppermute | solution.py:355
  23.2 5.6 %collective-permute-start.6 = (f32[48,128]{1,0:T(8,128)S(1)}, f32[48,128]{1,0:T(8,128)S(1)}, u32[]{:S(2)}, u32[]{:S(2)}) collective-permute-start(f32[48,128]{1,0:T(8,128)S(1)} %get-tuple-element.32.refs_3_), channel_id=1, source_target_pairs={{0,4},{1,5},{2,6},{3,7},{4,0},{5,1},{6,2},{7,3},{8,12},{9,13},{10,... | collective-permute-start | bytes 73736 | tf_op jit(solution)/shard_map/ppermute | solution.py:355
  25.8 3.8 %collective-permute-start.7 = (f32[48,128]{1,0:T(8,128)S(1)}, f32[48,128]{1,0:T(8,128)S(1)}, u32[]{:S(2)}, u32[]{:S(2)}) collective-permute-start(f32[48,128]{1,0:T(8,128)S(1)} %get-tuple-element.32.refs_3_), channel_id=1, source_target_pairs={{0,2},{1,3},{2,0},{3,1},{4,6},{5,7},{6,4},{7,5},{8,10},{9,11},{10,... | collective-permute-start | bytes 73736 | tf_op jit(solution)/shard_map/ppermute | solution.py:355
  27.6 3.9 %collective-permute-start.10 = (f32[48,128]{1,0:T(8,128)S(1)}, f32[48,128]{1,0:T(8,128)S(1)}, u32[]{:S(2)}, u32[]{:S(2)}) collective-permute-start(f32[48,128]{1,0:T(8,128)S(1)} %get-tuple-element.37), channel_id=1, source_target_pairs={{0,8},{8,0},{16,24},{24,16},{1,9},{9,1},{17,25},{25,17},{2,10},{10... | collective-permute-start | bytes 73736 | tf_op jit(solution)/shard_map/ppermute | solution.py:355
  29.6 1.9 %collective-permute-start.9 = (f32[48,128]{1,0:T(8,128)S(1)}, f32[48,128]{1,0:T(8,128)S(1)}, u32[]{:S(2)}, u32[]{:S(2)}) collective-permute-start(f32[48,128]{1,0:T(8,128)S(1)} %get-tuple-element.36), channel_id=1, source_target_pairs={{0,1},{1,0},{2,3},{3,2},{4,5},{5,4},{6,7},{7,6},{8,9},{9,8},{10,11... | collective-permute-start | bytes 73736 | tf_op jit(solution)/shard_map/ppermute | solution.py:355

commit v5 on v4

--- a/solution.py
+++ b/solution.py
@@ -114,6 +114,13 @@
     s_col[...] = turned
     dist[...] = turned.astype(BF16)
     return right
+
+
+def outline(pack, factor):
+    pos = pack[0:3] - 0.5
+    half = halves(pack)
+    norm = jnp.sum(pos * pos, axis=0, keepdims=True) + half
+    return jnp.concatenate([factor * pos, norm, half, jnp.zeros((3, pack.shape[1]), F32)])
 
 
 def interact(dist_a, s_a, dist_b, s_b, feat_a, qq, slots, sums_b):
@@ -159,14 +166,10 @@
         step()
 
 
-def interact_both(dist_a, s_a, dist_b, s_b, feat_a, feat_b, qq, images, sums_a, sums_b):
-    rows, n = s_a.shape[0], UNIT
-    blocks, chunks = s_b.shape[1] // n, rows // n
+def interact_both(col, rows_b, feat_a, feat_b, images, sums_a, sums_b):
+    rows, n = col.shape[0], UNIT
+    blocks, chunks = rows_b.shape[1] // n, rows // n
     half = rows // 2
-
-    def measure(block, c):
-        here, part = slice(c * n, (c + 1) * n), slice(block * n, (block + 1) * n)
-        qq[block % 2][here, :] = down(dist_a[here, :], dist_b[:, part])
 
     def onto_a(block, c, kind):
         here, part = slice(c * n, (c + 1) * n), slice(block * n, (block + 1) * n)
@@ -182,23 +185,21 @@
         share = down(f, image[here, at : at + n]) + down(f, image[here, at + n : at + 2 * n])
         sums_b[kind][:, part] = sums_b[kind][:, part] + share if later else share
 
-    for c in range(chunks):
-        measure(0, c)
     ready, delayed = [], []
     for block in range(blocks):
         image = images[block % 2]
         part = slice(block * n, (block + 1) * n)
         slots = [image.at[:, m * n : (m + 1) * n] for m in range(4)]
-        row = jnp.broadcast_to(s_b[0:1, part], (STRIP, n))
+        row = [jnp.broadcast_to(rows_b[m : m + 1, part], (STRIP, n)) for m in range(5)]
         for c in range(chunks):
             todo, ready, delayed = ready, delayed, []
-            if block + 1 < blocks:
-                todo.append(functools.partial(measure, block + 1, c))
             n_strip = n // STRIP
             per = max(1, n_strip // max(1, len(todo)))
             for m in range(n_strip):
                 here = slice(c * n + m * STRIP, c * n + (m + 1) * STRIP)
-                strip(qq[block % 2][here, :], s_a[here, 24:25] + row, slots, c * n + m * STRIP)
+                own = [col[here, q : q + 1] for q in range(5)]
+                qq = own[0] * row[0] + own[1] * row[1] + own[2] * row[2] + (own[3] + row[3])
+                strip(qq, own[4] + row[4], slots, c * n + m * STRIP)
                 if todo and (m + 1) % per == 0:
                     todo.pop(0)()
             for step in todo:
@@ -279,27 +280,24 @@
     return jnp.where(relative % 2 == 0, near[at], far[at])
 
 
-def prepare_kernel(pack, near, far, after, chosen, right, feat_g, feat_h):
+def prepare_kernel(pack, near, far, after, chosen, rows, feat_g, feat_h):
     del after
     m = jnp.max(listed(pack)[1]).astype(jnp.int32)
     chosen[...] = choose(m ^ here("row"), near, far)
-    right[...] = distances(chosen[...])[1]
+    rows[...] = outline(chosen[...], 1.0)
     feat_g[...], feat_h[...] = features(chosen[...])
 
 
-def pair_kernel(pack, near, far, bpack, right, feat_g, feat_h, after, out_a, out_b, apack, dist, s_col, *rest):
+def pair_kernel(pack, near, far, bpack, rows_b, feat_g, feat_h, after, out_a, out_b, apack, col, *rest):
     del after
-    sums_a, sums_b, qq, images = rest[0:2], rest[2:4], rest[4:6], rest[6:8]
+    sums_a, sums_b, images = rest[0:2], rest[2:4], rest[4:6]
     k, _, count = [jnp.max(value).astype(jnp.int32) for value in listed(pack)]
 
     @pl.when(count > 1)
     def _():
         apack[...] = choose(k ^ here("col"), near, far)
-        columns(apack[...], dist, s_col)
-        feat_a = features(apack[...])
-        interact_both(
-            dist, s_col, right, halves(bpack[...]), feat_a, (feat_g, feat_h), qq, images, sums_a, sums_b
-        )
+        col[...] = jnp.transpose(outline(apack[...], -2.0))
+        interact_both(col, rows_b, features(apack[...]), (feat_g, feat_h), images, sums_a, sums_b)
         store_dense(out_a, finish(apack[...], sums_a[0][...], sums_a[1][...]))
         store_dense(out_b, finish(bpack[...], sums_b[0][...], sums_b[1][...]))
 
@@ -343,10 +341,8 @@
 def pair_work(g):
     return [
         pltpu.VMEM((8, g), F32),
-        pltpu.VMEM((g, Q_ROWS), BF16),
-        pltpu.VMEM((g, Q_ROWS), F32),
+        pltpu.VMEM((g, 8), F32),
         *[pltpu.VMEM((G_ROWS, g), F32), pltpu.VMEM((H_ROWS, g), F32)] * 2,
-        *[pltpu.VMEM((g, UNIT), F32)] * 2,
         *[pltpu.VMEM((g, 4 * UNIT), BF16)] * 2,
     ]
 
@@ -443,7 +439,7 @@
         prepare_kernel,
         out_shape=(
             block,
-            jax.ShapeDtypeStruct((Q_ROWS, g), BF16),
+            block,
             jax.ShapeDtypeStruct((G_ROWS, g), BF16),
             jax.ShapeDtypeStruct((H_ROWS, g), BF16),
         ),

time: 32.4 us -> 34.6 us (1.068)
  starting transfers between devices: 13.9 us -> 21.9 us
  Pallas kernels: 11.1 us -> 6.38 us
  waiting for transfers between devices: 4.91 us -> 3.91 us
    ppermute x11, starting transfers between devices: 13.9 us -> 21.9 us  [swap(): return lax.ppermute(block, axis, [(i, i ^ step) for i in range(size)])]
    pallas_call x1, Pallas kernels: 4.79 us -> 0.12 us  [local(): pl.pallas_call(pair_kernel, out_shape=(dense, dense), in_specs=[vmem_spec...]
    ppermute x11, waiting for transfers between devices: 4.91 us -> 3.91 us  [swap(): return lax.ppermute(block, axis, [(i, i ^ step) for i in range(size)])]
  transfers between devices with their start and end apart: 11 -> 11, of which waited for: 6 -> 5; matrix products, arithmetic and copies ran while one was open for 0% -> 0% of each run, Pallas kernels for 13% -> 12%
where the time goes in v5:
time: 34.6 us; the launch traced here: 34.3 us
  starting transfers between devices  21.9 us (63%)
  Pallas kernels  6.38 us (18%)
  waiting for transfers between devices  3.91 us (11%)
  between operations  1.4 us (4%)
  local copies, waits for them, and re-layouts  0.8 us (2%)
    ppermute x11, starting transfers between devices, swap(): return lax.ppermute(block, axis, [(i, i ^ step) for i in range(size)])  21.9 us
    ppermute x11, waiting for transfers between devices, swap(): return lax.ppermute(block, axis, [(i, i ^ step) for i in range(size)])  3.91 us
    pallas_call x3, Pallas kernels, later(): chunk_call(functools.partial(later_kernel, n), out_shape=chunk, in_specs=...  2.77 us
    pallas_call x1, Pallas kernels, local(): pl.pallas_call(pack_kernel, out_shape=block, in_specs=[hbm_spec] * 5, out...  1.39 us
    pallas_call x1, Pallas kernels, local(): chunk_call(first_kernel, out_shape=(chunk, jax.ShapeDtypeStruct((g, Q_ROW...  1.19 us
    unnamed x4, local copies, waits for them, and re-layouts  0.8 us
  transfers between devices with their start and end apart: 11, of which 5 were waited for; matrix products, arithmetic and copies ran while one was open for 0% of the time, Pallas kernels for 12%

profile of v5, /device:TPU:0, one launch (start us, length us, event | category | flops | bytes accessed | tf_op | source)
XLA Modules:
  0.0 34.3 jit_solution(18039217058467984450)
XLA Ops:
  1.3 1.4 %pack_group.1.pack = f32[8,1024]{1,0:T(8,128)} custom-call(f32[3,1024]{1,0:T(4,128)} %positions.1, f32[3,1024]{1,0:T(4,128)} %strengths.1, f32[1,1024]{1,0:T(1,128)} %bitcast.6, s32[2,1,1,2]{3,2,1,0:T(1,128)} %pair_list.1, s32[1,1]{1,0:T(1,128)S(6)} %copy.7.pair_count), custom_call_target="tpu_custom_call" | custom-call | tf_op jit(solution)/shard_map/pack_group/pallas_call | solution.py:381
  2.7 4.1 %collective-permute-start = (f32[1,8,1024]{2,1,0:T(8,128)}, f32[1,8,1024]{2,1,0:T(8,128)S(1)}, u32[]{:S(2)}, u32[]{:S(2)}) collective-permute-start(f32[1,8,1024]{2,1,0:T(8,128)} %bitcast.2), channel_id=1, source_target_pairs={{0,4},{1,5},{2,6},{3,7},{4,0},{5,1},{6,2},{7,3},{8,12},{9,13},{10,... | collective-permute-start | bytes 98312 | tf_op jit(solution)/shard_map/ppermute | solution.py:351
  6.8 1.5 %collective-permute-start.1 = (f32[1,8,1024]{2,1,0:T(8,128)}, f32[1,8,1024]{2,1,0:T(8,128)S(1)}, u32[]{:S(2)}, u32[]{:S(2)}) collective-permute-start(f32[1,8,1024]{2,1,0:T(8,128)} %bitcast.3), channel_id=1, source_target_pairs={{0,16},{8,24},{16,0},{24,8},{1,17},{9,25},{17,1},{25,9},{2,18},{10... | collective-permute-start | bytes 98312 | tf_op jit(solution)/shard_map/ppermute | solution.py:351
  8.3 0.8 %copy-done = f32[8,1024]{1,0:T(8,128)S(1)} copy-done((f32[8,1024]{1,0:T(8,128)S(1)}, f32[8,1024]{1,0:T(8,128)}, u32[]{:S(2)}) %copy-start) | copy-done | bytes 32792
  9.1 1.2 %own_first.1 = (f32[6,256]{1,0:T(8,128)S(1)}, bf16[1024,32]{1,0:T(8,128)(2,1)S(1)}, f32[1024,32]{1,0:T(8,128)S(1)}, bf16[32,1024]{1,0:T(8,128)(2,1)S(1)}, bf16[3...) custom-call(f32[8,1024]{1,0:T(8,128)S(1)} %copy-done), custom_call_target="tpu_custom_call" | custom-call | flops 7864320 | bytes 65536 | tf_op jit(solution)/shard_map/own_first/pallas_call | solution.py:404
  10.3 0.6 %collective-permute-done.1.refs_3_.refs_5_ = f32[1,8,1024]{2,1,0:T(8,128)S(1)} collective-permute-done((f32[1,8,1024]{2,1,0:T(8,128)}, f32[1,8,1024]{2,1,0:T(8,128)S(1)}, u32[]{:S(2)}, u32[]{:S(2)}) %collective-permute-start.1) | collective-permute-done | bytes 32800 | tf_op jit(solution)/shard_map/ppermute | solution.py:351
  10.9 1.6 %collective-permute-start.2 = (f32[2,8,1024]{2,1,0:T(8,128)S(1)}, f32[2,8,1024]{2,1,0:T(8,128)S(1)}, u32[]{:S(2)}, u32[]{:S(2)}) collective-permute-start(f32[2,8,1024]{2,1,0:T(8,128)S(1)} %get-tuple-element.21.after.refs_0_), channel_id=1, source_target_pairs={{0,2},{1,3},{2,0},{3,1},{4,6},{5,7},{6,4},{7,5},{8,10},{9,11},{10,... | collective-permute-start | bytes 196616 | tf_op jit(solution)/shard_map/ppermute | solution.py:351
  12.6 1.5 %collective-permute-start.3 = (f32[2,8,1024]{2,1,0:T(8,128)S(1)}, f32[2,8,1024]{2,1,0:T(8,128)S(1)}, u32[]{:S(2)}, u32[]{:S(2)}) collective-permute-start(f32[2,8,1024]{2,1,0:T(8,128)S(1)} %get-tuple-element.27.near.refs_2_), channel_id=1, source_target_pairs={{0,8},{8,0},{16,24},{24,16},{1,9},{9,1},{17,25},{25,17},{2,10},{10... | collective-permute-start | bytes 196616 | tf_op jit(solution)/shard_map/ppermute | solution.py:351
  14.1 0.9 %own_2.1.refs_3_.after.refs_2_ = f32[6,256]{1,0:T(8,128)S(1)} custom-call(f32[8,1024]{1,0:T(8,128)S(1)} %copy-done, bf16[1024,32]{1,0:T(8,128)(2,1)S(1)} %get-tuple-element.22.dist, f32[1024,32]{1,0:T(8,128)S(1)} %get-tuple-element.23.s_col, bf16[32,1024]{1,0:T(8,128)(2,1)S(1)} %get-tuple-element.24.right, bf16[32,1024]{1,0:T(8,128)(2,1)S(1)} %get-tuple-element.25.feat_g, ...), custom_call_target="tpu_custom_call" | custom-call | flops 7864320 | bytes 65536 | tf_op jit(solution)/shard_map/own_2/pallas_call | solution.py:373
  15.0 0.9 %own_1.1.refs_2_.refs_1_ = f32[6,256]{1,0:T(8,128)S(1)} custom-call(f32[8,1024]{1,0:T(8,128)S(1)} %copy-done, bf16[1024,32]{1,0:T(8,128)(2,1)S(1)} %get-tuple-element.22.dist, f32[1024,32]{1,0:T(8,128)S(1)} %get-tuple-element.23.s_col, bf16[32,1024]{1,0:T(8,128)(2,1)S(1)} %get-tuple-element.24.right, bf16[32,1024]{1,0:T(8,128)(2,1)S(1)} %get-tuple-element.25.feat_g, ...), custom_call_target="tpu_custom_call" | custom-call | flops 7864320 | bytes 65536 | tf_op jit(solution)/shard_map/own_1/pallas_call | solution.py:373
  15.9 0.9 %collective-permute-done.3.refs_4_.far = f32[2,8,1024]{2,1,0:T(8,128)S(1)} collective-permute-done((f32[2,8,1024]{2,1,0:T(8,128)S(1)}, f32[2,8,1024]{2,1,0:T(8,128)S(1)}, u32[]{:S(2)}, u32[]{:S(2)}) %collective-permute-start.3) | collective-permute-done | bytes 65568 | tf_op jit(solution)/shard_map/ppermute | solution.py:351
  16.8 0.1 collective-permute-start.4
  16.9 0.2 prepare_group.1
  17.2 1.1 %collective-permute-done.4.far = f32[4,8,1024]{2,1,0:T(8,128)S(1)} collective-permute-done((f32[4,8,1024]{2,1,0:T(8,128)S(1)}, f32[4,8,1024]{2,1,0:T(8,128)S(1)}, u32[]{:S(2)}, u32[]{:S(2)}) %collective-permute-start.4) | collective-permute-done | bytes 131104 | tf_op jit(solution)/shard_map/ppermute | solution.py:351
  18.3 0.1 listed_pair.1
  18.4 7.0 %collective-permute-start.8 = (f32[48,128]{1,0:T(8,128)S(1)}, f32[48,128]{1,0:T(8,128)S(1)}, u32[]{:S(2)}, u32[]{:S(2)}) collective-permute-start(f32[48,128]{1,0:T(8,128)S(1)} %get-tuple-element.34.refs_1_), channel_id=1, source_target_pairs={{0,16},{8,24},{16,0},{24,8},{1,17},{9,25},{17,1},{25,9},{2,18},{10... | collective-permute-start | bytes 73736 | tf_op jit(solution)/shard_map/ppermute | solution.py:351
  25.4 1.9 %collective-permute-start.6 = (f32[48,128]{1,0:T(8,128)S(1)}, f32[48,128]{1,0:T(8,128)S(1)}, u32[]{:S(2)}, u32[]{:S(2)}) collective-permute-start(f32[48,128]{1,0:T(8,128)S(1)} %get-tuple-element.32.refs_3_), channel_id=1, source_target_pairs={{0,4},{1,5},{2,6},{3,7},{4,0},{5,1},{6,2},{7,3},{8,12},{9,13},{10,... | collective-permute-start | bytes 73736 | tf_op jit(solution)/shard_map/ppermute | solution.py:351
  27.3 2.5 %collective-permute-start.7 = (f32[48,128]{1,0:T(8,128)S(1)}, f32[48,128]{1,0:T(8,128)S(1)}, u32[]{:S(2)}, u32[]{:S(2)}) collective-permute-start(f32[48,128]{1,0:T(8,128)S(1)} %get-tuple-element.32.refs_3_), channel_id=1, source_target_pairs={{0,2},{1,3},{2,0},{3,1},{4,6},{5,7},{6,4},{7,5},{8,10},{9,11},{10,... | collective-permute-start | bytes 73736 | tf_op jit(solution)/shard_map/ppermute | solution.py:351
  29.8 1.6 %collective-permute-start.10 = (f32[48,128]{1,0:T(8,128)S(1)}, f32[48,128]{1,0:T(8,128)S(1)}, u32[]{:S(2)}, u32[]{:S(2)}) collective-permute-start(f32[48,128]{1,0:T(8,128)S(1)} %get-tuple-element.37), channel_id=1, source_target_pairs={{0,8},{8,0},{16,24},{24,16},{1,9},{9,1},{17,25},{25,17},{2,10},{10... | collective-permute-start | bytes 73736 | tf_op jit(solution)/shard_map/ppermute | solution.py:351
  31.4 0.2 collective-permute-done.7.refs_2_
  31.6 0.1 collective-permute-start.9
  31.7 0.9 %own_3.1.refs_3_ = f32[6,256]{1,0:T(8,128)S(1)} custom-call(f32[8,1024]{1,0:T(8,128)S(1)} %copy-done.1, bf16[1024,32]{1,0:T(8,128)(2,1)S(1)} %get-tuple-element.22.dist, f32[1024,32]{1,0:T(8,128)S(1)} %get-tuple-element.23.s_col, bf16[32,1024]{1,0:T(8,128)(2,1)S(1)} %get-tuple-element.24.right, bf16[32,1024]{1,0:T(8,128)(2,1)S(1)} %get-tuple-element.25.feat_g, ...), custom_call_target="tpu_custom_call" | custom-call | flops 7864320 | bytes 65536 | tf_op jit(solution)/shard_map/own_3/pallas_call | solution.py:373
  32.6 1.1 %collective-permute-done.10.part_b = f32[48,128]{1,0:T(8,128)S(1)} collective-permute-done((f32[48,128]{1,0:T(8,128)S(1)}, f32[48,128]{1,0:T(8,128)S(1)}, u32[]{:S(2)}, u32[]{:S(2)}) %collective-permute-start.10) | collective-permute-done | bytes 24608 | tf_op jit(solution)/shard_map/ppermute | solution.py:351
  33.7 0.6 %sum_parts.1 = (f32[3,1024]{1,0:T(4,128)}, f32[3,1024]{1,0:T(4,128)}) custom-call(f32[48,128]{1,0:T(8,128)S(1)} %get-tuple-element.33.after.keep_a, f32[48,128]{1,0:T(8,128)S(1)} %get-tuple-element.35.keep_b, f32[48,128]{1,0:T(8,128)S(1)} %collective-permute-done.9.part_a, f32[48,128]{1,0:T(8,128)S(1)} %collective-permute-done.10.part_b, ...), custom_call_target="tpu_custom_call" | custom-call | tf_op jit(solution)/shard_map/sum_parts/pallas_call | solution.py:483
  (14 shorter events, 0.1 us)
Async XLA Ops:
  2.7 7.6 %collective-permute-start = (f32[1,8,1024]{2,1,0:T(8,128)}, f32[1,8,1024]{2,1,0:T(8,128)S(1)}, u32[]{:S(2)}, u32[]{:S(2)}) collective-permute-start(f32[1,8,1024]{2,1,0:T(8,128)} %bitcast.2), channel_id=1, source_target_pairs={{0,4},{1,5},{2,6},{3,7},{4,0},{5,1},{6,2},{7,3},{8,12},{9,13},{10,... | collective-permute-start | bytes 98312 | tf_op jit(solution)/shard_map/ppermute | solution.py:351
  6.8 4.1 %collective-permute-start.1 = (f32[1,8,1024]{2,1,0:T(8,128)}, f32[1,8,1024]{2,1,0:T(8,128)S(1)}, u32[]{:S(2)}, u32[]{:S(2)}) collective-permute-start(f32[1,8,1024]{2,1,0:T(8,128)} %bitcast.3), channel_id=1, source_target_pairs={{0,16},{8,24},{16,0},{24,8},{1,17},{9,25},{17,1},{25,9},{2,18},{10... | collective-permute-start | bytes 98312 | tf_op jit(solution)/shard_map/ppermute | solution.py:351
  8.3 0.8 %copy-start = (f32[8,1024]{1,0:T(8,128)S(1)}, f32[8,1024]{1,0:T(8,128)}, u32[]{:S(2)}) copy-start(f32[8,1024]{1,0:T(8,128)} %pack_group.1.pack) | copy-start | bytes 98308
  10.9 5.0 %collective-permute-start.2 = (f32[2,8,1024]{2,1,0:T(8,128)S(1)}, f32[2,8,1024]{2,1,0:T(8,128)S(1)}, u32[]{:S(2)}, u32[]{:S(2)}) collective-permute-start(f32[2,8,1024]{2,1,0:T(8,128)S(1)} %get-tuple-element.21.after.refs_0_), channel_id=1, source_target_pairs={{0,2},{1,3},{2,0},{3,1},{4,6},{5,7},{6,4},{7,5},{8,10},{9,11},{10,... | collective-permute-start | bytes 196616 | tf_op jit(solution)/shard_map/ppermute | solution.py:351
  12.6 4.3 %collective-permute-start.3 = (f32[2,8,1024]{2,1,0:T(8,128)S(1)}, f32[2,8,1024]{2,1,0:T(8,128)S(1)}, u32[]{:S(2)}, u32[]{:S(2)}) collective-permute-start(f32[2,8,1024]{2,1,0:T(8,128)S(1)} %get-tuple-element.27.near.refs_2_), channel_id=1, source_target_pairs={{0,8},{8,0},{16,24},{24,16},{1,9},{9,1},{17,25},{25,17},{2,10},{10... | collective-permute-start | bytes 196616 | tf_op jit(solution)/shard_map/ppermute | solution.py:351
  15.9 1.0 %copy-start.1 = (f32[8,1024]{1,0:T(8,128)S(1)}, f32[8,1024]{1,0:T(8,128)}, u32[]{:S(2)}) copy-start(f32[8,1024]{1,0:T(8,128)} %pack_group.1.pack) | copy-start | bytes 98308
  16.8 1.4 %collective-permute-start.4 = (f32[4,8,1024]{2,1,0:T(8,128)S(1)}, f32[4,8,1024]{2,1,0:T(8,128)S(1)}, u32[]{:S(2)}, u32[]{:S(2)}) collective-permute-start(f32[4,8,1024]{2,1,0:T(8,128)S(1)} %stack_groups.3.after.near.refs_4_), channel_id=1, source_target_pairs={{0,1},{1,0},{2,3},{3,2},{4,5},{5,4},{6,7},{7,6},{8,9},{9,8},{10,11... | collective-permute-start | bytes 393224 | tf_op jit(solution)/shard_map/ppermute | solution.py:351
  18.4 11.4 %collective-permute-start.8 = (f32[48,128]{1,0:T(8,128)S(1)}, f32[48,128]{1,0:T(8,128)S(1)}, u32[]{:S(2)}, u32[]{:S(2)}) collective-permute-start(f32[48,128]{1,0:T(8,128)S(1)} %get-tuple-element.34.refs_1_), channel_id=1, source_target_pairs={{0,16},{8,24},{16,0},{24,8},{1,17},{9,25},{17,1},{25,9},{2,18},{10... | collective-permute-start | bytes 73736 | tf_op jit(solution)/shard_map/ppermute | solution.py:351
  25.4 6.0 %collective-permute-start.5 = (f32[48,128]{1,0:T(8,128)S(1)}, f32[48,128]{1,0:T(8,128)S(1)}, u32[]{:S(2)}, u32[]{:S(2)}) collective-permute-start(f32[48,128]{1,0:T(8,128)S(1)} %get-tuple-element.32.refs_3_), channel_id=1, source_target_pairs={{0,6},{1,7},{2,4},{3,5},{4,2},{5,3},{6,0},{7,1},{8,14},{9,15},{10,... | collective-permute-start | bytes 73736 | tf_op jit(solution)/shard_map/ppermute | solution.py:351
  25.4 6.0 %collective-permute-start.6 = (f32[48,128]{1,0:T(8,128)S(1)}, f32[48,128]{1,0:T(8,128)S(1)}, u32[]{:S(2)}, u32[]{:S(2)}) collective-permute-start(f32[48,128]{1,0:T(8,128)S(1)} %get-tuple-element.32.refs_3_), channel_id=1, source_target_pairs={{0,4},{1,5},{2,6},{3,7},{4,0},{5,1},{6,2},{7,3},{8,12},{9,13},{10,... | collective-permute-start | bytes 73736 | tf_op jit(solution)/shard_map/ppermute | solution.py:351
  27.3 4.3 %collective-permute-start.7 = (f32[48,128]{1,0:T(8,128)S(1)}, f32[48,128]{1,0:T(8,128)S(1)}, u32[]{:S(2)}, u32[]{:S(2)}) collective-permute-start(f32[48,128]{1,0:T(8,128)S(1)} %get-tuple-element.32.refs_3_), channel_id=1, source_target_pairs={{0,2},{1,3},{2,0},{3,1},{4,6},{5,7},{6,4},{7,5},{8,10},{9,11},{10,... | collective-permute-start | bytes 73736 | tf_op jit(solution)/shard_map/ppermute | solution.py:351
  29.8 3.9 %collective-permute-start.10 = (f32[48,128]{1,0:T(8,128)S(1)}, f32[48,128]{1,0:T(8,128)S(1)}, u32[]{:S(2)}, u32[]{:S(2)}) collective-permute-start(f32[48,128]{1,0:T(8,128)S(1)} %get-tuple-element.37), channel_id=1, source_target_pairs={{0,8},{8,0},{16,24},{24,16},{1,9},{9,1},{17,25},{25,17},{2,10},{10... | collective-permute-start | bytes 73736 | tf_op jit(solution)/shard_map/ppermute | solution.py:351
  31.6 2.1 %collective-permute-start.9 = (f32[48,128]{1,0:T(8,128)S(1)}, f32[48,128]{1,0:T(8,128)S(1)}, u32[]{:S(2)}, u32[]{:S(2)}) collective-permute-start(f32[48,128]{1,0:T(8,128)S(1)} %get-tuple-element.36), channel_id=1, source_target_pairs={{0,1},{1,0},{2,3},{3,2},{4,5},{5,4},{6,7},{7,6},{8,9},{9,8},{10,11... | collective-permute-start | bytes 73736 | tf_op jit(solution)/shard_map/ppermute | solution.py:351

commit v6 on v4

--- a/solution.py
+++ b/solution.py
@@ -43,6 +43,15 @@
     moments = jnp.concatenate([e0, pos[0:1] * e0, pos[1:2] * e0, pos[2:3] * e0])
     for_g = jnp.concatenate(split(e0) + [jnp.zeros_like(e0)]).astype(BF16)
     return for_g, jnp.concatenate(split(moments)).astype(BF16)
+
+
+def widen(pack):
+    for_g, for_h = features(pack)
+    both = jnp.transpose(jnp.concatenate([for_h.astype(F32), for_g.astype(F32)]))
+    at = lax.broadcasted_iota(jnp.int32, both.shape, 1)
+    wide_g = jnp.where(at < H_ROWS, 0.0, both).astype(BF16)
+    wide_h = jnp.where(at < H_ROWS, both, 0.0).astype(BF16)
+    return wide_g, wide_h
 
 
 def finish(pack, g, h):
@@ -86,10 +95,6 @@
 
 def down(f, image):
     return jnp.dot(f, image, preferred_element_type=F32)
-
-
-def across(f, image):
-    return lax.dot_general(f, image, (((1,), (1,)), ((), ())), preferred_element_type=F32)
 
 
 def halves(pack):
@@ -159,7 +164,7 @@
         step()
 
 
-def interact_both(dist_a, s_a, dist_b, s_b, feat_a, feat_b, qq, images, sums_a, sums_b):
+def interact_both(dist_a, s_a, dist_b, s_b, feat_a, wide_b, qq, images, acc, sums_b):
     rows, n = s_a.shape[0], UNIT
     blocks, chunks = s_b.shape[1] // n, rows // n
     half = rows // 2
@@ -168,11 +173,11 @@
         here, part = slice(c * n, (c + 1) * n), slice(block * n, (block + 1) * n)
         qq[block % 2][here, :] = down(dist_a[here, :], dist_b[:, part])
 
-    def onto_a(block, c, kind):
+    def onto_a(block, c):
         here, part = slice(c * n, (c + 1) * n), slice(block * n, (block + 1) * n)
-        f = jnp.concatenate([feat_b[kind][:, part]] * 2, axis=1)
-        share = across(f, images[block % 2][here, 2 * kind * n : 2 * (kind + 1) * n])
-        sums_a[kind][:, here] = share if block == 0 else sums_a[kind][:, here] + share
+        wide = jnp.concatenate([wide_b[0][part, :]] * 2 + [wide_b[1][part, :]] * 2)
+        share = down(images[block % 2][here, :], wide)
+        acc[here, :] = share if block == 0 else acc[here, :] + share
 
     def onto_b(block, later, kind):
         here, part = slice(later * half, (later + 1) * half), slice(block * n, (block + 1) * n)
@@ -203,8 +208,7 @@
                     todo.pop(0)()
             for step in todo:
                 step()
-            for kind in range(2):
-                ready.append(functools.partial(onto_a, block, c, kind))
+            ready.append(functools.partial(onto_a, block, c))
             if (c + 1) % (chunks // 2) == 0:
                 later = (c + 1) // (chunks // 2) - 1
                 ready.append(functools.partial(onto_b, block, later, 0))
@@ -279,17 +283,17 @@
     return jnp.where(relative % 2 == 0, near[at], far[at])
 
 
-def prepare_kernel(pack, near, far, after, chosen, right, feat_g, feat_h):
+def prepare_kernel(pack, near, far, after, chosen, right, wide_g, wide_h):
     del after
     m = jnp.max(listed(pack)[1]).astype(jnp.int32)
     chosen[...] = choose(m ^ here("row"), near, far)
     right[...] = distances(chosen[...])[1]
-    feat_g[...], feat_h[...] = features(chosen[...])
-
-
-def pair_kernel(pack, near, far, bpack, right, feat_g, feat_h, after, out_a, out_b, apack, dist, s_col, *rest):
+    wide_g[...], wide_h[...] = widen(chosen[...])
+
+
+def pair_kernel(pack, near, far, bpack, right, wide_g, wide_h, after, out_a, out_b, apack, dist, s_col, *rest):
     del after
-    sums_a, sums_b, qq, images = rest[0:2], rest[2:4], rest[4:6], rest[6:8]
+    acc, sums_b, qq, images = rest[0], rest[1:3], rest[3:5], rest[5:7]
     k, _, count = [jnp.max(value).astype(jnp.int32) for value in listed(pack)]
 
     @pl.when(count > 1)
@@ -298,9 +302,10 @@
         columns(apack[...], dist, s_col)
         feat_a = features(apack[...])
         interact_both(
-            dist, s_col, right, halves(bpack[...]), feat_a, (feat_g, feat_h), qq, images, sums_a, sums_b
+            dist, s_col, right, halves(bpack[...]), feat_a, (wide_g, wide_h), qq, images, acc, sums_b
         )
-        store_dense(out_a, finish(apack[...], sums_a[0][...], sums_a[1][...]))
+        total = jnp.transpose(acc[...])
+        store_dense(out_a, finish(apack[...], total[H_ROWS:], total[:H_ROWS]))
         store_dense(out_b, finish(bpack[...], sums_b[0][...], sums_b[1][...]))
 
 
@@ -345,7 +350,9 @@
         pltpu.VMEM((8, g), F32),
         pltpu.VMEM((g, Q_ROWS), BF16),
         pltpu.VMEM((g, Q_ROWS), F32),
-        *[pltpu.VMEM((G_ROWS, g), F32), pltpu.VMEM((H_ROWS, g), F32)] * 2,
+        pltpu.VMEM((g, G_ROWS + H_ROWS), F32),
+        pltpu.VMEM((G_ROWS, g), F32),
+        pltpu.VMEM((H_ROWS, g), F32),
         *[pltpu.VMEM((g, UNIT), F32)] * 2,
         *[pltpu.VMEM((g, 4 * UNIT), BF16)] * 2,
     ]
@@ -444,8 +451,7 @@
         out_shape=(
             block,
             jax.ShapeDtypeStruct((Q_ROWS, g), BF16),
-            jax.ShapeDtypeStruct((G_ROWS, g), BF16),
-            jax.ShapeDtypeStruct((H_ROWS, g), BF16),
+            *[jax.ShapeDtypeStruct((g, G_ROWS + H_ROWS), BF16)] * 2,
         ),
         in_specs=[vmem_spec] * 4,
         out_specs=(vmem_spec,) * 4,

time: 32.4 us -> 33.6 us (1.037)
  starting transfers between devices: 13.9 us -> 21.1 us
  Pallas kernels: 11.1 us -> 6.48 us
  waiting for transfers between devices: 4.91 us -> 3.27 us
    ppermute x11, starting transfers between devices: 13.9 us -> 21.1 us  [swap(): return lax.ppermute(block, axis, [(i, i ^ step) for i in range(size)])]
    pallas_call x1, Pallas kernels: 4.79 us -> 0.12 us  [local(): pl.pallas_call(pair_kernel, out_shape=(dense, dense), in_specs=[vmem_spec...]
    ppermute x11, waiting for transfers between devices: 4.91 us -> 3.27 us  [swap(): return lax.ppermute(block, axis, [(i, i ^ step) for i in range(size)])]
  transfers between devices with their start and end apart: 11 -> 11, of which waited for: 6 -> 4; matrix products, arithmetic and copies ran while one was open for 0% -> 0% of each run, Pallas kernels for 13% -> 13%
where the time goes in v6:
time: 33.6 us; the launch traced here: 33.1 us
  starting transfers between devices  21.1 us (63%)
  Pallas kernels  6.48 us (19%)
  waiting for transfers between devices  3.27 us (10%)
  between operations  1.4 us (4%)
  local copies, waits for them, and re-layouts  0.8 us (2%)
    ppermute x11, starting transfers between devices, swap(): return lax.ppermute(block, axis, [(i, i ^ step) for i in range(size)])  21.1 us
    ppermute x11, waiting for transfers between devices, swap(): return lax.ppermute(block, axis, [(i, i ^ step) for i in range(size)])  3.27 us
    pallas_call x3, Pallas kernels, later(): chunk_call(functools.partial(later_kernel, n), out_shape=chunk, in_specs=...  2.76 us
    pallas_call x1, Pallas kernels, local(): pl.pallas_call(pack_kernel, out_shape=block, in_specs=[hbm_spec] * 5, out...  1.39 us
    pallas_call x1, Pallas kernels, local(): chunk_call(first_kernel, out_shape=(chunk, jax.ShapeDtypeStruct((g, Q_ROW...  1.19 us
    unnamed x4, local copies, waits for them, and re-layouts  0.8 us
  transfers between devices with their start and end apart: 11, of which 4 were waited for; matrix products, arithmetic and copies ran while one was open for 0% of the time, Pallas kernels for 13%

profile of v6, /device:TPU:0, one launch (start us, length us, event | category | flops | bytes accessed | tf_op | source)
XLA Modules:
  0.0 33.1 jit_solution(18126384393419312662)
XLA Ops:
  1.3 1.4 %pack_group.1.pack = f32[8,1024]{1,0:T(8,128)} custom-call(f32[3,1024]{1,0:T(4,128)} %positions.1, f32[3,1024]{1,0:T(4,128)} %strengths.1, f32[1,1024]{1,0:T(1,128)} %bitcast.6, s32[2,1,1,2]{3,2,1,0:T(1,128)} %pair_list.1, s32[1,1]{1,0:T(1,128)S(6)} %copy.7.pair_count), custom_call_target="tpu_custom_call" | custom-call | tf_op jit(solution)/shard_map/pack_group/pallas_call | solution.py:392
  2.7 4.1 %collective-permute-start = (f32[1,8,1024]{2,1,0:T(8,128)}, f32[1,8,1024]{2,1,0:T(8,128)S(1)}, u32[]{:S(2)}, u32[]{:S(2)}) collective-permute-start(f32[1,8,1024]{2,1,0:T(8,128)} %bitcast.2), channel_id=1, source_target_pairs={{0,4},{1,5},{2,6},{3,7},{4,0},{5,1},{6,2},{7,3},{8,12},{9,13},{10,... | collective-permute-start | bytes 98312 | tf_op jit(solution)/shard_map/ppermute | solution.py:362
  6.8 1.5 %collective-permute-start.1 = (f32[1,8,1024]{2,1,0:T(8,128)}, f32[1,8,1024]{2,1,0:T(8,128)S(1)}, u32[]{:S(2)}, u32[]{:S(2)}) collective-permute-start(f32[1,8,1024]{2,1,0:T(8,128)} %bitcast.3), channel_id=1, source_target_pairs={{0,16},{8,24},{16,0},{24,8},{1,17},{9,25},{17,1},{25,9},{2,18},{10... | collective-permute-start | bytes 98312 | tf_op jit(solution)/shard_map/ppermute | solution.py:362
  8.3 0.8 %copy-done = f32[8,1024]{1,0:T(8,128)S(1)} copy-done((f32[8,1024]{1,0:T(8,128)S(1)}, f32[8,1024]{1,0:T(8,128)}, u32[]{:S(2)}) %copy-start) | copy-done | bytes 32792
  9.1 1.2 %own_first.1 = (f32[6,256]{1,0:T(8,128)S(1)}, bf16[1024,32]{1,0:T(8,128)(2,1)S(1)}, f32[1024,32]{1,0:T(8,128)S(1)}, bf16[32,1024]{1,0:T(8,128)(2,1)S(1)}, bf16[3...) custom-call(f32[8,1024]{1,0:T(8,128)S(1)} %copy-done), custom_call_target="tpu_custom_call" | custom-call | flops 7864320 | bytes 65536 | tf_op jit(solution)/shard_map/own_first/pallas_call | solution.py:415
  10.3 0.6 %collective-permute-done.1.refs_3_.refs_5_ = f32[1,8,1024]{2,1,0:T(8,128)S(1)} collective-permute-done((f32[1,8,1024]{2,1,0:T(8,128)}, f32[1,8,1024]{2,1,0:T(8,128)S(1)}, u32[]{:S(2)}, u32[]{:S(2)}) %collective-permute-start.1) | collective-permute-done | bytes 32800 | tf_op jit(solution)/shard_map/ppermute | solution.py:362
  10.9 1.6 %collective-permute-start.2 = (f32[2,8,1024]{2,1,0:T(8,128)S(1)}, f32[2,8,1024]{2,1,0:T(8,128)S(1)}, u32[]{:S(2)}, u32[]{:S(2)}) collective-permute-start(f32[2,8,1024]{2,1,0:T(8,128)S(1)} %get-tuple-element.21.after.refs_0_), channel_id=1, source_target_pairs={{0,2},{1,3},{2,0},{3,1},{4,6},{5,7},{6,4},{7,5},{8,10},{9,11},{10,... | collective-permute-start | bytes 196616 | tf_op jit(solution)/shard_map/ppermute | solution.py:362
  12.6 1.5 %collective-permute-start.3 = (f32[2,8,1024]{2,1,0:T(8,128)S(1)}, f32[2,8,1024]{2,1,0:T(8,128)S(1)}, u32[]{:S(2)}, u32[]{:S(2)}) collective-permute-start(f32[2,8,1024]{2,1,0:T(8,128)S(1)} %get-tuple-element.27.near.refs_2_), channel_id=1, source_target_pairs={{0,8},{8,0},{16,24},{24,16},{1,9},{9,1},{17,25},{25,17},{2,10},{10... | collective-permute-start | bytes 196616 | tf_op jit(solution)/shard_map/ppermute | solution.py:362
  14.1 0.9 %own_2.1.refs_3_.after.refs_2_ = f32[6,256]{1,0:T(8,128)S(1)} custom-call(f32[8,1024]{1,0:T(8,128)S(1)} %copy-done, bf16[1024,32]{1,0:T(8,128)(2,1)S(1)} %get-tuple-element.22.dist, f32[1024,32]{1,0:T(8,128)S(1)} %get-tuple-element.23.s_col, bf16[32,1024]{1,0:T(8,128)(2,1)S(1)} %get-tuple-element.24.right, bf16[32,1024]{1,0:T(8,128)(2,1)S(1)} %get-tuple-element.25.feat_g, ...), custom_call_target="tpu_custom_call" | custom-call | flops 7864320 | bytes 65536 | tf_op jit(solution)/shard_map/own_2/pallas_call | solution.py:384
  15.0 0.9 %own_1.1.refs_2_.refs_1_ = f32[6,256]{1,0:T(8,128)S(1)} custom-call(f32[8,1024]{1,0:T(8,128)S(1)} %copy-done, bf16[1024,32]{1,0:T(8,128)(2,1)S(1)} %get-tuple-element.22.dist, f32[1024,32]{1,0:T(8,128)S(1)} %get-tuple-element.23.s_col, bf16[32,1024]{1,0:T(8,128)(2,1)S(1)} %get-tuple-element.24.right, bf16[32,1024]{1,0:T(8,128)(2,1)S(1)} %get-tuple-element.25.feat_g, ...), custom_call_target="tpu_custom_call" | custom-call | flops 7864320 | bytes 65536 | tf_op jit(solution)/shard_map/own_1/pallas_call | solution.py:384
  15.9 0.9 %collective-permute-done.3.refs_4_.far = f32[2,8,1024]{2,1,0:T(8,128)S(1)} collective-permute-done((f32[2,8,1024]{2,1,0:T(8,128)S(1)}, f32[2,8,1024]{2,1,0:T(8,128)S(1)}, u32[]{:S(2)}, u32[]{:S(2)}) %collective-permute-start.3) | collective-permute-done | bytes 65568 | tf_op jit(solution)/shard_map/ppermute | solution.py:362
  16.8 0.1 collective-permute-start.4
  16.9 0.3 prepare_group.1
  17.3 1.0 %collective-permute-done.4.far = f32[4,8,1024]{2,1,0:T(8,128)S(1)} collective-permute-done((f32[4,8,1024]{2,1,0:T(8,128)S(1)}, f32[4,8,1024]{2,1,0:T(8,128)S(1)}, u32[]{:S(2)}, u32[]{:S(2)}) %collective-permute-start.4) | collective-permute-done | bytes 131104 | tf_op jit(solution)/shard_map/ppermute | solution.py:362
  18.3 0.1 listed_pair.1
  18.4 1.6 %collective-permute-start.8 = (f32[48,128]{1,0:T(8,128)S(1)}, f32[48,128]{1,0:T(8,128)S(1)}, u32[]{:S(2)}, u32[]{:S(2)}) collective-permute-start(f32[48,128]{1,0:T(8,128)S(1)} %get-tuple-element.34.refs_1_), channel_id=1, source_target_pairs={{0,16},{8,24},{16,0},{24,8},{1,17},{9,25},{17,1},{25,9},{2,18},{10... | collective-permute-start | bytes 73736 | tf_op jit(solution)/shard_map/ppermute | solution.py:362
  20.0 5.5 %collective-permute-start.5 = (f32[48,128]{1,0:T(8,128)S(1)}, f32[48,128]{1,0:T(8,128)S(1)}, u32[]{:S(2)}, u32[]{:S(2)}) collective-permute-start(f32[48,128]{1,0:T(8,128)S(1)} %get-tuple-element.32.refs_3_), channel_id=1, source_target_pairs={{0,6},{1,7},{2,4},{3,5},{4,2},{5,3},{6,0},{7,1},{8,14},{9,15},{10,... | collective-permute-start | bytes 73736 | tf_op jit(solution)/shard_map/ppermute | solution.py:362
  25.5 0.3 %collective-permute-start.6 = (f32[48,128]{1,0:T(8,128)S(1)}, f32[48,128]{1,0:T(8,128)S(1)}, u32[]{:S(2)}, u32[]{:S(2)}) collective-permute-start(f32[48,128]{1,0:T(8,128)S(1)} %get-tuple-element.32.refs_3_), channel_id=1, source_target_pairs={{0,4},{1,5},{2,6},{3,7},{4,0},{5,1},{6,2},{7,3},{8,12},{9,13},{10,... | collective-permute-start | bytes 73736 | tf_op jit(solution)/shard_map/ppermute | solution.py:362
  25.8 0.6 %collective-permute-start.7 = (f32[48,128]{1,0:T(8,128)S(1)}, f32[48,128]{1,0:T(8,128)S(1)}, u32[]{:S(2)}, u32[]{:S(2)}) collective-permute-start(f32[48,128]{1,0:T(8,128)S(1)} %get-tuple-element.32.refs_3_), channel_id=1, source_target_pairs={{0,2},{1,3},{2,0},{3,1},{4,6},{5,7},{6,4},{7,5},{8,10},{9,11},{10,... | collective-permute-start | bytes 73736 | tf_op jit(solution)/shard_map/ppermute | solution.py:362
  26.4 4.2 %collective-permute-start.10 = (f32[48,128]{1,0:T(8,128)S(1)}, f32[48,128]{1,0:T(8,128)S(1)}, u32[]{:S(2)}, u32[]{:S(2)}) collective-permute-start(f32[48,128]{1,0:T(8,128)S(1)} %get-tuple-element.37), channel_id=1, source_target_pairs={{0,8},{8,0},{16,24},{24,16},{1,9},{9,1},{17,25},{25,17},{2,10},{10... | collective-permute-start | bytes 73736 | tf_op jit(solution)/shard_map/ppermute | solution.py:362
  30.7 0.1 collective-permute-start.9
  30.8 0.9 %own_3.1.refs_3_ = f32[6,256]{1,0:T(8,128)S(1)} custom-call(f32[8,1024]{1,0:T(8,128)S(1)} %copy-done.1, bf16[1024,32]{1,0:T(8,128)(2,1)S(1)} %get-tuple-element.22.dist, f32[1024,32]{1,0:T(8,128)S(1)} %get-tuple-element.23.s_col, bf16[32,1024]{1,0:T(8,128)(2,1)S(1)} %get-tuple-element.24.right, bf16[32,1024]{1,0:T(8,128)(2,1)S(1)} %get-tuple-element.25.feat_g, ...), custom_call_target="tpu_custom_call" | custom-call | flops 7864320 | bytes 65536 | tf_op jit(solution)/shard_map/own_3/pallas_call | solution.py:384
  31.7 0.8 %collective-permute-done.10.part_b = f32[48,128]{1,0:T(8,128)S(1)} collective-permute-done((f32[48,128]{1,0:T(8,128)S(1)}, f32[48,128]{1,0:T(8,128)S(1)}, u32[]{:S(2)}, u32[]{:S(2)}) %collective-permute-start.10) | collective-permute-done | bytes 24608 | tf_op jit(solution)/shard_map/ppermute | solution.py:362
  32.4 0.6 %sum_parts.1 = (f32[3,1024]{1,0:T(4,128)}, f32[3,1024]{1,0:T(4,128)}) custom-call(f32[48,128]{1,0:T(8,128)S(1)} %get-tuple-element.33.after.keep_a, f32[48,128]{1,0:T(8,128)S(1)} %get-tuple-element.35.keep_b, f32[48,128]{1,0:T(8,128)S(1)} %collective-permute-done.9.part_a, f32[48,128]{1,0:T(8,128)S(1)} %collective-permute-done.10.part_b, ...), custom_call_target="tpu_custom_call" | custom-call | tf_op jit(solution)/shard_map/sum_parts/pallas_call | solution.py:493
  (14 shorter events, 0.1 us)
Async XLA Ops:
  2.7 7.6 %collective-permute-start = (f32[1,8,1024]{2,1,0:T(8,128)}, f32[1,8,1024]{2,1,0:T(8,128)S(1)}, u32[]{:S(2)}, u32[]{:S(2)}) collective-permute-start(f32[1,8,1024]{2,1,0:T(8,128)} %bitcast.2), channel_id=1, source_target_pairs={{0,4},{1,5},{2,6},{3,7},{4,0},{5,1},{6,2},{7,3},{8,12},{9,13},{10,... | collective-permute-start | bytes 98312 | tf_op jit(solution)/shard_map/ppermute | solution.py:362
  6.8 4.1 %collective-permute-start.1 = (f32[1,8,1024]{2,1,0:T(8,128)}, f32[1,8,1024]{2,1,0:T(8,128)S(1)}, u32[]{:S(2)}, u32[]{:S(2)}) collective-permute-start(f32[1,8,1024]{2,1,0:T(8,128)} %bitcast.3), channel_id=1, source_target_pairs={{0,16},{8,24},{16,0},{24,8},{1,17},{9,25},{17,1},{25,9},{2,18},{10... | collective-permute-start | bytes 98312 | tf_op jit(solution)/shard_map/ppermute | solution.py:362
  8.3 0.8 %copy-start = (f32[8,1024]{1,0:T(8,128)S(1)}, f32[8,1024]{1,0:T(8,128)}, u32[]{:S(2)}) copy-start(f32[8,1024]{1,0:T(8,128)} %pack_group.1.pack) | copy-start | bytes 98308
  10.9 5.0 %collective-permute-start.2 = (f32[2,8,1024]{2,1,0:T(8,128)S(1)}, f32[2,8,1024]{2,1,0:T(8,128)S(1)}, u32[]{:S(2)}, u32[]{:S(2)}) collective-permute-start(f32[2,8,1024]{2,1,0:T(8,128)S(1)} %get-tuple-element.21.after.refs_0_), channel_id=1, source_target_pairs={{0,2},{1,3},{2,0},{3,1},{4,6},{5,7},{6,4},{7,5},{8,10},{9,11},{10,... | collective-permute-start | bytes 196616 | tf_op jit(solution)/shard_map/ppermute | solution.py:362
  12.6 4.3 %collective-permute-start.3 = (f32[2,8,1024]{2,1,0:T(8,128)S(1)}, f32[2,8,1024]{2,1,0:T(8,128)S(1)}, u32[]{:S(2)}, u32[]{:S(2)}) collective-permute-start(f32[2,8,1024]{2,1,0:T(8,128)S(1)} %get-tuple-element.27.near.refs_2_), channel_id=1, source_target_pairs={{0,8},{8,0},{16,24},{24,16},{1,9},{9,1},{17,25},{25,17},{2,10},{10... | collective-permute-start | bytes 196616 | tf_op jit(solution)/shard_map/ppermute | solution.py:362
  15.9 1.0 %copy-start.1 = (f32[8,1024]{1,0:T(8,128)S(1)}, f32[8,1024]{1,0:T(8,128)}, u32[]{:S(2)}) copy-start(f32[8,1024]{1,0:T(8,128)} %pack_group.1.pack) | copy-start | bytes 98308
  16.8 1.4 %collective-permute-start.4 = (f32[4,8,1024]{2,1,0:T(8,128)S(1)}, f32[4,8,1024]{2,1,0:T(8,128)S(1)}, u32[]{:S(2)}, u32[]{:S(2)}) collective-permute-start(f32[4,8,1024]{2,1,0:T(8,128)S(1)} %stack_groups.3.after.near.refs_4_), channel_id=1, source_target_pairs={{0,1},{1,0},{2,3},{3,2},{4,5},{5,4},{6,7},{7,6},{8,9},{9,8},{10,11... | collective-permute-start | bytes 393224 | tf_op jit(solution)/shard_map/ppermute | solution.py:362
  18.4 8.0 %collective-permute-start.8 = (f32[48,128]{1,0:T(8,128)S(1)}, f32[48,128]{1,0:T(8,128)S(1)}, u32[]{:S(2)}, u32[]{:S(2)}) collective-permute-start(f32[48,128]{1,0:T(8,128)S(1)} %get-tuple-element.34.refs_1_), channel_id=1, source_target_pairs={{0,16},{8,24},{16,0},{24,8},{1,17},{9,25},{17,1},{25,9},{2,18},{10... | collective-permute-start | bytes 73736 | tf_op jit(solution)/shard_map/ppermute | solution.py:362
  20.0 10.7 %collective-permute-start.5 = (f32[48,128]{1,0:T(8,128)S(1)}, f32[48,128]{1,0:T(8,128)S(1)}, u32[]{:S(2)}, u32[]{:S(2)}) collective-permute-start(f32[48,128]{1,0:T(8,128)S(1)} %get-tuple-element.32.refs_3_), channel_id=1, source_target_pairs={{0,6},{1,7},{2,4},{3,5},{4,2},{5,3},{6,0},{7,1},{8,14},{9,15},{10,... | collective-permute-start | bytes 73736 | tf_op jit(solution)/shard_map/ppermute | solution.py:362
  25.5 5.2 %collective-permute-start.6 = (f32[48,128]{1,0:T(8,128)S(1)}, f32[48,128]{1,0:T(8,128)S(1)}, u32[]{:S(2)}, u32[]{:S(2)}) collective-permute-start(f32[48,128]{1,0:T(8,128)S(1)} %get-tuple-element.32.refs_3_), channel_id=1, source_target_pairs={{0,4},{1,5},{2,6},{3,7},{4,0},{5,1},{6,2},{7,3},{8,12},{9,13},{10,... | collective-permute-start | bytes 73736 | tf_op jit(solution)/shard_map/ppermute | solution.py:362
  25.8 4.8 %collective-permute-start.7 = (f32[48,128]{1,0:T(8,128)S(1)}, f32[48,128]{1,0:T(8,128)S(1)}, u32[]{:S(2)}, u32[]{:S(2)}) collective-permute-start(f32[48,128]{1,0:T(8,128)S(1)} %get-tuple-element.32.refs_3_), channel_id=1, source_target_pairs={{0,2},{1,3},{2,0},{3,1},{4,6},{5,7},{6,4},{7,5},{8,10},{9,11},{10,... | collective-permute-start | bytes 73736 | tf_op jit(solution)/shard_map/ppermute | solution.py:362
  26.4 6.0 %collective-permute-start.10 = (f32[48,128]{1,0:T(8,128)S(1)}, f32[48,128]{1,0:T(8,128)S(1)}, u32[]{:S(2)}, u32[]{:S(2)}) collective-permute-start(f32[48,128]{1,0:T(8,128)S(1)} %get-tuple-element.37), channel_id=1, source_target_pairs={{0,8},{8,0},{16,24},{24,16},{1,9},{9,1},{17,25},{25,17},{2,10},{10... | collective-permute-start | bytes 73736 | tf_op jit(solution)/shard_map/ppermute | solution.py:362
  30.7 1.8 %collective-permute-start.9 = (f32[48,128]{1,0:T(8,128)S(1)}, f32[48,128]{1,0:T(8,128)S(1)}, u32[]{:S(2)}, u32[]{:S(2)}) collective-permute-start(f32[48,128]{1,0:T(8,128)S(1)} %get-tuple-element.36), channel_id=1, source_target_pairs={{0,1},{1,0},{2,3},{3,2},{4,5},{5,4},{6,7},{7,6},{8,9},{9,8},{10,11... | collective-permute-start | bytes 73736 | tf_op jit(solution)/shard_map/ppermute | solution.py:362

commit v7 on v6

--- a/solution.py
+++ b/solution.py
@@ -11,7 +11,7 @@
 F32 = jnp.float32
 BF16 = jnp.bfloat16
 UNIT = 256
-STRIP = 16
+STRIP = 32
 G_ROWS = 32
 H_ROWS = 96
 Q_ROWS = 32

time: 33.6 us -> 33.6 us (level); the launches traced: 33.1 us -> 33.6 us
  waiting for transfers between devices: 3.27 us -> 5.25 us
  starting transfers between devices: 21.1 us -> 19.7 us
    ppermute x11, waiting for transfers between devices: 3.27 us -> 5.25 us  [swap(): return lax.ppermute(block, axis, [(i, i ^ step) for i in range(size)])]
    ppermute x11, starting transfers between devices: 21.1 us -> 19.7 us  [swap(): return lax.ppermute(block, axis, [(i, i ^ step) for i in range(size)])]
  transfers between devices with their start and end apart: 11 -> 11, of which waited for: 4 -> 7; matrix products, arithmetic and copies ran while one was open for 0% -> 0% of each run, Pallas kernels for 13% -> 13%
where the time goes in v7:
time: 33.6 us
  starting transfers between devices  19.7 us (59%)
  Pallas kernels  6.48 us (19%)
  waiting for transfers between devices  5.25 us (16%)
  between operations  1.4 us (4%)
  local copies, waits for them, and re-layouts  0.8 us (2%)
    ppermute x11, starting transfers between devices, swap(): return lax.ppermute(block, axis, [(i, i ^ step) for i in range(size)])  19.7 us
    ppermute x11, waiting for transfers between devices, swap(): return lax.ppermute(block, axis, [(i, i ^ step) for i in range(size)])  5.25 us
    pallas_call x3, Pallas kernels, later(): chunk_call(functools.partial(later_kernel, n), out_shape=chunk, in_specs=...  2.76 us
    pallas_call x1, Pallas kernels, local(): pl.pallas_call(pack_kernel, out_shape=block, in_specs=[hbm_spec] * 5, out...  1.39 us
    pallas_call x1, Pallas kernels, local(): chunk_call(first_kernel, out_shape=(chunk, jax.ShapeDtypeStruct((g, Q_ROW...  1.19 us
    unnamed x4, local copies, waits for them, and re-layouts  0.8 us
  transfers between devices with their start and end apart: 11, of which 7 were waited for; matrix products, arithmetic and copies ran while one was open for 0% of the time, Pallas kernels for 13%

profile of v7, /device:TPU:0, one launch (start us, length us, event | category | flops | bytes accessed | tf_op | source)
XLA Modules:
  0.0 33.6 jit_solution(18126384393419312662)
XLA Ops:
  1.3 1.4 %pack_group.1.pack = f32[8,1024]{1,0:T(8,128)} custom-call(f32[3,1024]{1,0:T(4,128)} %positions.1, f32[3,1024]{1,0:T(4,128)} %strengths.1, f32[1,1024]{1,0:T(1,128)} %bitcast.6, s32[2,1,1,2]{3,2,1,0:T(1,128)} %pair_list.1, s32[1,1]{1,0:T(1,128)S(6)} %copy.7.pair_count), custom_call_target="tpu_custom_call" | custom-call | tf_op jit(solution)/shard_map/pack_group/pallas_call | solution.py:392
  2.7 4.1 %collective-permute-start = (f32[1,8,1024]{2,1,0:T(8,128)}, f32[1,8,1024]{2,1,0:T(8,128)S(1)}, u32[]{:S(2)}, u32[]{:S(2)}) collective-permute-start(f32[1,8,1024]{2,1,0:T(8,128)} %bitcast.2), channel_id=1, source_target_pairs={{0,4},{1,5},{2,6},{3,7},{4,0},{5,1},{6,2},{7,3},{8,12},{9,13},{10,... | collective-permute-start | bytes 98312 | tf_op jit(solution)/shard_map/ppermute | solution.py:362
  6.8 1.5 %collective-permute-start.1 = (f32[1,8,1024]{2,1,0:T(8,128)}, f32[1,8,1024]{2,1,0:T(8,128)S(1)}, u32[]{:S(2)}, u32[]{:S(2)}) collective-permute-start(f32[1,8,1024]{2,1,0:T(8,128)} %bitcast.3), channel_id=1, source_target_pairs={{0,16},{8,24},{16,0},{24,8},{1,17},{9,25},{17,1},{25,9},{2,18},{10... | collective-permute-start | bytes 98312 | tf_op jit(solution)/shard_map/ppermute | solution.py:362
  8.3 0.8 %copy-done = f32[8,1024]{1,0:T(8,128)S(1)} copy-done((f32[8,1024]{1,0:T(8,128)S(1)}, f32[8,1024]{1,0:T(8,128)}, u32[]{:S(2)}) %copy-start) | copy-done | bytes 32792
  9.1 1.2 %own_first.1 = (f32[6,256]{1,0:T(8,128)S(1)}, bf16[1024,32]{1,0:T(8,128)(2,1)S(1)}, f32[1024,32]{1,0:T(8,128)S(1)}, bf16[32,1024]{1,0:T(8,128)(2,1)S(1)}, bf16[3...) custom-call(f32[8,1024]{1,0:T(8,128)S(1)} %copy-done), custom_call_target="tpu_custom_call" | custom-call | flops 7864320 | bytes 65536 | tf_op jit(solution)/shard_map/own_first/pallas_call | solution.py:415
  10.3 0.6 %collective-permute-done.1.refs_3_.refs_5_ = f32[1,8,1024]{2,1,0:T(8,128)S(1)} collective-permute-done((f32[1,8,1024]{2,1,0:T(8,128)}, f32[1,8,1024]{2,1,0:T(8,128)S(1)}, u32[]{:S(2)}, u32[]{:S(2)}) %collective-permute-start.1) | collective-permute-done | bytes 32800 | tf_op jit(solution)/shard_map/ppermute | solution.py:362
  10.9 1.6 %collective-permute-start.2 = (f32[2,8,1024]{2,1,0:T(8,128)S(1)}, f32[2,8,1024]{2,1,0:T(8,128)S(1)}, u32[]{:S(2)}, u32[]{:S(2)}) collective-permute-start(f32[2,8,1024]{2,1,0:T(8,128)S(1)} %get-tuple-element.21.after.refs_0_), channel_id=1, source_target_pairs={{0,2},{1,3},{2,0},{3,1},{4,6},{5,7},{6,4},{7,5},{8,10},{9,11},{10,... | collective-permute-start | bytes 196616 | tf_op jit(solution)/shard_map/ppermute | solution.py:362
  12.6 1.5 %collective-permute-start.3 = (f32[2,8,1024]{2,1,0:T(8,128)S(1)}, f32[2,8,1024]{2,1,0:T(8,128)S(1)}, u32[]{:S(2)}, u32[]{:S(2)}) collective-permute-start(f32[2,8,1024]{2,1,0:T(8,128)S(1)} %get-tuple-element.27.near.refs_2_), channel_id=1, source_target_pairs={{0,8},{8,0},{16,24},{24,16},{1,9},{9,1},{17,25},{25,17},{2,10},{10... | collective-permute-start | bytes 196616 | tf_op jit(solution)/shard_map/ppermute | solution.py:362
  14.1 0.9 %own_2.1.refs_3_.after.refs_2_ = f32[6,256]{1,0:T(8,128)S(1)} custom-call(f32[8,1024]{1,0:T(8,128)S(1)} %copy-done, bf16[1024,32]{1,0:T(8,128)(2,1)S(1)} %get-tuple-element.22.dist, f32[1024,32]{1,0:T(8,128)S(1)} %get-tuple-element.23.s_col, bf16[32,1024]{1,0:T(8,128)(2,1)S(1)} %get-tuple-element.24.right, bf16[32,1024]{1,0:T(8,128)(2,1)S(1)} %get-tuple-element.25.feat_g, ...), custom_call_target="tpu_custom_call" | custom-call | flops 7864320 | bytes 65536 | tf_op jit(solution)/shard_map/own_2/pallas_call | solution.py:384
  15.0 0.9 %own_1.1.refs_2_.refs_1_ = f32[6,256]{1,0:T(8,128)S(1)} custom-call(f32[8,1024]{1,0:T(8,128)S(1)} %copy-done, bf16[1024,32]{1,0:T(8,128)(2,1)S(1)} %get-tuple-element.22.dist, f32[1024,32]{1,0:T(8,128)S(1)} %get-tuple-element.23.s_col, bf16[32,1024]{1,0:T(8,128)(2,1)S(1)} %get-tuple-element.24.right, bf16[32,1024]{1,0:T(8,128)(2,1)S(1)} %get-tuple-element.25.feat_g, ...), custom_call_target="tpu_custom_call" | custom-call | flops 7864320 | bytes 65536 | tf_op jit(solution)/shard_map/own_1/pallas_call | solution.py:384
  15.9 0.9 %collective-permute-done.3.refs_4_.far = f32[2,8,1024]{2,1,0:T(8,128)S(1)} collective-permute-done((f32[2,8,1024]{2,1,0:T(8,128)S(1)}, f32[2,8,1024]{2,1,0:T(8,128)S(1)}, u32[]{:S(2)}, u32[]{:S(2)}) %collective-permute-start.3) | collective-permute-done | bytes 65568 | tf_op jit(solution)/shard_map/ppermute | solution.py:362
  16.9 0.3 prepare_group.1
  17.3 1.0 %collective-permute-done.4.far = f32[4,8,1024]{2,1,0:T(8,128)S(1)} collective-permute-done((f32[4,8,1024]{2,1,0:T(8,128)S(1)}, f32[4,8,1024]{2,1,0:T(8,128)S(1)}, u32[]{:S(2)}, u32[]{:S(2)}) %collective-permute-start.4) | collective-permute-done | bytes 131104 | tf_op jit(solution)/shard_map/ppermute | solution.py:362
  18.3 0.1 listed_pair.1
  18.4 6.3 %collective-permute-start.8 = (f32[48,128]{1,0:T(8,128)S(1)}, f32[48,128]{1,0:T(8,128)S(1)}, u32[]{:S(2)}, u32[]{:S(2)}) collective-permute-start(f32[48,128]{1,0:T(8,128)S(1)} %get-tuple-element.34.refs_1_), channel_id=1, source_target_pairs={{0,16},{8,24},{16,0},{24,8},{1,17},{9,25},{17,1},{25,9},{2,18},{10... | collective-permute-start | bytes 73736 | tf_op jit(solution)/shard_map/ppermute | solution.py:362
  24.7 0.8 %collective-permute-start.5 = (f32[48,128]{1,0:T(8,128)S(1)}, f32[48,128]{1,0:T(8,128)S(1)}, u32[]{:S(2)}, u32[]{:S(2)}) collective-permute-start(f32[48,128]{1,0:T(8,128)S(1)} %get-tuple-element.32.refs_3_), channel_id=1, source_target_pairs={{0,6},{1,7},{2,4},{3,5},{4,2},{5,3},{6,0},{7,1},{8,14},{9,15},{10,... | collective-permute-start | bytes 73736 | tf_op jit(solution)/shard_map/ppermute | solution.py:362
  25.5 0.3 %collective-permute-start.6 = (f32[48,128]{1,0:T(8,128)S(1)}, f32[48,128]{1,0:T(8,128)S(1)}, u32[]{:S(2)}, u32[]{:S(2)}) collective-permute-start(f32[48,128]{1,0:T(8,128)S(1)} %get-tuple-element.32.refs_3_), channel_id=1, source_target_pairs={{0,4},{1,5},{2,6},{3,7},{4,0},{5,1},{6,2},{7,3},{8,12},{9,13},{10,... | collective-permute-start | bytes 73736 | tf_op jit(solution)/shard_map/ppermute | solution.py:362
  25.8 3.2 %collective-permute-start.7 = (f32[48,128]{1,0:T(8,128)S(1)}, f32[48,128]{1,0:T(8,128)S(1)}, u32[]{:S(2)}, u32[]{:S(2)}) collective-permute-start(f32[48,128]{1,0:T(8,128)S(1)} %get-tuple-element.32.refs_3_), channel_id=1, source_target_pairs={{0,2},{1,3},{2,0},{3,1},{4,6},{5,7},{6,4},{7,5},{8,10},{9,11},{10,... | collective-permute-start | bytes 73736 | tf_op jit(solution)/shard_map/ppermute | solution.py:362
  29.1 0.1 collective-permute-start.10
  29.2 1.2 %collective-permute-done.5.refs_0_ = f32[48,128]{1,0:T(8,128)S(1)} collective-permute-done((f32[48,128]{1,0:T(8,128)S(1)}, f32[48,128]{1,0:T(8,128)S(1)}, u32[]{:S(2)}, u32[]{:S(2)}) %collective-permute-start.5) | collective-permute-done | bytes 24608 | tf_op jit(solution)/shard_map/ppermute | solution.py:362
  30.4 0.4 %collective-permute-done.6.refs_1_ = f32[48,128]{1,0:T(8,128)S(1)} collective-permute-done((f32[48,128]{1,0:T(8,128)S(1)}, f32[48,128]{1,0:T(8,128)S(1)}, u32[]{:S(2)}, u32[]{:S(2)}) %collective-permute-start.6) | collective-permute-done | bytes 24608 | tf_op jit(solution)/shard_map/ppermute | solution.py:362
  31.0 0.9 %own_3.1.refs_3_ = f32[6,256]{1,0:T(8,128)S(1)} custom-call(f32[8,1024]{1,0:T(8,128)S(1)} %copy-done.1, bf16[1024,32]{1,0:T(8,128)(2,1)S(1)} %get-tuple-element.22.dist, f32[1024,32]{1,0:T(8,128)S(1)} %get-tuple-element.23.s_col, bf16[32,1024]{1,0:T(8,128)(2,1)S(1)} %get-tuple-element.24.right, bf16[32,1024]{1,0:T(8,128)(2,1)S(1)} %get-tuple-element.25.feat_g, ...), custom_call_target="tpu_custom_call" | custom-call | flops 7864320 | bytes 65536 | tf_op jit(solution)/shard_map/own_3/pallas_call | solution.py:384
  32.0 1.0 %collective-permute-done.10.part_b = f32[48,128]{1,0:T(8,128)S(1)} collective-permute-done((f32[48,128]{1,0:T(8,128)S(1)}, f32[48,128]{1,0:T(8,128)S(1)}, u32[]{:S(2)}, u32[]{:S(2)}) %collective-permute-start.10) | collective-permute-done | bytes 24608 | tf_op jit(solution)/shard_map/ppermute | solution.py:362
  33.0 0.6 %sum_parts.1 = (f32[3,1024]{1,0:T(4,128)}, f32[3,1024]{1,0:T(4,128)}) custom-call(f32[48,128]{1,0:T(8,128)S(1)} %get-tuple-element.33.after.keep_a, f32[48,128]{1,0:T(8,128)S(1)} %get-tuple-element.35.keep_b, f32[48,128]{1,0:T(8,128)S(1)} %collective-permute-done.9.part_a, f32[48,128]{1,0:T(8,128)S(1)} %collective-permute-done.10.part_b, ...), custom_call_target="tpu_custom_call" | custom-call | tf_op jit(solution)/shard_map/sum_parts/pallas_call | solution.py:493
  (14 shorter events, 0.3 us)
Async XLA Ops:
  2.7 7.6 %collective-permute-start = (f32[1,8,1024]{2,1,0:T(8,128)}, f32[1,8,1024]{2,1,0:T(8,128)S(1)}, u32[]{:S(2)}, u32[]{:S(2)}) collective-permute-start(f32[1,8,1024]{2,1,0:T(8,128)} %bitcast.2), channel_id=1, source_target_pairs={{0,4},{1,5},{2,6},{3,7},{4,0},{5,1},{6,2},{7,3},{8,12},{9,13},{10,... | collective-permute-start | bytes 98312 | tf_op jit(solution)/shard_map/ppermute | solution.py:362
  6.8 4.1 %collective-permute-start.1 = (f32[1,8,1024]{2,1,0:T(8,128)}, f32[1,8,1024]{2,1,0:T(8,128)S(1)}, u32[]{:S(2)}, u32[]{:S(2)}) collective-permute-start(f32[1,8,1024]{2,1,0:T(8,128)} %bitcast.3), channel_id=1, source_target_pairs={{0,16},{8,24},{16,0},{24,8},{1,17},{9,25},{17,1},{25,9},{2,18},{10... | collective-permute-start | bytes 98312 | tf_op jit(solution)/shard_map/ppermute | solution.py:362
  8.3 0.8 %copy-start = (f32[8,1024]{1,0:T(8,128)S(1)}, f32[8,1024]{1,0:T(8,128)}, u32[]{:S(2)}) copy-start(f32[8,1024]{1,0:T(8,128)} %pack_group.1.pack) | copy-start | bytes 98308
  10.9 5.0 %collective-permute-start.2 = (f32[2,8,1024]{2,1,0:T(8,128)S(1)}, f32[2,8,1024]{2,1,0:T(8,128)S(1)}, u32[]{:S(2)}, u32[]{:S(2)}) collective-permute-start(f32[2,8,1024]{2,1,0:T(8,128)S(1)} %get-tuple-element.21.after.refs_0_), channel_id=1, source_target_pairs={{0,2},{1,3},{2,0},{3,1},{4,6},{5,7},{6,4},{7,5},{8,10},{9,11},{10,... | collective-permute-start | bytes 196616 | tf_op jit(solution)/shard_map/ppermute | solution.py:362
  12.6 4.3 %collective-permute-start.3 = (f32[2,8,1024]{2,1,0:T(8,128)S(1)}, f32[2,8,1024]{2,1,0:T(8,128)S(1)}, u32[]{:S(2)}, u32[]{:S(2)}) collective-permute-start(f32[2,8,1024]{2,1,0:T(8,128)S(1)} %get-tuple-element.27.near.refs_2_), channel_id=1, source_target_pairs={{0,8},{8,0},{16,24},{24,16},{1,9},{9,1},{17,25},{25,17},{2,10},{10... | collective-permute-start | bytes 196616 | tf_op jit(solution)/shard_map/ppermute | solution.py:362
  15.9 1.0 %copy-start.1 = (f32[8,1024]{1,0:T(8,128)S(1)}, f32[8,1024]{1,0:T(8,128)}, u32[]{:S(2)}) copy-start(f32[8,1024]{1,0:T(8,128)} %pack_group.1.pack) | copy-start | bytes 98308
  16.8 1.4 %collective-permute-start.4 = (f32[4,8,1024]{2,1,0:T(8,128)S(1)}, f32[4,8,1024]{2,1,0:T(8,128)S(1)}, u32[]{:S(2)}, u32[]{:S(2)}) collective-permute-start(f32[4,8,1024]{2,1,0:T(8,128)S(1)} %stack_groups.3.after.near.refs_4_), channel_id=1, source_target_pairs={{0,1},{1,0},{2,3},{3,2},{4,5},{5,4},{6,7},{7,6},{8,9},{9,8},{10,11... | collective-permute-start | bytes 393224 | tf_op jit(solution)/shard_map/ppermute | solution.py:362
  18.4 10.7 %collective-permute-start.8 = (f32[48,128]{1,0:T(8,128)S(1)}, f32[48,128]{1,0:T(8,128)S(1)}, u32[]{:S(2)}, u32[]{:S(2)}) collective-permute-start(f32[48,128]{1,0:T(8,128)S(1)} %get-tuple-element.34.refs_1_), channel_id=1, source_target_pairs={{0,16},{8,24},{16,0},{24,8},{1,17},{9,25},{17,1},{25,9},{2,18},{10... | collective-permute-start | bytes 73736 | tf_op jit(solution)/shard_map/ppermute | solution.py:362
  24.7 5.7 %collective-permute-start.5 = (f32[48,128]{1,0:T(8,128)S(1)}, f32[48,128]{1,0:T(8,128)S(1)}, u32[]{:S(2)}, u32[]{:S(2)}) collective-permute-start(f32[48,128]{1,0:T(8,128)S(1)} %get-tuple-element.32.refs_3_), channel_id=1, source_target_pairs={{0,6},{1,7},{2,4},{3,5},{4,2},{5,3},{6,0},{7,1},{8,14},{9,15},{10,... | collective-permute-start | bytes 73736 | tf_op jit(solution)/shard_map/ppermute | solution.py:362
  25.5 5.4 %collective-permute-start.6 = (f32[48,128]{1,0:T(8,128)S(1)}, f32[48,128]{1,0:T(8,128)S(1)}, u32[]{:S(2)}, u32[]{:S(2)}) collective-permute-start(f32[48,128]{1,0:T(8,128)S(1)} %get-tuple-element.32.refs_3_), channel_id=1, source_target_pairs={{0,4},{1,5},{2,6},{3,7},{4,0},{5,1},{6,2},{7,3},{8,12},{9,13},{10,... | collective-permute-start | bytes 73736 | tf_op jit(solution)/shard_map/ppermute | solution.py:362
  25.8 5.1 %collective-permute-start.7 = (f32[48,128]{1,0:T(8,128)S(1)}, f32[48,128]{1,0:T(8,128)S(1)}, u32[]{:S(2)}, u32[]{:S(2)}) collective-permute-start(f32[48,128]{1,0:T(8,128)S(1)} %get-tuple-element.32.refs_3_), channel_id=1, source_target_pairs={{0,2},{1,3},{2,0},{3,1},{4,6},{5,7},{6,4},{7,5},{8,10},{9,11},{10,... | collective-permute-start | bytes 73736 | tf_op jit(solution)/shard_map/ppermute | solution.py:362
  29.1 3.9 %collective-permute-start.10 = (f32[48,128]{1,0:T(8,128)S(1)}, f32[48,128]{1,0:T(8,128)S(1)}, u32[]{:S(2)}, u32[]{:S(2)}) collective-permute-start(f32[48,128]{1,0:T(8,128)S(1)} %get-tuple-element.37), channel_id=1, source_target_pairs={{0,8},{8,0},{16,24},{24,16},{1,9},{9,1},{17,25},{25,17},{2,10},{10... | collective-permute-start | bytes 73736 | tf_op jit(solution)/shard_map/ppermute | solution.py:362
  31.0 2.0 %collective-permute-start.9 = (f32[48,128]{1,0:T(8,128)S(1)}, f32[48,128]{1,0:T(8,128)S(1)}, u32[]{:S(2)}, u32[]{:S(2)}) collective-permute-start(f32[48,128]{1,0:T(8,128)S(1)} %get-tuple-element.36), channel_id=1, source_target_pairs={{0,1},{1,0},{2,3},{3,2},{4,5},{5,4},{6,7},{7,6},{8,9},{9,8},{10,11... | collective-permute-start | bytes 73736 | tf_op jit(solution)/shard_map/ppermute | solution.py:362
